TPU v7x, 32 devices: a whole 2x2x4 slice. The times are simulated.
32 devices in a mesh: branch: 4 (over y, x), rows: 8 (over z, core).
Axes of the slice: x: 2, y: 2, z: 4, core: 2. Of those that a mesh axis runs over, the one named last changes fastest.
Arguments:
- maps_four: bfloat16 [48, 64, 1024], P(None, 'rows', 'branch'), may hold values from -6 to 6
- maps_eight: bfloat16 [96, 32, 512], P(None, 'rows', 'branch'), may hold values from -6 to 6
- maps_sixteen: bfloat16 [192, 16, 256], P(None, 'rows', 'branch'), may hold values from -6 to 6
- maps_thirtytwo: bfloat16 [384, 8, 128], P(None, 'rows', 'branch'), may hold values from -6 to 6
- kernel_four: bfloat16 [3, 3, 48, 48], replicated, may hold values from -0.3125 to 0.3125
- kernel_eight: bfloat16 [3, 3, 96, 96], replicated, may hold values from -0.21875 to 0.21875
- kernel_sixteen: bfloat16 [3, 3, 192, 192], replicated, may hold values from -0.15625 to 0.15625
- kernel_thirtytwo: bfloat16 [3, 3, 384, 384], replicated, may hold values from -0.109375 to 0.109375
- gain_four: float32 [48], replicated, may hold values from 0.1 to 1.9
- gain_eight: float32 [96], replicated, may hold values from 0.1 to 1.9
- gain_sixteen: float32 [192], replicated, may hold values from 0.1 to 1.9
- gain_thirtytwo: float32 [384], replicated, may hold values from 0.1 to 1.9
- mixer_four: bfloat16 [48, 672], replicated, may hold values from -0.25 to 0.25
- mixer_eight: bfloat16 [96, 624], replicated, may hold values from -0.25 to 0.25
- mixer_sixteen: bfloat16 [192, 528], replicated, may hold values from -0.25 to 0.25
- mixer_thirtytwo: bfloat16 [384, 336], replicated, may hold values from -0.3125 to 0.3125
- cotan_four: bfloat16 [48, 64, 1024], P(None, 'rows', 'branch'), may hold values from -6 to 6
- cotan_eight: bfloat16 [96, 32, 512], P(None, 'rows', 'branch'), may hold values from -6 to 6
- cotan_sixteen: bfloat16 [192, 16, 256], P(None, 'rows', 'branch'), may hold values from -6 to 6
- cotan_thirtytwo: bfloat16 [384, 8, 128], P(None, 'rows', 'branch'), may hold values from -6 to 6
Outputs:
- merged_four: bfloat16 [48, 64, 1024], P(None, 'rows', 'branch')
- merged_eight: bfloat16 [96, 32, 512], P(None, 'rows', 'branch')
- merged_sixteen: bfloat16 [192, 16, 256], P(None, 'rows', 'branch')
- merged_thirtytwo: bfloat16 [384, 8, 128], P(None, 'rows', 'branch')
- backprop_four: bfloat16 [48, 64, 1024], P(None, 'rows', 'branch')
- backprop_eight: bfloat16 [96, 32, 512], P(None, 'rows', 'branch')
- backprop_sixteen: bfloat16 [192, 16, 256], P(None, 'rows', 'branch')
- backprop_thirtytwo: bfloat16 [384, 8, 128], P(None, 'rows', 'branch')
- kernelgrad_four: bfloat16 [3, 3, 48, 48], replicated
- kernelgrad_eight: bfloat16 [3, 3, 96, 96], replicated
- kernelgrad_sixteen: bfloat16 [3, 3, 192, 192], replicated
- kernelgrad_thirtytwo: bfloat16 [3, 3, 384, 384], replicated
All inputs are finite; a program needn't handle non-finite values.
Results may differ from a plain program's by a relative error of at most 0.015.
Values may be sent and summed in bfloat16 or wider, within the bound.
No kernel may reach another device: no remote copies, remote signals or barrier semaphores. Data moves between devices by JAX's collectives and lax.ppermute only.
A program may use at most 128 MiB of HBM per device.

v0:
```python
import math

import jax
import jax.numpy as jnp
from jax import lax
from jax.sharding import PartitionSpec as P


def extended_2(block, sides, width):
    for axis, dim in sides:
        count = lax.axis_size(axis)
        forward = [(i, i + 1) for i in range(count - 1)]
        backward = [(target, source) for source, target in forward]
        low = lax.ppermute(
            lax.slice_in_dim(block, block.shape[dim] - width, None, axis=dim), axis, forward
        )
        high = lax.ppermute(lax.slice_in_dim(block, 0, width, axis=dim), axis, backward)
        block = jnp.concatenate([low, block, high], axis=dim)
    return block


def extend_maps(values):
    return extended_2(values, (("branch", 2), ("rows", 1)), 1)


def extend_grads(values):
    return extended_2(values, (("branch", 2), ("rows", 1)), 1)


def forward_taps(padded, kernel):
    channels = padded.shape[0]
    height = padded.shape[1] - 2
    columns = padded.shape[2] - 2
    summed = jnp.zeros((kernel.shape[2], height * columns), jnp.float32)
    for row_off in range(3):
        for col_off in range(3):
            window = padded[:, row_off : row_off + height, col_off : col_off + columns].reshape(
                channels, height * columns
            )
            summed = summed + jnp.dot(
                kernel[row_off, col_off], window, preferred_element_type=jnp.float32
            )
    return summed.reshape(kernel.shape[2], height, columns)


def adjoint_taps(padded, kernel):
    channels = padded.shape[0]
    height = padded.shape[1] - 2
    columns = padded.shape[2] - 2
    summed = jnp.zeros((kernel.shape[3], height * columns), jnp.float32)
    for row_off in range(3):
        for col_off in range(3):
            window = padded[
                :, 2 - row_off : 2 - row_off + height, 2 - col_off : 2 - col_off + columns
            ].reshape(channels, height * columns)
            summed = summed + lax.dot_general(
                kernel[row_off, col_off],
                window,
                (((0,), (0,)), ((), ())),
                preferred_element_type=jnp.float32,
            )
    return summed.reshape(kernel.shape[3], height, columns)


def kernel_taps(padded, gradient):
    channels = padded.shape[0]
    outputs = gradient.shape[0]
    height = gradient.shape[1]
    columns = gradient.shape[2]
    flattened = gradient.reshape(outputs, height * columns)
    tap_list = []
    for row_off in range(3):
        for col_off in range(3):
            window = padded[:, row_off : row_off + height, col_off : col_off + columns].reshape(
                channels, height * columns
            )
            tap_list.append(
                lax.dot_general(
                    flattened, window, (((1,), (1,)), ((), ())), preferred_element_type=jnp.float32
                )
            )
    return jnp.stack(tap_list).reshape(3, 3, outputs, channels)


def upsample(values, factor):
    channels, height, columns = values.shape
    spread_out = jnp.broadcast_to(
        values[:, :, None, :, None], (channels, height, factor, columns, factor)
    )
    return spread_out.reshape(channels, height * factor, columns * factor)


def source_offset(channel_counts, target, source):
    return sum((channel_counts[index] for index in range(source) if index != target))


def merged_maps(results, mixers, target):
    channel_counts = [item.shape[0] for item in results]
    summed = results[target].astype(jnp.float32)
    height = results[target].shape[1]
    columns = results[target].shape[2]
    for source in range(4):
        if source == target:
            continue
        width_in = channel_counts[source]
        offset = source_offset(channel_counts, target, source)
        mixer_block = mixers[target][:, offset : offset + width_in]
        if source > target:
            factor = 2 ** (source - target)
            projected = jnp.dot(
                mixer_block,
                results[source].reshape(width_in, -1),
                preferred_element_type=jnp.float32,
            )
            projected = projected.reshape(-1, results[source].shape[1], results[source].shape[2])
            summed = summed + upsample(projected, factor)
        else:
            factor = 2 ** (target - source)
            pooled = (
                results[source]
                .astype(jnp.float32)
                .reshape(width_in, height, factor, columns, factor)
                .mean(axis=(2, 4))
                .astype(jnp.bfloat16)
            )
            projected = jnp.dot(
                mixer_block, pooled.reshape(width_in, -1), preferred_element_type=jnp.float32
            )
            summed = summed + projected.reshape(-1, height, columns)
    return summed


def merged_adjoint(cotans, mixers, source):
    channel_counts = [item.shape[0] for item in cotans]
    summed = cotans[source].astype(jnp.float32)
    width_in = channel_counts[source]
    height = cotans[source].shape[1]
    columns = cotans[source].shape[2]
    for target in range(4):
        if target == source:
            continue
        offset = source_offset(channel_counts, target, source)
        mixer_block = mixers[target][:, offset : offset + width_in]
        outward = channel_counts[target]
        if source > target:
            factor = 2 ** (source - target)
            blocksum = (
                cotans[target]
                .astype(jnp.float32)
                .reshape(outward, height, factor, columns, factor)
                .sum(axis=(2, 4))
                .astype(jnp.bfloat16)
            )
            projected = lax.dot_general(
                mixer_block,
                blocksum.reshape(outward, -1),
                (((0,), (0,)), ((), ())),
                preferred_element_type=jnp.float32,
            )
            summed = summed + projected.reshape(width_in, height, columns)
        else:
            factor = 2 ** (target - source)
            projected = lax.dot_general(
                mixer_block,
                cotans[target].reshape(outward, -1),
                (((0,), (0,)), ((), ())),
                preferred_element_type=jnp.float32,
            )
            projected = projected.reshape(
                width_in, cotans[target].shape[1], cotans[target].shape[2]
            )
            summed = summed + upsample(projected, factor) / float(factor * factor)
    return summed


def local(
    maps_four,
    maps_eight,
    maps_sixteen,
    maps_thirtytwo,
    kernel_four,
    kernel_eight,
    kernel_sixteen,
    kernel_thirtytwo,
    gain_four,
    gain_eight,
    gain_sixteen,
    gain_thirtytwo,
    mixer_four,
    mixer_eight,
    mixer_sixteen,
    mixer_thirtytwo,
    cotan_four,
    cotan_eight,
    cotan_sixteen,
    cotan_thirtytwo,
):
    features = [maps_four, maps_eight, maps_sixteen, maps_thirtytwo]
    kernels = [kernel_four, kernel_eight, kernel_sixteen, kernel_thirtytwo]
    gain_list = [gain_four, gain_eight, gain_sixteen, gain_thirtytwo]
    mixers = [mixer_four, mixer_eight, mixer_sixteen, mixer_thirtytwo]
    cotans = [cotan_four, cotan_eight, cotan_sixteen, cotan_thirtytwo]
    rows_count = lax.axis_size("rows")
    bands_count = lax.axis_size("branch")
    actives = [
        jnp.maximum(features[branch], jnp.zeros((), features[branch].dtype)) for branch in range(4)
    ]
    upstreams = [merged_adjoint(cotans, mixers, branch) for branch in range(4)]
    scaled_list = [
        (gain_list[branch][:, None, None] * upstreams[branch]).astype(jnp.bfloat16)
        for branch in range(4)
    ]
    extended = []
    grads_extended = []
    for branch in range(4):
        extended.append(extend_maps(actives[branch]))
    for branch in range(4):
        grads_extended.append(extend_grads(scaled_list[branch]))
    results = []
    for branch in range(4):
        response = forward_taps(extended[branch], kernels[branch])
        results.append(
            (
                features[branch].astype(jnp.float32) + gain_list[branch][:, None, None] * response
            ).astype(jnp.bfloat16)
        )
    merged = [merged_maps(results, mixers, target).astype(jnp.bfloat16) for target in range(4)]
    backward_list = []
    partials = []
    for branch in range(4):
        adjoint = adjoint_taps(grads_extended[branch], kernels[branch])
        backward = upstreams[branch] + jnp.where(
            features[branch] > 0, adjoint, jnp.zeros((), jnp.float32)
        )
        backward_list.append(backward.astype(jnp.bfloat16))
        partial_sum = kernel_taps(extended[branch], scaled_list[branch])
        partials.append(partial_sum)
    totals = lax.psum((partials[0], partials[1], partials[2], partials[3]), ("branch", "rows"))
    kernel_list = []
    for branch in range(4):
        pixels = features[branch].shape[1] * rows_count * features[branch].shape[2] * bands_count
        kernel_list.append((totals[branch] * (1.0 / math.sqrt(pixels))).astype(jnp.bfloat16))
    return (
        merged[0],
        merged[1],
        merged[2],
        merged[3],
        backward_list[0],
        backward_list[1],
        backward_list[2],
        backward_list[3],
        kernel_list[0],
        kernel_list[1],
        kernel_list[2],
        kernel_list[3],
    )


def solution(mesh):
    in_specs = (
        P(None, "rows", "branch"),
        P(None, "rows", "branch"),
        P(None, "rows", "branch"),
        P(None, "rows", "branch"),
        P(),
        P(),
        P(),
        P(),
        P(),
        P(),
        P(),
        P(),
        P(),
        P(),
        P(),
        P(),
        P(None, "rows", "branch"),
        P(None, "rows", "branch"),
        P(None, "rows", "branch"),
        P(None, "rows", "branch"),
    )
    out_specs = (
        P(None, "rows", "branch"),
        P(None, "rows", "branch"),
        P(None, "rows", "branch"),
        P(None, "rows", "branch"),
        P(None, "rows", "branch"),
        P(None, "rows", "branch"),
        P(None, "rows", "branch"),
        P(None, "rows", "branch"),
        P(),
        P(),
        P(),
        P(),
    )
    return jax.shard_map(local, mesh=mesh, in_specs=in_specs, out_specs=out_specs, check_vma=False)
```

profile of v0, /device:TPU:0, one launch (start us, length us, event | category | flops | bytes accessed | tf_op | source)
XLA Modules:
  0.0 491.9 jit_solution(8760165795100862663)
XLA Ops:
  8.6 4.8 collective-permute-start.12
  16.2 4.5 collective-permute-start.8
  24.4 5.6 %collective-permute-start.4 = (bf16[96,4,1]{2,0,1:T(8,128)(2,1)}, bf16[96,4,1]{2,0,1:T(8,128)(2,1)}, u32[]{:S(2)}, u32[]{:S(2)}) collective-permute-start(bf16[96,4,1]{2,0,1:T(8,128)(2,1)} %get-tuple-element.136), channel_id=1, source_target_pairs={{0,8},{8,16},{16,24},{1,9},{9,17},{17,25},{2,10},{10,18},{18,26},{... | collective-permute-start | bytes 2312 | tf_op jit(solution)/shard_map/ppermute | solution.py:14
  51.2 2.3 copy.206
  55.9 4.2 collective-permute-start.24
  65.6 3.9 collective-permute-start
  73.6 5.4 %collective-permute-start.20 = (bf16[96,4,1]{2,0,1:T(8,128)(2,1)S(1)}, bf16[96,4,1]{2,0,1:T(8,128)(2,1)S(1)}, u32[]{:S(2)}, u32[]{:S(2)}) collective-permute-start(bf16[96,4,1]{2,0,1:T(8,128)(2,1)S(1)} %copy-done.57), channel_id=1, source_target_pairs={{0,8},{8,16},{16,24},{1,9},{9,17},{17,25},{2,10},{10,18},{18,26},{... | collective-permute-start | bytes 2312 | tf_op jit(solution)/shard_map/ppermute | solution.py:14
  83.6 5.4 %collective-permute-start.16 = (bf16[48,8,1]{2,0,1:T(8,128)(2,1)S(1)}, bf16[48,8,1]{2,0,1:T(8,128)(2,1)S(1)}, u32[]{:S(2)}, u32[]{:S(2)}) collective-permute-start(bf16[48,8,1]{2,0,1:T(8,128)(2,1)S(1)} %get-tuple-element.104), channel_id=1, source_target_pairs={{0,8},{8,16},{16,24},{1,9},{9,17},{17,25},{2,10},{10,18},{18,26},{... | collective-permute-start | bytes 2312 | tf_op jit(solution)/shard_map/ppermute | solution.py:14
  93.9 3.6 collective-permute-start.14
  97.6 3.1 collective-permute-start.10
  102.3 3.0 collective-permute-start.2
  105.9 3.0 collective-permute-start.19
  114.5 4.3 collective-permute-start.6
  134.3 2.8 reduce_sum.123
  147.1 3.3 collective-permute-start.23
  198.9 2.3 copy.179
  201.2 4.9 collective-permute-start.27
  230.6 2.5 convert_reduce_fusion
  242.5 2.3 copy.182
  244.8 5.4 %collective-permute-start.28 = (bf16[384,1,1]{0,2,1:T(2,128)(2,1)}, bf16[384,1,1]{0,2,1:T(2,128)(2,1)S(1)}, u32[]{:S(2)}, u32[]{:S(2)}) collective-permute-start(bf16[384,1,1]{0,2,1:T(2,128)(2,1)} %get-tuple-element.158), channel_id=1, source_target_pairs={{0,8},{8,16},{16,24},{1,9},{9,17},{17,25},{2,10},{10,18},{18,26},{... | collective-permute-start | bytes 2312 | tf_op jit(solution)/shard_map/ppermute | solution.py:14
  274.9 3.0 collective-permute-start.31
  307.1 167.6 %all-reduce.3.cloned.1.call-done = (f32[3,3,48,48]{3,2,1,0:T(8,128)}, f32[3,3,96,96]{3,2,1,0:T(8,128)}, f32[3,3,192,192]{3,2,1,0:T(8,128)}, f32[3,3,384,384]{3,2,1,0:T(8,128)}) async-done(((f32[3,3,48,48]{3,2,1,0:T(8,128)}, f32[3,3,96,96]{3,2,1,0:T(8,128)}, f32[3,3,192,192]{3,2,1,0:T(8,128)}, f32[3,3,384,384]{3,2,1,0:T(8,128)}), (f32[3,3,48,48]{3,2,1,0:T(8,128)}, f32[3,3,96,96]{3,2,1,0:T(8,128)}, ...) | async-done | bytes 7050256 | tf_op jit(solution)/shard_map/psum | solution.py:238
  478.0 2.5 multiply_convert_fusion.1
  480.5 4.5 multiply_convert_fusion
  (465 shorter events, 221.2 us)
Async XLA Ops:
  7.2 467.4 %all-reduce.3.cloned.1.call-start = ((), (), s32[]{:S(2)}) async-start(), calls=%async_computation | async-start | bytes 15482880 | tf_op jit(solution)/shard_map/psum | solution.py:238
  8.6 62.2 %collective-permute-start.12 = (bf16[384,1,1]{0,2,1:T(2,128)(2,1)}, bf16[384,1,1]{0,2,1:T(2,128)(2,1)S(1)}, u32[]{:S(2)}, u32[]{:S(2)}) collective-permute-start(bf16[384,1,1]{0,2,1:T(2,128)(2,1)} %get-tuple-element.160), channel_id=1, source_target_pairs={{0,8},{8,16},{16,24},{1,9},{9,17},{17,25},{2,10},{10,18},{18,26},{... | collective-permute-start | bytes 2312 | tf_op jit(solution)/shard_map/ppermute | solution.py:14
  13.5 70.2 %collective-permute-start.13 = (bf16[384,1,1]{0,2,1:T(2,128)(2,1)}, bf16[384,1,1]{0,2,1:T(2,128)(2,1)S(1)}, u32[]{:S(2)}, u32[]{:S(2)}) collective-permute-start(bf16[384,1,1]{0,2,1:T(2,128)(2,1)} %get-tuple-element.161), channel_id=1, source_target_pairs={{8,0},{16,8},{24,16},{9,1},{17,9},{25,17},{10,2},{18,10},{26,18},{... | collective-permute-start | bytes 2312 | tf_op jit(solution)/shard_map/ppermute | solution.py:17
  16.2 39.6 %collective-permute-start.8 = (bf16[192,2,1]{0,2,1:T(2,128)(2,1)}, bf16[192,2,1]{0,2,1:T(2,128)(2,1)S(1)}, u32[]{:S(2)}, u32[]{:S(2)}) collective-permute-start(bf16[192,2,1]{0,2,1:T(2,128)(2,1)} %get-tuple-element.156), channel_id=1, source_target_pairs={{0,8},{8,16},{16,24},{1,9},{9,17},{17,25},{2,10},{10,18},{18,26},{... | collective-permute-start | bytes 2312 | tf_op jit(solution)/shard_map/ppermute | solution.py:14
  20.8 39.3 %collective-permute-start.9 = (bf16[192,2,1]{0,2,1:T(2,128)(2,1)S(1)}, bf16[192,2,1]{0,2,1:T(2,128)(2,1)S(1)}, u32[]{:S(2)}, u32[]{:S(2)}) collective-permute-start(bf16[192,2,1]{0,2,1:T(2,128)(2,1)S(1)} %get-tuple-element.157), channel_id=1, source_target_pairs={{8,0},{16,8},{24,16},{9,1},{17,9},{25,17},{10,2},{18,10},{26,18},{... | collective-permute-start | bytes 2312 | tf_op jit(solution)/shard_map/ppermute | solution.py:17
  24.4 49.2 %collective-permute-start.4 = (bf16[96,4,1]{2,0,1:T(8,128)(2,1)}, bf16[96,4,1]{2,0,1:T(8,128)(2,1)}, u32[]{:S(2)}, u32[]{:S(2)}) collective-permute-start(bf16[96,4,1]{2,0,1:T(8,128)(2,1)} %get-tuple-element.136), channel_id=1, source_target_pairs={{0,8},{8,16},{16,24},{1,9},{9,17},{17,25},{2,10},{10,18},{18,26},{... | collective-permute-start | bytes 2312 | tf_op jit(solution)/shard_map/ppermute | solution.py:14
  62.9 16.2 %collective-permute-start.5 = (bf16[96,4,1]{2,0,1:T(8,128)(2,1)S(1)}, bf16[96,4,1]{2,0,1:T(8,128)(2,1)S(1)}, u32[]{:S(2)}, u32[]{:S(2)}) collective-permute-start(bf16[96,4,1]{2,0,1:T(8,128)(2,1)S(1)} %copy-done.55), channel_id=1, source_target_pairs={{8,0},{16,8},{24,16},{9,1},{17,9},{25,17},{10,2},{18,10},{26,18},{... | collective-permute-start | bytes 2312 | tf_op jit(solution)/shard_map/ppermute | solution.py:17
  65.6 28.4 %collective-permute-start = (bf16[48,8,1]{2,0,1:T(8,128)(2,1)S(1)}, bf16[48,8,1]{2,0,1:T(8,128)(2,1)S(1)}, u32[]{:S(2)}, u32[]{:S(2)}) collective-permute-start(bf16[48,8,1]{2,0,1:T(8,128)(2,1)S(1)} %copy-done.54), channel_id=1, source_target_pairs={{0,8},{8,16},{16,24},{1,9},{9,17},{17,25},{2,10},{10,18},{18,26},{... | collective-permute-start | bytes 2312 | tf_op jit(solution)/shard_map/ppermute | solution.py:14
  70.8 26.8 %collective-permute-start.1 = (bf16[48,8,1]{2,0,1:T(8,128)(2,1)S(1)}, bf16[48,8,1]{2,0,1:T(8,128)(2,1)S(1)}, u32[]{:S(2)}, u32[]{:S(2)}) collective-permute-start(bf16[48,8,1]{2,0,1:T(8,128)(2,1)S(1)} %copy-done.53), channel_id=1, source_target_pairs={{8,0},{16,8},{24,16},{9,1},{17,9},{25,17},{10,2},{18,10},{26,18},{... | collective-permute-start | bytes 2312 | tf_op jit(solution)/shard_map/ppermute | solution.py:17
  73.6 16.1 %collective-permute-start.20 = (bf16[96,4,1]{2,0,1:T(8,128)(2,1)S(1)}, bf16[96,4,1]{2,0,1:T(8,128)(2,1)S(1)}, u32[]{:S(2)}, u32[]{:S(2)}) collective-permute-start(bf16[96,4,1]{2,0,1:T(8,128)(2,1)S(1)} %copy-done.57), channel_id=1, source_target_pairs={{0,8},{8,16},{16,24},{1,9},{9,17},{17,25},{2,10},{10,18},{18,26},{... | collective-permute-start | bytes 2312 | tf_op jit(solution)/shard_map/ppermute | solution.py:14
  83.6 17.4 %collective-permute-start.16 = (bf16[48,8,1]{2,0,1:T(8,128)(2,1)S(1)}, bf16[48,8,1]{2,0,1:T(8,128)(2,1)S(1)}, u32[]{:S(2)}, u32[]{:S(2)}) collective-permute-start(bf16[48,8,1]{2,0,1:T(8,128)(2,1)S(1)} %get-tuple-element.104), channel_id=1, source_target_pairs={{0,8},{8,16},{16,24},{1,9},{9,17},{17,25},{2,10},{10,18},{18,26},{... | collective-permute-start | bytes 2312 | tf_op jit(solution)/shard_map/ppermute | solution.py:14
  89.7 12.6 %collective-permute-start.17 = (bf16[48,8,1]{2,0,1:T(8,128)(2,1)S(1)}, bf16[48,8,1]{2,0,1:T(8,128)(2,1)S(1)}, u32[]{:S(2)}, u32[]{:S(2)}) collective-permute-start(bf16[48,8,1]{2,0,1:T(8,128)(2,1)S(1)} %get-tuple-element.105), channel_id=1, source_target_pairs={{8,0},{16,8},{24,16},{9,1},{17,9},{25,17},{10,2},{18,10},{26,18},{... | collective-permute-start | bytes 2312 | tf_op jit(solution)/shard_map/ppermute | solution.py:17
  91.0 176.5 %collective-permute-start.15 = (bf16[384,1,34]{0,2,1:T(8,128)(2,1)}, bf16[384,1,34]{0,2,1:T(8,128)(2,1)}, u32[]{:S(2)}, u32[]{:S(2)}) collective-permute-start(bf16[384,1,34]{0,2,1:T(8,128)(2,1)} %pad_maximum_fusion.34), channel_id=1, source_target_pairs={{1,0},{2,1},{3,2},{4,3},{5,4},{6,5},{7,6},{9,8},{10,9},{11,10},{12... | collective-permute-start | bytes 78344 | tf_op jit(solution)/shard_map/ppermute | solution.py:17
  93.9 171.6 %collective-permute-start.14 = (bf16[384,1,34]{0,2,1:T(8,128)(2,1)}, bf16[384,1,34]{0,2,1:T(8,128)(2,1)}, u32[]{:S(2)}, u32[]{:S(2)}) collective-permute-start(bf16[384,1,34]{0,2,1:T(8,128)(2,1)} %pad_maximum_fusion.34), channel_id=1, source_target_pairs={{0,1},{1,2},{2,3},{3,4},{4,5},{5,6},{6,7},{8,9},{9,10},{10,11},{11... | collective-permute-start | bytes 78344 | tf_op jit(solution)/shard_map/ppermute | solution.py:14
  97.6 103.6 %collective-permute-start.10 = (bf16[192,1,66]{0,2,1:T(8,128)(2,1)}, bf16[192,1,66]{0,2,1:T(8,128)(2,1)}, u32[]{:S(2)}, u32[]{:S(2)}) collective-permute-start(bf16[192,1,66]{0,2,1:T(8,128)(2,1)} %get-tuple-element.140), channel_id=1, source_target_pairs={{0,1},{1,2},{2,3},{3,4},{4,5},{5,6},{6,7},{8,9},{9,10},{10,11},{11... | collective-permute-start | bytes 76040 | tf_op jit(solution)/shard_map/ppermute | solution.py:14
  113.2 33.9 %collective-permute-start.7 = (bf16[96,1,130]{2,0,1:T(8,128)(2,1)}, bf16[96,1,130]{2,0,1:T(8,128)(2,1)}, u32[]{:S(2)}, u32[]{:S(2)}) collective-permute-start(bf16[96,1,130]{2,0,1:T(8,128)(2,1)} %get-tuple-element.84), channel_id=1, source_target_pairs={{1,0},{2,1},{3,2},{4,3},{5,4},{6,5},{7,6},{9,8},{10,9},{11,10},{12... | collective-permute-start | bytes 74888 | tf_op jit(solution)/shard_map/ppermute | solution.py:17
  114.5 35.9 %collective-permute-start.6 = (bf16[96,1,130]{2,0,1:T(8,128)(2,1)}, bf16[96,1,130]{2,0,1:T(8,128)(2,1)}, u32[]{:S(2)}, u32[]{:S(2)}) collective-permute-start(bf16[96,1,130]{2,0,1:T(8,128)(2,1)} %get-tuple-element.85), channel_id=1, source_target_pairs={{0,1},{1,2},{2,3},{3,4},{4,5},{5,6},{6,7},{8,9},{9,10},{10,11},{11... | collective-permute-start | bytes 74888 | tf_op jit(solution)/shard_map/ppermute | solution.py:14
  154.1 52.0 %collective-permute-start.11 = (bf16[192,1,66]{0,2,1:T(8,128)(2,1)}, bf16[192,1,66]{0,2,1:T(8,128)(2,1)}, u32[]{:S(2)}, u32[]{:S(2)}) collective-permute-start(bf16[192,1,66]{0,2,1:T(8,128)(2,1)} %get-tuple-element.141), channel_id=1, source_target_pairs={{1,0},{2,1},{3,2},{4,3},{5,4},{6,5},{7,6},{9,8},{10,9},{11,10},{12... | collective-permute-start | bytes 76040 | tf_op jit(solution)/shard_map/ppermute | solution.py:17
  155.4 62.7 %collective-permute-start.26 = (bf16[192,1,66]{0,2,1:T(8,128)(2,1)}, bf16[192,1,66]{0,2,1:T(8,128)(2,1)}, u32[]{:S(2)}, u32[]{:S(2)}) collective-permute-start(bf16[192,1,66]{0,2,1:T(8,128)(2,1)} %get-tuple-element.138), channel_id=1, source_target_pairs={{1,0},{2,1},{3,2},{4,3},{5,4},{6,5},{7,6},{9,8},{10,9},{11,10},{12... | collective-permute-start | bytes 76040 | tf_op jit(solution)/shard_map/ppermute | solution.py:17
  201.2 17.0 %collective-permute-start.27 = (bf16[192,1,66]{0,2,1:T(8,128)(2,1)}, bf16[192,1,66]{0,2,1:T(8,128)(2,1)}, u32[]{:S(2)}, u32[]{:S(2)}) collective-permute-start(bf16[192,1,66]{0,2,1:T(8,128)(2,1)} %get-tuple-element.139), channel_id=1, source_target_pairs={{0,1},{1,2},{2,3},{3,4},{4,5},{5,6},{6,7},{8,9},{9,10},{10,11},{11... | collective-permute-start | bytes 76040 | tf_op jit(solution)/shard_map/ppermute | solution.py:14
  244.8 29.6 %collective-permute-start.28 = (bf16[384,1,1]{0,2,1:T(2,128)(2,1)}, bf16[384,1,1]{0,2,1:T(2,128)(2,1)S(1)}, u32[]{:S(2)}, u32[]{:S(2)}) collective-permute-start(bf16[384,1,1]{0,2,1:T(2,128)(2,1)} %get-tuple-element.158), channel_id=1, source_target_pairs={{0,8},{8,16},{16,24},{1,9},{9,17},{17,25},{2,10},{10,18},{18,26},{... | collective-permute-start | bytes 2312 | tf_op jit(solution)/shard_map/ppermute | solution.py:14
  250.2 24.1 %collective-permute-start.29 = (bf16[384,1,1]{0,2,1:T(2,128)(2,1)}, bf16[384,1,1]{0,2,1:T(2,128)(2,1)S(1)}, u32[]{:S(2)}, u32[]{:S(2)}) collective-permute-start(bf16[384,1,1]{0,2,1:T(2,128)(2,1)} %get-tuple-element.159), channel_id=1, source_target_pairs={{8,0},{16,8},{24,16},{9,1},{17,9},{25,17},{10,2},{18,10},{26,18},{... | collective-permute-start | bytes 2312 | tf_op jit(solution)/shard_map/ppermute | solution.py:17
  274.9 30.7 %collective-permute-start.31 = (bf16[384,1,34]{0,2,1:T(8,128)(2,1)}, bf16[384,1,34]{0,2,1:T(8,128)(2,1)S(1)}, u32[]{:S(2)}, u32[]{:S(2)}) collective-permute-start(bf16[384,1,34]{0,2,1:T(8,128)(2,1)} %pad_maximum_fusion.35), channel_id=1, source_target_pairs={{0,1},{1,2},{2,3},{3,4},{4,5},{5,6},{6,7},{8,9},{9,10},{10,11},{11... | collective-permute-start | bytes 78344 | tf_op jit(solution)/shard_map/ppermute | solution.py:14
  277.9 27.3 %collective-permute-start.30 = (bf16[384,1,34]{0,2,1:T(8,128)(2,1)}, bf16[384,1,34]{0,2,1:T(8,128)(2,1)S(1)}, u32[]{:S(2)}, u32[]{:S(2)}) collective-permute-start(bf16[384,1,34]{0,2,1:T(8,128)(2,1)} %pad_maximum_fusion.35), channel_id=1, source_target_pairs={{1,0},{2,1},{3,2},{4,3},{5,4},{6,5},{7,6},{9,8},{10,9},{11,10},{12... | collective-permute-start | bytes 78344 | tf_op jit(solution)/shard_map/ppermute | solution.py:17
  (84 other events, 1136.7 us)
Sparse Core Ops, SparseCore 0:
  294.6 180.0 all-reduce.2
where the time goes:
time: 497 us; the launch traced here: 492 us
  waiting for transfers between devices  169 us (34%)
  matrix products  108 us (22%)
  starting transfers between devices  88.4 us (18%)
  local copies, waits for them, and re-layouts  56.4 us (11%)
  other arithmetic  53.5 us (11%)
  between operations  16.3 us (3%)
    psum x1, waiting for transfers between devices, local(): lax.psum((partials[0], partials[1], partials[2], partials[3]), ('branch',...  168 us
    ppermute x16, starting transfers between devices, extended_2(): lax.ppermute(lax.slice_in_dim(block, block.shape[dim] - width, None, axis...  67.6 us
    dot_general x36, matrix products, kernel_taps(): lax.dot_general(flattened, window, (((1,), (1,)), ((), ())), preferred_el...  39.2 us
    dot_general x36, matrix products, forward_taps(): jnp.dot(kernel[row_off, col_off], window, preferred_element_type=jnp.floa...  23.7 us
    ppermute x16, starting transfers between devices, extended_2(): lax.ppermute(lax.slice_in_dim(block, 0, width, axis=dim), axis, backward)  20.8 us
    dot_general x36, matrix products, adjoint_taps(): lax.dot_general(kernel[row_off, col_off], window, (((0,), (0,)), ((), ())...  19.9 us
    broadcast_in_dim x16, local copies, waits for them, and re-layouts, upsample(): jnp.broadcast_to(values[:, :, None, :, None], (channels, height, factor,...  12.3 us
    concatenate x16, other arithmetic, extended_2(): block = jnp.concatenate([low, block, high], axis=dim)  10.9 us
  transfers between devices with their start and end apart: 33, of which 2 were waited for; matrix products, arithmetic and copies ran while one was open for 42% of the time, Pallas kernels for 0%

commit v1 on v0

v1 whole, which is shorter than its diff:
```python
import functools
import math

import jax
import jax.numpy as jnp
from jax import lax
from jax.experimental import pallas as pl
from jax.experimental.pallas import tpu as pltpu
from jax.sharding import PartitionSpec as P

BF = jnp.bfloat16
F32 = jnp.float32
LEFT = 8
PACK = 384


def dot(a, b, ca=1, cb=0):
    return lax.dot_general(a, b, (((ca,), (cb,)), ((), ())), preferred_element_type=F32)


def source_offset(channels, target, source):
    return sum(channels[k] for k in range(source) if k != target)


def call(body, outs, args, scratch=(), flops=10**8, nbytes=10**6):
    return pl.pallas_call(
        body,
        out_shape=outs,
        in_specs=[pl.BlockSpec(memory_space=pltpu.VMEM) for _ in args],
        out_specs=[pl.BlockSpec(memory_space=pltpu.VMEM) for _ in outs],
        scratch_shapes=list(scratch),
        compiler_params=pltpu.CompilerParams(vmem_limit_bytes=48 * 1024 * 1024),
        cost_estimate=pl.CostEstimate(flops=flops, bytes_accessed=nbytes, transcendentals=0),
    )(*args)


def sds(shape, dtype):
    return jax.ShapeDtypeStruct(shape, dtype)


def group_matrix(groups, cells, factor, transposed=False):
    shape = (cells, groups) if transposed else (groups, cells)
    g = lax.broadcasted_iota(jnp.int32, shape, 1 if transposed else 0)
    c = lax.broadcasted_iota(jnp.int32, shape, 0 if transposed else 1)
    return jnp.where((c >= g * factor) & (c < g * factor + factor), 1.0, 0.0).astype(BF)


def row_pack(row, channels):
    blocks = PACK // channels
    part = row.shape[0] // blocks
    return jnp.concatenate([row[k * part : (k + 1) * part] for k in range(blocks)], axis=1)


def row_unpack(packed, channels):
    blocks = PACK // channels
    return jnp.concatenate(
        [packed[:, k * channels : (k + 1) * channels] for k in range(blocks)], axis=0
    )


def col_rows(heights):
    starts, at = [], 0
    for h in heights:
        starts.append(at)
        at += h
    return starts


def upstream_kernel(dims, *refs):
    heights, widths, channels = dims
    x_refs, d_refs, g_refs, f_refs = refs[0:4], refs[4:8], refs[8:12], refs[12:16]
    xt4, xt8 = refs[16], refs[17]
    up_refs, sc_refs = refs[18:22], refs[22:26]
    top, bot, left, right = refs[26:30]
    dt = [None] * 4
    xt = [None] * 4
    for b in range(4):
        if b < 2:
            eye = group_matrix(channels[b], channels[b], 1)
            xs = jnp.swapaxes(x_refs[b][...].astype(F32), 0, 1).astype(BF)
            ds = jnp.swapaxes(d_refs[b][...].astype(F32), 0, 1).astype(BF)
            xt[b] = [dot(xs[r], eye, 0, 0).astype(BF) for r in range(heights[b])]
            dt[b] = [dot(ds[r], eye, 0, 0).astype(BF) for r in range(heights[b])]
            for r in range(heights[b]):
                (xt4, xt8)[b][r] = xt[b][r]
        else:
            xt[b] = [x_refs[b][r] for r in range(heights[b])]
            dt[b] = [d_refs[b][r] for r in range(heights[b])]
    mixers = [f_refs[j][...] for j in range(4)]

    def block(j, i):
        off = source_offset(channels, j, i)
        if j == 3:
            return mixers[3][off : off + channels[i]]
        return mixers[j][:, off : off + channels[i]]

    acc = [[dt[i][r].astype(F32) for r in range(heights[i])] for i in range(4)]
    for j in range(4):
        for i in range(j + 1, 4):
            f = 2 ** (i - j)
            pool = group_matrix(widths[i], widths[j], f)
            mat = block(j, i)
            for r in range(heights[i]):
                s = dot(pool, dt[j][r * f])
                for k in range(1, f):
                    s = s + dot(pool, dt[j][r * f + k])
                acc[i][r] = acc[i][r] + dot(s.astype(BF), mat)
        for i in range(j):
            f = 2 ** (j - i)
            spread = group_matrix(widths[j], widths[i], f, True)
            mat = block(j, i)
            for r in range(heights[j]):
                z = dot(spread, dt[j][r]).astype(BF)
                if j == 3:
                    v = dot(z, mat, 1, 1)
                else:
                    v = dot(z, mat)
                v = v * (1.0 / (f * f))
                for k in range(f):
                    acc[i][r * f + k] = acc[i][r * f + k] + v
    starts = col_rows(heights)
    left[...] = jnp.zeros(left.shape, F32).astype(BF)
    right[...] = jnp.zeros(right.shape, F32).astype(BF)
    top[:, 4 * 32 :, :] = jnp.zeros((2, 16, PACK), F32).astype(BF)
    bot[:, 4 * 32 :, :] = jnp.zeros((2, 16, PACK), F32).astype(BF)
    for b in range(4):
        h, w, c = heights[b], widths[b], channels[b]
        gain = g_refs[b][...]
        act, scl = [], []
        for r in range(h):
            up_refs[b][r] = acc[b][r]
            s = (gain * acc[b][r]).astype(BF)
            sc_refs[b][r] = s
            act.append(jnp.maximum(xt[b][r].astype(F32), 0.0))
            scl.append(s.astype(F32))
        for n, rows in enumerate((act, scl)):
            for out, row in ((top, rows[0]), (bot, rows[h - 1])):
                out[n, b * 32 : (b + 1) * 32, :] = row_pack(row, c).astype(BF)
                out[n, 128 + b : 129 + b, :c] = row[0:1].astype(BF)
                out[n, 136 + b : 137 + b, :c] = row[w - 1 : w].astype(BF)
            firsts = jnp.concatenate([row[0:1] for row in rows], axis=0)
            lasts = jnp.concatenate([row[w - 1 : w] for row in rows], axis=0)
            left[n, starts[b] : starts[b] + h, :c] = firsts.astype(BF)
            right[n, starts[b] : starts[b] + h, :c] = lasts.astype(BF)


def fill(scr, n, b, dims, interior, top, bot, left, right):
    heights, widths, channels = dims
    h, w, c = heights[b], widths[b], channels[b]
    start = col_rows(heights)[b]
    for r in range(h):
        scr[r + 1, LEFT : LEFT + w, :] = interior(r)
    for edge, at in ((top, 0), (bot, h + 1)):
        packed = edge[n, b * 32 : (b + 1) * 32, :].astype(F32)
        scr[at, LEFT : LEFT + w, :] = row_unpack(packed, c)
    for edge, at in ((left, LEFT - 1), (right, LEFT + w)):
        vals = edge[n].astype(F32)
        for r in range(h):
            scr[r + 1, at : at + 1, :] = vals[start + r : start + r + 1, :c]
        scr[0, at : at + 1, :] = vals[16 + b : 17 + b, :c]
        scr[h + 1, at : at + 1, :] = vals[24 + b : 25 + b, :c]


def shifted(scr, h, w, q):
    return [scr[r, LEFT - 1 + q : LEFT - 1 + q + w, :].astype(BF) for r in range(h + 2)]


def stack(rows):
    return rows[0] if len(rows) == 1 else jnp.concatenate(rows, axis=0)


def weight_grads_kernel(dims, *refs):
    heights, widths, channels = dims
    x_refs, sc_refs = refs[0:3], refs[3:6]
    top, bot, left, right = refs[6:10]
    out = refs[10]
    scrs = refs[11:14]
    c0, c1, c2 = channels[0], channels[1], channels[2]
    for b in range(3):
        h, w, c = heights[b], widths[b], channels[b]
        fill(
            scrs[b], 0, b, dims,
            lambda r: jnp.maximum(x_refs[b][r].astype(F32), 0.0), top, bot, left, right,
        )
        s_all = stack([sc_refs[b][r] for r in range(h)])
        for q in range(3):
            rows = shifted(scrs[b], h, w, q)
            for p in range(3):
                g = dot(s_all, stack(rows[p : p + h]), 0, 0)
                tap = p * 3 + q
                if b == 2:
                    out[tap * c2 : (tap + 1) * c2, :] = g[:, :128].astype(BF)
                    half = c2 // 2
                    at = 9 * c2 + tap * half
                    both = jnp.concatenate([g[:half, 128:], g[half:, 128:]], axis=1)
                    out[at : at + half, :] = both.astype(BF)
                elif b == 1:
                    at = 9 * c2 * 3 // 2 + tap * c1
                    out[at : at + c1, :c1] = g.astype(BF)
                else:
                    at = 9 * c2 * 3 // 2 + 9 * c1 + (tap // 2) * c0
                    lane = 64 * (tap % 2)
                    out[at : at + c0, lane : lane + c0] = g.astype(BF)


def maps_kernel(dims, *refs):
    heights, widths, channels = dims
    x_refs, sc_refs, up_refs = refs[0:4], refs[4:8], refs[8:12]
    g_refs, f_refs, k_refs = refs[12:16], refs[16:20], refs[20:24]
    top, bot, left, right = refs[24:28]
    merged_refs, back_refs = refs[28:32], refs[32:36]
    act_scrs, grad_scrs = refs[36:40], refs[40:44]
    wide = refs[44:48]
    units = []

    def emit(b, out, rows):
        if b >= 2:
            for r in range(heights[b]):
                out[r] = rows[r].astype(BF)
            return
        stage = wide[b]
        for r in range(heights[b]):
            stage[r] = rows[r].T
        out[...] = jnp.swapaxes(stage[...], 0, 1).astype(BF)

    for b in range(4):
        h, w, c = heights[b], widths[b], channels[b]
        fill(
            act_scrs[b], 0, b, dims,
            lambda r: jnp.maximum(x_refs[b][r].astype(F32), 0.0), top, bot, left, right,
        )
        fill(
            grad_scrs[b], 1, b, dims,
            lambda r: sc_refs[b][r].astype(F32), top, bot, left, right,
        )
        resp = jnp.zeros((h * w, c), F32)
        adj = jnp.zeros((h * w, c), F32)
        for q in range(3):
            rows = shifted(act_scrs[b], h, w, q)
            grads = shifted(grad_scrs[b], h, w, 2 - q)
            for p in range(3):
                k = k_refs[b][p, q]
                resp = resp + dot(stack(rows[p : p + h]), k, 1, 1)
                adj = adj + dot(stack(grads[2 - p : 2 - p + h]), k)
        gain = g_refs[b][...]
        unit, back = [], []
        for r in range(h):
            x = x_refs[b][r].astype(F32)
            unit.append((x + gain * resp[r * w : (r + 1) * w]).astype(BF))
            back.append(up_refs[b][r] + jnp.where(x > 0, adj[r * w : (r + 1) * w], 0.0))
        units.append(unit)
        emit(b, back_refs[b], back)
    mixers = [f_refs[j][...] for j in range(4)]

    def mix(v, j, i):
        off = source_offset(channels, j, i)
        if j == 3:
            return dot(v, mixers[3][off : off + channels[i]])
        return dot(v, mixers[j][:, off : off + channels[i]], 1, 1)

    sums = [[u.astype(F32) for u in units[j]] for j in range(4)]
    for i in range(4):
        for j in range(i + 1, 4):
            f = 2 ** (j - i)
            pool = group_matrix(widths[j], widths[i], f)
            for r in range(heights[j]):
                s = dot(pool, units[i][r * f])
                for k in range(1, f):
                    s = s + dot(pool, units[i][r * f + k])
                s = (s * (1.0 / (f * f))).astype(BF)
                sums[j][r] = sums[j][r] + mix(s, j, i)
        for j in range(i):
            f = 2 ** (i - j)
            spread = group_matrix(widths[i], widths[j], f, True)
            for r in range(heights[i]):
                v = mix(dot(spread, units[i][r]).astype(BF), j, i)
                for k in range(f):
                    sums[j][r * f + k] = sums[j][r * f + k] + v
    for j in range(4):
        emit(j, merged_refs[j], sums[j])


def gather_positions(n_branch, n_chip):
    return [(m, l, k) for m in range(2) for l in range(n_branch) for k in range(n_chip)]


def finish_kernel(dims, n_branch, n_chip, scales, *refs):
    heights, widths, channels = dims
    idx, own, other = refs[0], refs[1], refs[2]
    outs = refs[3:7]
    flat, act, scl, acc = refs[7:11]
    size = flat.shape[1]
    c0, c1, c2, c3 = channels
    w3 = widths[3]
    rows, cols = 2 * n_chip, n_branch * w3
    core, branch, chip = idx[0], idx[1], idx[2]
    act[0] = jnp.zeros(act.shape[1:], F32)
    act[rows + 1] = jnp.zeros(act.shape[1:], F32)
    for r in range(rows):
        act[r + 1, 0:LEFT, :] = jnp.zeros((LEFT, c3), F32)
        act[r + 1, LEFT + cols :, :] = jnp.zeros((8, c3), F32)
    for m, l, k in gather_positions(n_branch, n_chip):
        src = own if m == 0 else other
        c = (core + m) % 2
        b = (branch + l) % n_branch
        z = (chip + k) % n_chip
        piece = (c * n_branch + b) * n_chip + z
        flat[piece] = src[l, k, 0:size, :]
        r = z * 2 + c
        off = pl.multiple_of(b * w3, w3)
        for t in range(3):
            at = size + t * w3
            act[r + 1, pl.ds(LEFT + off, w3), t * 128 : (t + 1) * 128] = src[
                l, k, at : at + w3, :
            ].astype(F32)
            at = size + (3 + t) * w3
            scl[r, pl.ds(off, w3), t * 128 : (t + 1) * 128] = src[l, k, at : at + w3, :]
    full = flat[...].astype(F32).reshape(flat.shape[0] * size, 128)
    base1 = 9 * c2 * 3 // 2
    base0 = base1 + 9 * c1
    half = c2 // 2
    for tap in range(9):
        p, q = tap // 3, tap % 3
        outs[2][p, q, :, 0:128] = (full[tap * c2 : (tap + 1) * c2] * scales[2]).astype(BF)
        at = 9 * c2 + tap * half
        both = full[at : at + half]
        tail = jnp.concatenate([both[:, :64], both[:, 64:]], axis=0)
        outs[2][p, q, :, 128:c2] = (tail * scales[2]).astype(BF)
        at = base1 + tap * c1
        outs[1][p, q] = (full[at : at + c1, :c1] * scales[1]).astype(BF)
        at = base0 + (tap // 2) * c0
        lane = 64 * (tap % 2)
        outs[0][p, q] = (full[at : at + c0, lane : lane + c0] * scales[0]).astype(BF)
    for q in range(3):
        for p in range(3):
            acc[...] = jnp.zeros(acc.shape, F32)
            step = 4 if rows % 4 == 0 else 2

            @pl.loop(0, rows // step)
            def _(t, p=p, q=q, step=step):
                win = jnp.concatenate(
                    [
                        act[t * step + s + p, LEFT - 1 + q : LEFT - 1 + q + cols, :].astype(BF)
                        for s in range(step)
                    ],
                    axis=0,
                )
                grad = jnp.concatenate([scl[t * step + s] for s in range(step)], axis=0)
                acc[...] += dot(grad, win, 0, 0)

            outs[3][p, q] = (acc[...] * scales[3]).astype(BF)


def local(*args):
    maps, kernels, gains, mixers, cotans = (args[4 * k : 4 * k + 4] for k in range(5))
    n_rows, n_branch = lax.axis_size("rows"), lax.axis_size("branch")
    n_chip = n_rows // 2
    channels = [a.shape[0] for a in maps]
    heights = [a.shape[1] for a in maps]
    widths = [a.shape[2] for a in maps]
    dims = (heights, widths, channels)
    last = lambda a: jnp.transpose(a, (1, 2, 0))
    xs = [maps[0], maps[1], last(maps[2]), last(maps[3])]
    ds = [cotans[0], cotans[1], last(cotans[2]), last(cotans[3])]
    gs = [g.reshape(1, -1) for g in gains]
    fs = [mixers[0], mixers[1], mixers[2], mixers[3].T]
    shapes = [(heights[b], widths[b], channels[b]) for b in range(4)]
    edge = sds((2, 144, PACK), BF)
    side = sds((2, 16, PACK), BF)
    outs = call(
        functools.partial(upstream_kernel, dims),
        [sds(shapes[0], BF), sds(shapes[1], BF)]
        + [sds(s, F32) for s in shapes]
        + [sds(s, BF) for s in shapes]
        + [edge, edge, side, side],
        xs + ds + gs + fs,
    )
    xt = [outs[0], outs[1], xs[2], xs[3]]
    ups, scs = outs[2:6], outs[6:10]
    top, bot, left, right = outs[10:14]
    down = [(i, i + 1) for i in range(n_rows - 1)]
    rise = [(i + 1, i) for i in range(n_rows - 1)]
    from_top = lax.ppermute(bot, "rows", down)
    from_bot = lax.ppermute(top, "rows", rise)
    left = jnp.concatenate([left, from_top[:, 128:136], from_bot[:, 128:136]], axis=1)
    right = jnp.concatenate([right, from_top[:, 136:144], from_bot[:, 136:144]], axis=1)
    ahead = [(i, i + 1) for i in range(n_branch - 1)]
    behind = [(i + 1, i) for i in range(n_branch - 1)]
    from_left = lax.ppermute(right, "branch", ahead)
    from_right = lax.ppermute(left, "branch", behind)
    edges = [from_top, from_bot, from_left, from_right]

    pad = lambda b: pltpu.VMEM((heights[b] + 2, widths[b] + 16, channels[b]), F32)
    pieces = 2 * n_branch * n_chip
    packed_rows = 9 * (channels[2] * 3 // 2 + channels[1]) + 5 * channels[0]
    size = -(-packed_rows // (8 * pieces)) * 8
    (partial,) = call(
        functools.partial(weight_grads_kernel, dims),
        [sds((pieces * size, 128), BF)],
        xt[:3] + list(scs[:3]) + edges,
        [pad(0), pad(1), pad(2)],
    )
    row_id = lax.axis_index("rows")
    core, chip, branch = row_id % 2, row_id // 2, lax.axis_index("branch")

    def reduce_stage(values, axis, n, me, pairs):
        own = lax.dynamic_index_in_dim(values, me, 0, False)
        got = [
            lax.ppermute(lax.dynamic_index_in_dim(values, (me + k) % n, 0, False), axis, pairs(k))
            for k in range(1, n)
        ]
        out = own.astype(F32)
        for g in got:
            out = out + g.astype(F32)
        return out.astype(BF)

    swap = lambda k: [(i, i ^ 1) for i in range(n_rows)]
    around = lambda k: [(i, (i + k) % n_branch) for i in range(n_branch)]
    along = lambda k: [(i, (i + 2 * k) % n_rows) for i in range(n_rows)]
    part = partial.reshape(2, n_branch, n_chip, -1, 128)
    part = reduce_stage(part, "rows", 2, core, swap)
    part = reduce_stage(part, "branch", n_branch, branch, around)
    part = reduce_stage(part, "rows", n_chip, chip, along)

    act32 = jnp.maximum(xt[3], jnp.zeros((), BF)).reshape(widths[3], channels[3])
    lanes = lambda a: [a[:, k * 128 : (k + 1) * 128] for k in range(channels[3] // 128)]
    mine = jnp.concatenate(
        [part] + lanes(act32) + lanes(scs[3].reshape(widths[3], channels[3])), axis=0
    )

    def gather_stage(values, axis, n, pairs):
        back = lambda k: [(t, s) for s, t in pairs(k)]
        return jnp.stack([values] + [lax.ppermute(values, axis, back(k)) for k in range(1, n)])

    got = gather_stage(mine, "rows", n_chip, along)
    got = gather_stage(got, "branch", n_branch, around)
    other = lax.ppermute(got, "rows", swap(1))

    merged_back = call(
        functools.partial(maps_kernel, dims),
        [sds(maps[0].shape, BF), sds(maps[1].shape, BF), sds(shapes[2], BF), sds(shapes[3], BF)] * 2,
        xt + list(scs) + list(ups) + gs + fs + list(kernels) + edges,
        [pad(b) for b in range(4)] * 2
        + [pltpu.VMEM((heights[b], channels[b], widths[b]), F32) for b in range(4)],
    )
    scales = [
        1.0 / math.sqrt(heights[b] * n_rows * widths[b] * n_branch) for b in range(4)
    ]
    idx = jnp.stack([core, branch, chip]).astype(jnp.int32)
    cols = n_branch * widths[3]
    kgrads = pl.pallas_call(
        functools.partial(finish_kernel, dims, n_branch, n_chip, scales),
        out_shape=[sds(k.shape, BF) for k in kernels],
        in_specs=[pl.BlockSpec(memory_space=pltpu.SMEM)]
        + [pl.BlockSpec(memory_space=pltpu.VMEM)] * 2,
        out_specs=[pl.BlockSpec(memory_space=pltpu.VMEM)] * 4,
        scratch_shapes=[
            pltpu.VMEM((pieces, size, 128), BF),
            pltpu.VMEM((n_rows + 2, cols + 16, channels[3]), F32),
            pltpu.VMEM((n_rows, cols, channels[3]), BF),
            pltpu.VMEM((channels[3], channels[3]), F32),
        ],
        compiler_params=pltpu.CompilerParams(vmem_limit_bytes=60 * 1024 * 1024),
        cost_estimate=pl.CostEstimate(flops=3 * 10**9, bytes_accessed=10**7, transcendentals=0),
    )(idx, got, other)
    unlast = lambda a: jnp.transpose(a, (2, 0, 1))
    m, bk = merged_back[:4], merged_back[4:]
    return (
        m[0], m[1], unlast(m[2]), unlast(m[3]),
        bk[0], bk[1], unlast(bk[2]), unlast(bk[3]),
        *kgrads,
    )


def solution(mesh):
    maps = P(None, "rows", "branch")
    in_specs = (maps,) * 4 + (P(),) * 12 + (maps,) * 4
    out_specs = (maps,) * 8 + (P(),) * 4
    return jax.shard_map(
        lambda *args: local(*args),
        mesh=mesh, in_specs=in_specs, out_specs=out_specs, check_vma=False,
    )
```

time: 497 us -> 120 us (0.24)
  waiting for transfers between devices: 169 us -> 33.3 us
  matrix products: 108 us -> 0 us
  starting transfers between devices: 88.4 us -> 28.9 us
  other arithmetic: 53.5 us -> 3.02 us
  local copies, waits for them, and re-layouts: 56.4 us -> 25 us
  Pallas kernels: 0 us -> 26.7 us
  between operations: 16.3 us -> 1.06 us
    psum x1 -> x0, waiting for transfers between devices: 168 us -> none  [local(): lax.psum((partials[0], partials[1], partials[2], partials[3]), ('branch',...]
    dot_general x132 -> x0, matrix products: 108 us -> none  [the longest x36 39.2 us: kernel_taps(): lax.dot_general(flattened, window, (((1,), (1,)), ((), ())), preferred_el...]
    ppermute x32 -> x18, starting transfers between devices: 88.4 us -> 28.9 us  [the longest x7 12.1 us: reduce_stage(): lax.ppermute(lax.dynamic_index_in_dim(values, (me + k) % n, 0, False), ax...]
    ppermute x32 -> x18, waiting for transfers between devices: 1.44 us -> 33.3 us  [the longest x6 14.5 us: gather_stage(): lax.ppermute(values, axis, back(k))]
    pallas_call x0 -> x4, Pallas kernels: none -> 26.7 us  [the longest x3 15.1 us: call(): pl.pallas_call(body, out_shape=outs, in_specs=[pl.BlockSpec(memory_space=...]
    reduce_sum x15 -> x0, other arithmetic: 19.1 us -> none  [the longest x6 9.6 us: merged_maps(): pooled = results[source].astype(jnp.float32).reshape(width_in, height, fa...]
    unnamed x158 -> x111, local copies, waits for them, and re-layouts: 6.2 us -> 23.5 us
    convert_element_type x14 -> x2, other arithmetic: 16.6 us -> 2.15 us  [reduce_stage(): return out.astype(BF)]
  transfers between devices with their start and end apart: 33 -> 18, of which waited for: 2 -> 13; matrix products, arithmetic and copies ran while one was open for 42% -> 1% of each run, Pallas kernels for 0% -> 9%
where the time goes in v1:
time: 120 us; the launch traced here: 118 us
  waiting for transfers between devices  33.3 us (28%)
  starting transfers between devices  28.9 us (24%)
  Pallas kernels  26.7 us (22%)
  local copies, waits for them, and re-layouts  25 us (21%)
  other arithmetic  3.02 us (3%)
    unnamed x111, local copies, waits for them, and re-layouts  23.5 us
    pallas_call x3, Pallas kernels, call(): pl.pallas_call(body, out_shape=outs, in_specs=[pl.BlockSpec(memory_space=...  15.1 us
    ppermute x6, waiting for transfers between devices, gather_stage(): lax.ppermute(values, axis, back(k))  14.5 us
    ppermute x7, starting transfers between devices, reduce_stage(): lax.ppermute(lax.dynamic_index_in_dim(values, (me + k) % n, 0, False), ax...  12.1 us
    pallas_call x1, Pallas kernels, local(): pl.pallas_call(functools.partial(finish_kernel, dims, n_branch, n_chip, s...  11.6 us
    ppermute x7, waiting for transfers between devices, reduce_stage(): lax.ppermute(lax.dynamic_index_in_dim(values, (me + k) % n, 0, False), ax...  10.6 us
    ppermute x6, starting transfers between devices, gather_stage(): lax.ppermute(values, axis, back(k))  8.35 us
    ppermute x1, waiting for transfers between devices, local(): from_bot = lax.ppermute(top, 'rows', rise)  4.23 us
  transfers between devices with their start and end apart: 18, of which 13 were waited for; matrix products, arithmetic and copies ran while one was open for 1% of the time, Pallas kernels for 9%

profile of v1, /device:TPU:0, one launch (start us, length us, event | category | flops | bytes accessed | tf_op | source)
XLA Modules:
  0.0 118.0 jit_solution(6815054387930367410)
XLA Ops:
  13.8 3.5 %shard_map.283 = (bf16[8,256,48]{2,1,0:T(8,128)(2,1)S(1)}, bf16[4,128,96]{2,1,0:T(8,128)(2,1)S(1)}, f32[8,256,48]{2,1,0:T(8,128)S(1)}, f32[4,128,96]{2,1,0:T(8,1...) custom-call(bf16[48,8,256]{2,1,0:T(8,128)(2,1)S(1)} %copy-done.32, ...), custom_call_target="tpu_custom_call" | custom-call | flops 100000000 | bytes 1000000 | tf_op jit(solution)/shard_map/pallas_call | solution.py:26
  20.0 2.4 %collective-permute-start = (bf16[2,144,384]{2,1,0:T(8,128)(2,1)S(1)}, bf16[2,144,384]{2,1,0:T(8,128)(2,1)S(1)}, u32[]{:S(2)}, u32[]{:S(2)}) collective-permute-start(bf16[2,144,384]{2,1,0:T(8,128)(2,1)S(1)} %get-tuple-element.48), channel_id=1, source_target_pairs={{0,1},{1,2},{2,3},{3,4},{4,5},{5,6},{6,7},{8,9},{9,10},{10,11},{11... | collective-permute-start | bytes 663560 | tf_op jit(solution)/shard_map/ppermute | solution.py:383
  23.7 4.2 %collective-permute-done.1.refs_25_.refs_7_ = bf16[2,144,384]{2,1,0:T(8,128)(2,1)S(1)} collective-permute-done((bf16[2,144,384]{2,1,0:T(8,128)(2,1)S(1)}, bf16[2,144,384]{2,1,0:T(8,128)(2,1)S(1)}, u32[]{:S(2)}, u32[]{:S(2)}) %collective-permute-start.1) | collective-permute-done | bytes 221216 | tf_op jit(solution)/shard_map/ppermute | solution.py:384
  27.9 3.4 %collective-permute-start.2 = (bf16[2,32,384]{2,1,0:T(8,128)(2,1)S(1)}, bf16[2,32,384]{2,1,0:T(8,128)(2,1)S(1)}, u32[]{:S(2)}, u32[]{:S(2)}) collective-permute-start(bf16[2,32,384]{2,1,0:T(8,128)(2,1)S(1)} %pad_maximum_fusion.2), channel_id=1, source_target_pairs={{0,8},{8,16},{16,24},{1,9},{9,17},{17,25},{2,10},{10,18},{18,26},{... | collective-permute-start | bytes 147464 | tf_op jit(solution)/shard_map/ppermute | solution.py:389
  33.7 3.7 %collective-permute-done.3.refs_27_.refs_9_ = bf16[2,32,384]{2,1,0:T(8,128)(2,1)S(1)} collective-permute-done((bf16[2,32,384]{2,1,0:T(8,128)(2,1)S(1)}, bf16[2,32,384]{2,1,0:T(8,128)(2,1)S(1)}, u32[]{:S(2)}, u32[]{:S(2)}) %collective-permute-start.3) | collective-permute-done | bytes 49184 | tf_op jit(solution)/shard_map/ppermute | solution.py:390
  43.1 1.5 %shard_map.285 = bf16[3840,128]{1,0:T(8,128)(2,1)S(1)} custom-call(bf16[8,256,48]{2,1,0:T(8,128)(2,1)S(1)} %get-tuple-element.38.refs_0_, bf16[4,128,96]{2,1,0:T(8,128)(2,1)S(1)} %copy-done.9, bf16[2,64,192]{2,1,0:T(8,128)(2,1)S(1)} %bitcast.57, bf16[8,256,48]{2,1,0:T(8,128)(2,1)S(1)} %get-tuple-element.40.refs_4_.refs_3_, ...), custom_call_target="tpu_custom_call" | custom-call | flops 100000000 | bytes 1000000 | tf_op jit(solution)/shard_map/pallas_call | solution.py:26
  45.4 2.9 %collective-permute-start.4 = (bf16[4,4,120,128]{3,2,1,0:T(8,128)(2,1)}, bf16[4,4,120,128]{3,2,1,0:T(8,128)(2,1)}, u32[]{:S(2)}, u32[]{:S(2)}) collective-permute-start(bf16[4,4,120,128]{3,2,1,0:T(8,128)(2,1)} %dynamic-slice_bitcast_fusion), channel_id=1, source_target_pairs={{0,1},{1,0},{2,3},{3,2},{4,5},{5,4},{6,7},{7,6},{8,9},{9,8},{10,11... | collective-permute-start | bytes 1474568 | tf_op jit(solution)/shard_map/ppermute | solution.py:409
  48.4 1.8 %collective-permute-done.4 = bf16[4,4,120,128]{3,2,1,0:T(8,128)(2,1)} collective-permute-done((bf16[4,4,120,128]{3,2,1,0:T(8,128)(2,1)}, bf16[4,4,120,128]{3,2,1,0:T(8,128)(2,1)}, u32[]{:S(2)}, u32[]{:S(2)}) %collective-permute-start.4) | collective-permute-done | bytes 491552 | tf_op jit(solution)/shard_map/ppermute | solution.py:409
  52.2 2.4 %collective-permute-start.5 = (bf16[4,120,128]{2,1,0:T(8,128)(2,1)S(1)}, bf16[4,120,128]{2,1,0:T(8,128)(2,1)S(1)}, u32[]{:S(2)}, u32[]{:S(2)}) collective-permute-start(bf16[4,120,128]{2,1,0:T(8,128)(2,1)S(1)} %get-tuple-element.64), channel_id=1, source_target_pairs={{0,8},{8,16},{16,24},{24,0},{1,9},{9,17},{17,25},{25,1},{2,10},{10... | collective-permute-start | bytes 368648 | tf_op jit(solution)/shard_map/ppermute | solution.py:409
  55.2 1.5 %collective-permute-start.6 = (bf16[4,120,128]{2,1,0:T(8,128)(2,1)S(1)}, bf16[4,120,128]{2,1,0:T(8,128)(2,1)S(1)}, u32[]{:S(2)}, u32[]{:S(2)}) collective-permute-start(bf16[4,120,128]{2,1,0:T(8,128)(2,1)S(1)} %get-tuple-element.66), channel_id=1, source_target_pairs={{0,16},{8,24},{16,0},{24,8},{1,17},{9,25},{17,1},{25,9},{2,18},{10... | collective-permute-start | bytes 368648 | tf_op jit(solution)/shard_map/ppermute | solution.py:409
  56.7 2.6 %collective-permute-done.5 = bf16[4,120,128]{2,1,0:T(8,128)(2,1)S(1)} collective-permute-done((bf16[4,120,128]{2,1,0:T(8,128)(2,1)S(1)}, bf16[4,120,128]{2,1,0:T(8,128)(2,1)S(1)}, u32[]{:S(2)}, u32[]{:S(2)}) %collective-permute-start.5) | collective-permute-done | bytes 122912 | tf_op jit(solution)/shard_map/ppermute | solution.py:409
  59.3 2.1 %collective-permute-done.7 = bf16[4,120,128]{2,1,0:T(8,128)(2,1)S(1)} collective-permute-done((bf16[4,120,128]{2,1,0:T(8,128)(2,1)S(1)}, bf16[4,120,128]{2,1,0:T(8,128)(2,1)S(1)}, u32[]{:S(2)}, u32[]{:S(2)}) %collective-permute-start.7) | collective-permute-done | bytes 122912 | tf_op jit(solution)/shard_map/ppermute | solution.py:409
  62.4 1.6 %collective-permute-start.8 = (bf16[120,128]{1,0:T(8,128)(2,1)S(1)}, bf16[120,128]{1,0:T(8,128)(2,1)S(1)}, u32[]{:S(2)}, u32[]{:S(2)}) collective-permute-start(bf16[120,128]{1,0:T(8,128)(2,1)S(1)} %get-tuple-element.73), channel_id=1, source_target_pairs={{0,2},{1,3},{2,4},{3,5},{4,6},{5,7},{6,0},{7,1},{8,10},{9,11},{10,... | collective-permute-start | bytes 92168 | tf_op jit(solution)/shard_map/ppermute | solution.py:409
  64.1 2.2 %collective-permute-start.10 = (bf16[120,128]{1,0:T(8,128)(2,1)S(1)}, bf16[120,128]{1,0:T(8,128)(2,1)S(1)}, u32[]{:S(2)}, u32[]{:S(2)}) collective-permute-start(bf16[120,128]{1,0:T(8,128)(2,1)S(1)} %get-tuple-element.74), channel_id=1, source_target_pairs={{0,6},{1,7},{2,0},{3,1},{4,2},{5,3},{6,4},{7,5},{8,14},{9,15},{10,... | collective-permute-start | bytes 92168 | tf_op jit(solution)/shard_map/ppermute | solution.py:409
  68.3 2.8 %collective-permute-done.9 = bf16[120,128]{1,0:T(8,128)(2,1)S(1)} collective-permute-done((bf16[120,128]{1,0:T(8,128)(2,1)S(1)}, bf16[120,128]{1,0:T(8,128)(2,1)S(1)}, u32[]{:S(2)}, u32[]{:S(2)}) %collective-permute-start.9) | collective-permute-done | bytes 30752 | tf_op jit(solution)/shard_map/ppermute | solution.py:409
  71.3 2.4 %collective-permute-start.12 = (bf16[312,128]{1,0:T(8,128)(2,1)S(1)}, bf16[312,128]{1,0:T(8,128)(2,1)S(1)}, u32[]{:S(2)}, u32[]{:S(2)}) collective-permute-start(bf16[312,128]{1,0:T(8,128)(2,1)S(1)} %constant_dynamic-update-slice_fusion), channel_id=1, source_target_pairs={{4,0},{5,1},{6,2},{7,3},{0,4},{1,5},{2,6},{3,7},{12,8},{13,9},{14,... | collective-permute-start | bytes 239624 | tf_op jit(solution)/shard_map/ppermute | solution.py:433
  73.7 1.4 %collective-permute-start.11 = (bf16[312,128]{1,0:T(8,128)(2,1)S(1)}, bf16[312,128]{1,0:T(8,128)(2,1)S(1)}, u32[]{:S(2)}, u32[]{:S(2)}) collective-permute-start(bf16[312,128]{1,0:T(8,128)(2,1)S(1)} %constant_dynamic-update-slice_fusion), channel_id=1, source_target_pairs={{2,0},{3,1},{4,2},{5,3},{6,4},{7,5},{0,6},{1,7},{10,8},{11,9},{12,... | collective-permute-start | bytes 239624 | tf_op jit(solution)/shard_map/ppermute | solution.py:433
  75.1 2.5 %collective-permute-done.13 = bf16[312,128]{1,0:T(8,128)(2,1)S(1)} collective-permute-done((bf16[312,128]{1,0:T(8,128)(2,1)S(1)}, bf16[312,128]{1,0:T(8,128)(2,1)S(1)}, u32[]{:S(2)}, u32[]{:S(2)}) %collective-permute-start.13) | collective-permute-done | bytes 79904 | tf_op jit(solution)/shard_map/ppermute | solution.py:433
  79.0 1.6 %collective-permute-start.15 = (bf16[4,312,128]{2,1,0:T(8,128)(2,1)S(1)}, bf16[4,312,128]{2,1,0:T(8,128)(2,1)S(1)}, u32[]{:S(2)}, u32[]{:S(2)}) collective-permute-start(bf16[4,312,128]{2,1,0:T(8,128)(2,1)S(1)} %get-tuple-element.68), channel_id=1, source_target_pairs={{16,0},{24,8},{0,16},{8,24},{17,1},{25,9},{1,17},{9,25},{18,2},{26... | collective-permute-start | bytes 958472 | tf_op jit(solution)/shard_map/ppermute | solution.py:433
  80.5 2.9 %collective-permute-start.14 = (bf16[4,312,128]{2,1,0:T(8,128)(2,1)S(1)}, bf16[4,312,128]{2,1,0:T(8,128)(2,1)S(1)}, u32[]{:S(2)}, u32[]{:S(2)}) collective-permute-start(bf16[4,312,128]{2,1,0:T(8,128)(2,1)S(1)} %get-tuple-element.68), channel_id=1, source_target_pairs={{8,0},{16,8},{24,16},{0,24},{9,1},{17,9},{25,17},{1,25},{10,2},{18... | collective-permute-start | bytes 958472 | tf_op jit(solution)/shard_map/ppermute | solution.py:433
  83.4 5.9 %collective-permute-done.15 = bf16[4,312,128]{2,1,0:T(8,128)(2,1)S(1)} collective-permute-done((bf16[4,312,128]{2,1,0:T(8,128)(2,1)S(1)}, bf16[4,312,128]{2,1,0:T(8,128)(2,1)S(1)}, u32[]{:S(2)}, u32[]{:S(2)}) %collective-permute-start.15) | collective-permute-done | bytes 319520 | tf_op jit(solution)/shard_map/ppermute | solution.py:433
  90.0 4.1 %collective-permute-done.16 = bf16[4,312,128]{2,1,0:T(8,128)(2,1)S(1)} collective-permute-done((bf16[4,312,128]{2,1,0:T(8,128)(2,1)S(1)}, bf16[4,312,128]{2,1,0:T(8,128)(2,1)S(1)}, u32[]{:S(2)}, u32[]{:S(2)}) %collective-permute-start.16) | collective-permute-done | bytes 319520 | tf_op jit(solution)/shard_map/ppermute | solution.py:433
  96.3 10.0 %shard_map.284 = (bf16[48,8,256]{2,1,0:T(8,128)(2,1)}, bf16[96,4,128]{2,1,0:T(4,128)(2,1)}, bf16[2,64,192]{2,1,0:T(8,128)(2,1)}, bf16[1,32,384]{2,1,0:T(8,128)(2...) custom-call(bf16[8,256,48]{2,1,0:T(8,128)(2,1)S(1)} %get-tuple-eleme, ...), custom_call_target="tpu_custom_call" | custom-call | flops 100000000 | bytes 1000000 | tf_op jit(solution)/shard_map/pallas_call | solution.py:26
  106.4 11.6 %shard_map.286 = (bf16[3,3,48,48]{3,2,1,0:T(8,128)(2,1)}, bf16[3,3,96,96]{3,2,1,0:T(8,128)(2,1)}, bf16[3,3,192,192]{3,2,1,0:T(8,128)(2,1)}, bf16[3,3,384,384]{3,2,1,0:T(8,128)(2,1)}) custom-call(s32[3]{0:T(128)} %pad_add_fusion.refs_0_, bf16[4,4,312,128]{3,2,1,0:T(8,128)(2,1)} %copy-done.52, bf16[4,4,312,128]{3,2,1,0:T(8,128)(2,1)} %collective-permute-done.17.refs_2_), custom_call_target="tpu_custom_call" | custom-call | flops 3000000000 | bytes 10000000 | tf_op jit(solution)/shard_map/pallas_call | solution.py:451
  (143 shorter events, 35.6 us)
Async XLA Ops:
  20.0 12.7 %copy-start.42 = (f32[1,32,384]{2,1,0:T(8,128)}, f32[1,32,384]{2,1,0:T(8,128)S(1)}, u32[]{:S(2)}) copy-start(f32[1,32,384]{2,1,0:T(8,128)S(1)} %get-tuple-element.47.refs_11_) | copy-start | bytes 147460
  20.0 3.7 %collective-permute-start = (bf16[2,144,384]{2,1,0:T(8,128)(2,1)S(1)}, bf16[2,144,384]{2,1,0:T(8,128)(2,1)S(1)}, u32[]{:S(2)}, u32[]{:S(2)}) collective-permute-start(bf16[2,144,384]{2,1,0:T(8,128)(2,1)S(1)} %get-tuple-element.48), channel_id=1, source_target_pairs={{0,1},{1,2},{2,3},{3,4},{4,5},{5,6},{6,7},{8,9},{9,10},{10,11},{11... | collective-permute-start | bytes 663560 | tf_op jit(solution)/shard_map/ppermute | solution.py:383
  22.4 5.6 %collective-permute-start.1 = (bf16[2,144,384]{2,1,0:T(8,128)(2,1)S(1)}, bf16[2,144,384]{2,1,0:T(8,128)(2,1)S(1)}, u32[]{:S(2)}, u32[]{:S(2)}) collective-permute-start(bf16[2,144,384]{2,1,0:T(8,128)(2,1)S(1)} %get-tuple-element.49), channel_id=1, source_target_pairs={{1,0},{2,1},{3,2},{4,3},{5,4},{6,5},{7,6},{9,8},{10,9},{11,10},{12... | collective-permute-start | bytes 663560 | tf_op jit(solution)/shard_map/ppermute | solution.py:384
  27.9 5.1 %collective-permute-start.2 = (bf16[2,32,384]{2,1,0:T(8,128)(2,1)S(1)}, bf16[2,32,384]{2,1,0:T(8,128)(2,1)S(1)}, u32[]{:S(2)}, u32[]{:S(2)}) collective-permute-start(bf16[2,32,384]{2,1,0:T(8,128)(2,1)S(1)} %pad_maximum_fusion.2), channel_id=1, source_target_pairs={{0,8},{8,16},{16,24},{1,9},{9,17},{17,25},{2,10},{10,18},{18,26},{... | collective-permute-start | bytes 147464 | tf_op jit(solution)/shard_map/ppermute | solution.py:389
  31.4 6.0 %collective-permute-start.3 = (bf16[2,32,384]{2,1,0:T(8,128)(2,1)S(1)}, bf16[2,32,384]{2,1,0:T(8,128)(2,1)S(1)}, u32[]{:S(2)}, u32[]{:S(2)}) collective-permute-start(bf16[2,32,384]{2,1,0:T(8,128)(2,1)S(1)} %pad_maximum_fusion.3), channel_id=1, source_target_pairs={{8,0},{16,8},{24,16},{9,1},{17,9},{25,17},{10,2},{18,10},{26,18},{... | collective-permute-start | bytes 147464 | tf_op jit(solution)/shard_map/ppermute | solution.py:390
  45.4 4.8 %collective-permute-start.4 = (bf16[4,4,120,128]{3,2,1,0:T(8,128)(2,1)}, bf16[4,4,120,128]{3,2,1,0:T(8,128)(2,1)}, u32[]{:S(2)}, u32[]{:S(2)}) collective-permute-start(bf16[4,4,120,128]{3,2,1,0:T(8,128)(2,1)} %dynamic-slice_bitcast_fusion), channel_id=1, source_target_pairs={{0,1},{1,0},{2,3},{3,2},{4,5},{5,4},{6,7},{7,6},{8,9},{9,8},{10,11... | collective-permute-start | bytes 1474568 | tf_op jit(solution)/shard_map/ppermute | solution.py:409
  48.3 18.7 %copy-start.25 = (bf16[384,1,32]{0,2,1:T(8,128)(2,1)S(1)}, bf16[384,1,32]{0,2,1:T(8,128)(2,1)}, u32[]{:S(2)}) copy-start(bf16[384,1,32]{0,2,1:T(8,128)(2,1)} %param.23) | copy-start | bytes 73732
  52.1 19.0 %copy-start.38 = (bf16[1,32,384]{2,1,0:T(8,128)(2,1)S(1)}, bf16[1,32,384]{2,1,0:T(8,128)(2,1)}, u32[]{:S(2)}) copy-start(bf16[1,32,384]{2,1,0:T(8,128)(2,1)} %copy-done.37) | copy-start | bytes 73732
  52.2 7.1 %collective-permute-start.5 = (bf16[4,120,128]{2,1,0:T(8,128)(2,1)S(1)}, bf16[4,120,128]{2,1,0:T(8,128)(2,1)S(1)}, u32[]{:S(2)}, u32[]{:S(2)}) collective-permute-start(bf16[4,120,128]{2,1,0:T(8,128)(2,1)S(1)} %get-tuple-element.64), channel_id=1, source_target_pairs={{0,8},{8,16},{16,24},{24,0},{1,9},{9,17},{17,25},{25,1},{2,10},{10... | collective-permute-start | bytes 368648 | tf_op jit(solution)/shard_map/ppermute | solution.py:409
  54.6 6.8 %collective-permute-start.7 = (bf16[4,120,128]{2,1,0:T(8,128)(2,1)S(1)}, bf16[4,120,128]{2,1,0:T(8,128)(2,1)S(1)}, u32[]{:S(2)}, u32[]{:S(2)}) collective-permute-start(bf16[4,120,128]{2,1,0:T(8,128)(2,1)S(1)} %get-tuple-element.65), channel_id=1, source_target_pairs={{0,24},{8,0},{16,8},{24,16},{1,25},{9,1},{17,9},{25,17},{2,26},{10... | collective-permute-start | bytes 368648 | tf_op jit(solution)/shard_map/ppermute | solution.py:409
  55.2 6.3 %collective-permute-start.6 = (bf16[4,120,128]{2,1,0:T(8,128)(2,1)S(1)}, bf16[4,120,128]{2,1,0:T(8,128)(2,1)S(1)}, u32[]{:S(2)}, u32[]{:S(2)}) collective-permute-start(bf16[4,120,128]{2,1,0:T(8,128)(2,1)S(1)} %get-tuple-element.66), channel_id=1, source_target_pairs={{0,16},{8,24},{16,0},{24,8},{1,17},{9,25},{17,1},{25,9},{2,18},{10... | collective-permute-start | bytes 368648 | tf_op jit(solution)/shard_map/ppermute | solution.py:409
  62.4 5.9 %collective-permute-start.8 = (bf16[120,128]{1,0:T(8,128)(2,1)S(1)}, bf16[120,128]{1,0:T(8,128)(2,1)S(1)}, u32[]{:S(2)}, u32[]{:S(2)}) collective-permute-start(bf16[120,128]{1,0:T(8,128)(2,1)S(1)} %get-tuple-element.73), channel_id=1, source_target_pairs={{0,2},{1,3},{2,4},{3,5},{4,6},{5,7},{6,0},{7,1},{8,10},{9,11},{10,... | collective-permute-start | bytes 92168 | tf_op jit(solution)/shard_map/ppermute | solution.py:409
  64.1 4.2 %collective-permute-start.10 = (bf16[120,128]{1,0:T(8,128)(2,1)S(1)}, bf16[120,128]{1,0:T(8,128)(2,1)S(1)}, u32[]{:S(2)}, u32[]{:S(2)}) collective-permute-start(bf16[120,128]{1,0:T(8,128)(2,1)S(1)} %get-tuple-element.74), channel_id=1, source_target_pairs={{0,6},{1,7},{2,0},{3,1},{4,2},{5,3},{6,4},{7,5},{8,14},{9,15},{10,... | collective-permute-start | bytes 92168 | tf_op jit(solution)/shard_map/ppermute | solution.py:409
  66.3 4.8 %collective-permute-start.9 = (bf16[120,128]{1,0:T(8,128)(2,1)S(1)}, bf16[120,128]{1,0:T(8,128)(2,1)S(1)}, u32[]{:S(2)}, u32[]{:S(2)}) collective-permute-start(bf16[120,128]{1,0:T(8,128)(2,1)S(1)} %get-tuple-element.75), channel_id=1, source_target_pairs={{0,4},{1,5},{2,6},{3,7},{4,0},{5,1},{6,2},{7,3},{8,12},{9,13},{10,... | collective-permute-start | bytes 92168 | tf_op jit(solution)/shard_map/ppermute | solution.py:409
  71.2 6.4 %collective-permute-start.13 = (bf16[312,128]{1,0:T(8,128)(2,1)S(1)}, bf16[312,128]{1,0:T(8,128)(2,1)S(1)}, u32[]{:S(2)}, u32[]{:S(2)}) collective-permute-start(bf16[312,128]{1,0:T(8,128)(2,1)S(1)} %constant_dynamic-update-slice_fusion), channel_id=1, source_target_pairs={{6,0},{7,1},{0,2},{1,3},{2,4},{3,5},{4,6},{5,7},{14,8},{15,9},{8,1... | collective-permute-start | bytes 239624 | tf_op jit(solution)/shard_map/ppermute | solution.py:433
  71.3 7.6 %collective-permute-start.12 = (bf16[312,128]{1,0:T(8,128)(2,1)S(1)}, bf16[312,128]{1,0:T(8,128)(2,1)S(1)}, u32[]{:S(2)}, u32[]{:S(2)}) collective-permute-start(bf16[312,128]{1,0:T(8,128)(2,1)S(1)} %constant_dynamic-update-slice_fusion), channel_id=1, source_target_pairs={{4,0},{5,1},{6,2},{7,3},{0,4},{1,5},{2,6},{3,7},{12,8},{13,9},{14,... | collective-permute-start | bytes 239624 | tf_op jit(solution)/shard_map/ppermute | solution.py:433
  73.7 5.2 %collective-permute-start.11 = (bf16[312,128]{1,0:T(8,128)(2,1)S(1)}, bf16[312,128]{1,0:T(8,128)(2,1)S(1)}, u32[]{:S(2)}, u32[]{:S(2)}) collective-permute-start(bf16[312,128]{1,0:T(8,128)(2,1)S(1)} %constant_dynamic-update-slice_fusion), channel_id=1, source_target_pairs={{2,0},{3,1},{4,2},{5,3},{6,4},{7,5},{0,6},{1,7},{10,8},{11,9},{12,... | collective-permute-start | bytes 239624 | tf_op jit(solution)/shard_map/ppermute | solution.py:433
  78.9 16.3 %copy-start.35 = (f32[2,64,192]{2,1,0:T(8,128)S(1)}, f32[2,64,192]{2,1,0:T(8,128)}, u32[]{:S(2)}) copy-start(f32[2,64,192]{2,1,0:T(8,128)} %copy-done.34) | copy-start | bytes 294916
  78.9 16.3 %copy-start.36 = (bf16[3,3,48,48]{3,2,1,0:T(8,128)(2,1)S(1)}, bf16[3,3,48,48]{3,2,1,0:T(8,128)(2,1)}, u32[]{:S(2)}) copy-start(bf16[3,3,48,48]{3,2,1,0:T(8,128)(2,1)} %refs_20_.1) | copy-start | bytes 124420
  78.9 16.3 %copy-start.43 = (f32[1,32,384]{2,1,0:T(8,128)S(1)}, f32[1,32,384]{2,1,0:T(8,128)}, u32[]{:S(2)}) copy-start(f32[1,32,384]{2,1,0:T(8,128)} %copy-done.42) | copy-start | bytes 147460
  79.0 10.4 %collective-permute-start.15 = (bf16[4,312,128]{2,1,0:T(8,128)(2,1)S(1)}, bf16[4,312,128]{2,1,0:T(8,128)(2,1)S(1)}, u32[]{:S(2)}, u32[]{:S(2)}) collective-permute-start(bf16[4,312,128]{2,1,0:T(8,128)(2,1)S(1)} %get-tuple-element.68), channel_id=1, source_target_pairs={{16,0},{24,8},{0,16},{8,24},{17,1},{25,9},{1,17},{9,25},{18,2},{26... | collective-permute-start | bytes 958472 | tf_op jit(solution)/shard_map/ppermute | solution.py:433
  80.5 9.5 %collective-permute-start.14 = (bf16[4,312,128]{2,1,0:T(8,128)(2,1)S(1)}, bf16[4,312,128]{2,1,0:T(8,128)(2,1)S(1)}, u32[]{:S(2)}, u32[]{:S(2)}) collective-permute-start(bf16[4,312,128]{2,1,0:T(8,128)(2,1)S(1)} %get-tuple-element.68), channel_id=1, source_target_pairs={{8,0},{16,8},{24,16},{0,24},{9,1},{17,9},{25,17},{1,25},{10,2},{18... | collective-permute-start | bytes 958472 | tf_op jit(solution)/shard_map/ppermute | solution.py:433
  83.4 10.7 %collective-permute-start.16 = (bf16[4,312,128]{2,1,0:T(8,128)(2,1)S(1)}, bf16[4,312,128]{2,1,0:T(8,128)(2,1)S(1)}, u32[]{:S(2)}, u32[]{:S(2)}) collective-permute-start(bf16[4,312,128]{2,1,0:T(8,128)(2,1)S(1)} %get-tuple-element.68), channel_id=1, source_target_pairs={{24,0},{0,8},{8,16},{16,24},{25,1},{1,9},{9,17},{17,25},{26,2},{2,... | collective-permute-start | bytes 958472 | tf_op jit(solution)/shard_map/ppermute | solution.py:433
  94.5 11.9 %collective-permute-start.17 = (bf16[4,4,312,128]{3,2,1,0:T(8,128)(2,1)S(1)}, bf16[4,4,312,128]{3,2,1,0:T(8,128)(2,1)}, u32[]{:S(2)}, u32[]{:S(2)}) collective-permute-start(bf16[4,4,312,128]{3,2,1,0:T(8,128)(2,1)S(1)} %pad_maximum_fusion.refs_1_), channel_id=1, source_target_pairs={{0,1},{1,0},{2,3},{3,2},{4,5},{5,4},{6,7},{7,6},{8,9},{9,8},{10,11... | collective-permute-start | bytes 3833864 | tf_op jit(solution)/shard_map/ppermute | solution.py:437
  (47 other events, 86.9 us)

commit v2 on v1

v2 whole, which is shorter than its diff:
```python
import functools
import math

import jax
import jax.numpy as jnp
from jax import lax
from jax.experimental import pallas as pl
from jax.experimental.pallas import tpu as pltpu
from jax.sharding import PartitionSpec as P

BF = jnp.bfloat16
F32 = jnp.float32
LEFT = 8
PACK = 384
WHOLE = 61
COARSE = 46


def dot(a, b, ca=1, cb=0):
    return lax.dot_general(a, b, (((ca,), (cb,)), ((), ())), preferred_element_type=F32)


def source_offset(channels, target, source):
    return sum(channels[k] for k in range(source) if k != target)


class Fetched:
    def __init__(self, ref, copy):
        self.ref, self.copy, self.shape = ref, copy, ref.shape
        copy.start()

    def wait(self):
        if self.copy is not None:
            self.copy.wait()
            self.copy = None

    def __getitem__(self, at):
        self.wait()
        return self.ref[at]


class Sent:
    def __init__(self, ref, copy):
        self.ref, self.copy, self.shape, self.started = ref, copy, ref.shape, False

    def __setitem__(self, at, value):
        self.ref[at] = value

    def __getitem__(self, at):
        return self.ref[at]

    def flush(self):
        if not self.started:
            self.copy.start()
            self.started = True

    def wait(self):
        self.flush()
        self.copy.wait()


def flush(*refs):
    for ref in refs:
        if isinstance(ref, Sent):
            ref.flush()


def call(body, outs, args, scratch=(), far=(), far_out=(), placed=False, deps=(), raw_out=(), flops=2 * 10**9, limit=24):
    far, far_out = list(far), list(far_out)
    n_in, n_out, n_far = len(args), len(outs), len(far)
    n_moved = n_far + len(far_out)

    def wrapped(*refs):
        row = lax.axis_index("rows")
        place = (row % 2, lax.axis_index("branch"), row // 2)
        ins, rest = list(refs[:n_in]), refs[n_in + len(deps) :]
        results, held, sems = list(rest[:n_out]), rest[n_out : n_out + n_moved], rest[-1]
        copy = lambda a, b, k: pltpu.make_async_copy(a, b, sems.at[k])
        for at, k in enumerate(far):
            ins[k] = Fetched(held[at], copy(ins[k], held[at], at))
        for at, k in enumerate(far_out, n_far):
            results[k] = Sent(held[at], copy(held[at], results[k], at))
        body(*([place] if placed else []), *ins, *results, *rest[n_out + n_moved : -1])
        for k in far_out:
            results[k].flush()
        for ref in [ins[k] for k in far] + [results[k] for k in far_out]:
            ref.wait()

    def space(k, kept):
        return pl.BlockSpec(memory_space=pl.ANY if k in kept else pltpu.VMEM)

    moved = [args[k] for k in far] + [outs[k] for k in far_out]
    return pl.pallas_call(
        wrapped,
        out_shape=outs,
        in_specs=[space(k, far) for k in range(n_in)]
        + [pl.BlockSpec(memory_space=pl.ANY) for _ in deps],
        out_specs=[space(k, far_out + list(raw_out)) for k in range(n_out)],
        scratch_shapes=[pltpu.VMEM(a.shape, a.dtype) for a in moved]
        + list(scratch)
        + [pltpu.SemaphoreType.DMA((max(n_moved, 1),))],
        compiler_params=pltpu.CompilerParams(vmem_limit_bytes=limit * 1024 * 1024),
        cost_estimate=pl.CostEstimate(flops=flops, bytes_accessed=10**6, transcendentals=0),
    )(*args, *deps)


def sds(shape, dtype):
    return jax.ShapeDtypeStruct(shape, dtype)


def group_matrix(groups, cells, factor, transposed=False):
    shape = (cells, groups) if transposed else (groups, cells)
    g = lax.broadcasted_iota(jnp.int32, shape, 1 if transposed else 0)
    c = lax.broadcasted_iota(jnp.int32, shape, 0 if transposed else 1)
    return jnp.where((c >= g * factor) & (c < g * factor + factor), 1.0, 0.0).astype(BF)


def row_pack(row, channels):
    blocks = PACK // channels
    part = row.shape[0] // blocks
    return jnp.concatenate([row[k * part : (k + 1) * part] for k in range(blocks)], axis=1)


def row_unpack(packed, channels):
    blocks = PACK // channels
    return jnp.concatenate(
        [packed[:, k * channels : (k + 1) * channels] for k in range(blocks)], axis=0
    )


def col_rows(heights):
    starts, at = [], 0
    for h in heights:
        starts.append(at)
        at += h
    return starts


def channels_last(ref, height, channels):
    eye = group_matrix(channels, channels, 1)
    rows = jnp.swapaxes(ref[...].astype(F32), 0, 1).astype(BF)
    return [dot(rows[r], eye, 0, 0).astype(BF) for r in range(height)]


def pack_edges(n, b, dims, rows, top, bot, left, right):
    heights, widths, channels = dims
    h, w, c = heights[b], widths[b], channels[b]
    start = col_rows(heights)[b]
    for out, row in ((top, rows[0]), (bot, rows[h - 1])):
        out[n, b * 32 : (b + 1) * 32, :] = row_pack(row, c).astype(BF)
        out[n, 128 + b : 129 + b, :c] = row[0:1].astype(BF)
        out[n, 136 + b : 137 + b, :c] = row[w - 1 : w].astype(BF)
    left[n, start : start + h, :c] = stack([row[0:1] for row in rows]).astype(BF)
    right[n, start : start + h, :c] = stack([row[w - 1 : w] for row in rows]).astype(BF)


def gain_row(ref):
    g = ref[...]
    return jnp.concatenate([g[k : k + 1] for k in range(g.shape[0])], axis=1)


def stack(rows):
    return rows[0] if len(rows) == 1 else jnp.concatenate(rows, axis=0)


def upstream_kernel(dims, idx, *refs):
    heights, widths, channels = dims
    d_refs, f_refs, g_refs, x_refs = refs[0:4], refs[4:8], refs[8:12], refs[12:16]
    xt, up_refs, sc_refs = refs[16:20], refs[20:24], refs[24:28]
    inner, outer, left, right, coarse, ends = refs[28:34]
    edges = [ends.at[0], ends.at[1], left, right]
    left[...] = jnp.zeros(left.shape, F32).astype(BF)
    right[...] = jnp.zeros(right.shape, F32).astype(BF)
    ends[:, :, 128:, :] = jnp.zeros((2, 2, 16, PACK), F32).astype(BF)
    dt = []
    for b in range(4):
        if b < 2:
            dt.append(channels_last(d_refs[b], heights[b], channels[b]))
        else:
            dt.append([d_refs[b][r] for r in range(heights[b])])
    mixers = [f_refs[j][...] for j in range(4)]

    def block(j, i):
        off = source_offset(channels, j, i)
        if j == 3:
            return mixers[3][off : off + channels[i]]
        return mixers[j][:, off : off + channels[i]]

    acc = [[dt[i][r].astype(F32) for r in range(heights[i])] for i in range(4)]
    for j in range(4):
        for i in range(j + 1, 4):
            f = 2 ** (i - j)
            pool = group_matrix(widths[i], widths[j], f)
            mat = block(j, i)
            for r in range(heights[i]):
                s = dot(pool, dt[j][r * f])
                for k in range(1, f):
                    s = s + dot(pool, dt[j][r * f + k])
                acc[i][r] = acc[i][r] + dot(s.astype(BF), mat)
        for i in range(j):
            f = 2 ** (j - i)
            spread = group_matrix(widths[j], widths[i], f, True)
            mat = block(j, i)
            for r in range(heights[j]):
                z = dot(spread, dt[j][r]).astype(BF)
                v = dot(z, mat, 1, 1) if j == 3 else dot(z, mat)
                v = v * (1.0 / (f * f))
                for k in range(f):
                    acc[i][r * f + k] = acc[i][r * f + k] + v
    for b in range(4):
        gain = gain_row(g_refs[b])
        scaled = []
        for r in range(heights[b]):
            Packed(up_refs[b], channels[b])[r] = acc[b][r]
            s = (gain * acc[b][r]).astype(BF)
            Packed(sc_refs[b], channels[b])[r] = s
            scaled.append(s.astype(F32))
        flush(up_refs[b], sc_refs[b])
        pack_edges(1, b, dims, scaled, *edges)
        if b < 2:
            rows = channels_last(x_refs[b], heights[b], channels[b])
        else:
            rows = [x_refs[b][r] for r in range(heights[b])]
        for r in range(heights[b]):
            Packed(xt[b], channels[b])[r] = rows[r]
        flush(xt[b])
        pack_edges(0, b, dims, [jnp.maximum(v.astype(F32), 0.0) for v in rows], *edges)
    inner[...] = ends[1 - idx[0]]
    outer[...] = ends[idx[0]]
    w3 = widths[3]
    for r in range(heights[3]):
        coarse[0, r * w3 : (r + 1) * w3] = jnp.maximum(x_refs[3][r].astype(F32), 0.0).astype(BF)
        coarse[1, r * w3 : (r + 1) * w3] = sc_refs[3][r]


class Packed:
    def __init__(self, ref, channels):
        self.ref, self.c, self.two = ref, channels, channels <= 64

    def __getitem__(self, r):
        row = self.ref[r]
        if self.two:
            row = jnp.concatenate([row[:, : self.c], row[:, 64 : 64 + self.c]], axis=0)
        return row

    def __setitem__(self, r, row):
        row = row.astype(F32)
        if self.two:
            half = row.shape[0] // 2
            gap = jnp.zeros((half, 64 - self.c), F32)
            row = jnp.concatenate([row[:half], gap, row[half:], gap], axis=1)
        self.ref[r] = row.astype(BF)


def packed(dims, refs):
    return [Packed(ref, c) for ref, c in zip(refs, dims[2])]


def pick(odd, first, second):
    return jnp.where(odd == 0, first.astype(F32), second.astype(F32))


def fill(scr, n, b, dims, interior, idx, in_row, out_row, in_col, out_col):
    heights, widths, channels = dims
    h, w, c = heights[b], widths[b], channels[b]
    start = col_rows(heights)[b]
    for r in range(h):
        scr[r + 1, LEFT : LEFT + w, :] = interior(r)
    lines = slice(b * 32, (b + 1) * 32)
    core, band = idx[0], idx[1] % 2
    for first, second, at in ((out_row, in_row, 0), (in_row, out_row, h + 1)):
        packed = pick(core, first[n, lines, :], second[n, lines, :])
        scr[at, LEFT : LEFT + w, :] = row_unpack(packed, c)
    for first, second, at in ((out_col, in_col, LEFT - 1), (in_col, out_col, LEFT + w)):
        vals = pick(band, first[n], second[n])
        for r in range(h):
            scr[r + 1, at : at + 1, :] = vals[start + r : start + r + 1, :c]
        scr[0, at : at + 1, :] = vals[16 + b : 17 + b, :c]
        scr[h + 1, at : at + 1, :] = vals[24 + b : 25 + b, :c]


def shifted(scr, h, w, q):
    return [scr[r, LEFT - 1 + q : LEFT - 1 + q + w, :].astype(BF) for r in range(h + 2)]


def side_by_side(scr, h, w, order):
    gap = jnp.zeros((w, 64 - scr.shape[2]), F32)
    rows = []
    for r in range(h + 2):
        parts = []
        for q in order:
            parts += [scr[r, LEFT - 1 + q : LEFT - 1 + q + w, :], gap]
        rows.append(jnp.concatenate(parts, axis=1).astype(BF))
    return rows


def apart(blocks, axis):
    parts = []
    for block in blocks:
        shape = list(block.shape)
        shape[axis] = 64 - shape[axis]
        parts += [block.astype(F32), jnp.zeros(shape, F32)]
    return jnp.concatenate(parts, axis=axis).astype(BF)


def forward_taps(scr, kernel, h, w):
    if scr.shape[2] <= 64:
        rows = side_by_side(scr, h, w, range(3))
        return sum(
            dot(stack(rows[p : p + h]), apart([kernel[p, q] for q in range(3)], 1), 1, 1)
            for p in range(3)
        )
    total = 0
    for q in range(3):
        rows = shifted(scr, h, w, q)
        total = total + sum(dot(stack(rows[p : p + h]), kernel[p, q], 1, 1) for p in range(3))
    return total


def adjoint_taps(scr, kernel, h, w):
    if scr.shape[2] <= 64:
        rows = side_by_side(scr, h, w, (2, 1, 0))
        return sum(
            dot(stack(rows[2 - p : 2 - p + h]), apart([kernel[p, q] for q in range(3)], 0))
            for p in range(3)
        )
    total = 0
    for q in range(3):
        rows = shifted(scr, h, w, 2 - q)
        total = total + sum(dot(stack(rows[2 - p : 2 - p + h]), kernel[p, q]) for p in range(3))
    return total


def weight_grads_kernel(dims, *refs):
    heights, widths, channels = dims
    idx, x_refs, sc_refs = refs[0], packed(dims, refs[1:4]), packed(dims, refs[4:7])
    edges = refs[7:11]
    keep, send, out, *scrs = refs[11:]
    c0, c1, c2 = channels[0], channels[1], channels[2]
    for b in (2, 1, 0):
        h, w, c = heights[b], widths[b], channels[b]
        fill(scrs[b], 0, b, dims, lambda r: jnp.maximum(x_refs[b][r].astype(F32), 0.0), idx, *edges)
        s_all = stack([sc_refs[b][r] for r in range(h)])
        if c <= 64:
            rows = side_by_side(scrs[b], h, w, range(3))
            wide = [dot(s_all, stack(rows[p : p + h]), 0, 0) for p in range(3)]
        for q in range(3):
            if c > 64:
                rows = shifted(scrs[b], h, w, q)
            for p in range(3):
                if c > 64:
                    g = dot(s_all, stack(rows[p : p + h]), 0, 0)
                else:
                    g = wide[p][:, 64 * q : 64 * q + c]
                tap = p * 3 + q
                if b == 2:
                    out[tap * c2 : (tap + 1) * c2, :] = g[:, :128].astype(BF)
                    half = c2 // 2
                    at = 9 * c2 + tap * half
                    both = jnp.concatenate([g[:half, 128:], g[half:, 128:]], axis=1)
                    out[at : at + half, :] = both.astype(BF)
                elif b == 1:
                    at = 9 * c2 * 3 // 2 + tap * c1
                    out[at : at + c1, :c1] = g.astype(BF)
                else:
                    at = 9 * c2 * 3 // 2 + 9 * c1 + (tap // 2) * c0
                    lane = 64 * (tap % 2)
                    out[at : at + c0, lane : lane + c0] = g.astype(BF)
    half = keep.shape[0]
    keep[...] = out[pl.ds(pl.multiple_of(idx[0] * half, 16), half), :]
    send[...] = out[pl.ds(pl.multiple_of((1 - idx[0]) * half, 16), half), :]


def pair_sum_kernel(n_branch, idx, keep, got, coarse, *outs):
    size = outs[0].shape[0]
    for k in range(n_branch):
        at = pl.ds(pl.multiple_of((idx[1] + k) % n_branch * size, 16), size)
        outs[k][...] = (keep[at, :].astype(F32) + got[at, :].astype(F32)).astype(BF)
    outs[-1][...] = coarse[...]


def stack_kernel(count, *refs):
    for k in range(count):
        refs[-1][k] = refs[k][...]


def corner_kernel(idx, left, right, in_row, out_row, inner, outer):
    core, band = idx[0], idx[1] % 2
    cols = []
    for side, at in ((left, 128), (right, 136)):
        in_part, out_part = in_row[:, at : at + 8, :], out_row[:, at : at + 8, :]
        above, below = pick(core, out_part, in_part), pick(core, in_part, out_part)
        cols.append(jnp.concatenate([side[...].astype(F32), above, below], axis=1))
    inner[...] = pick(band, cols[1], cols[0]).astype(BF)
    outer[...] = pick(band, cols[0], cols[1]).astype(BF)


def sum_kernel(count, *refs):
    total = refs[0][...].astype(F32)
    for k in range(1, count):
        total = total + refs[k][...].astype(F32)
    refs[-1][...] = total.astype(BF)


def ordered_sum_kernel(n, idx, *refs):
    held = refs[-1]
    for k in range(n):
        held[(idx[2] + k) % n] = refs[k][...]
    total = held[0].astype(F32)
    for k in range(1, n):
        total = total + held[k].astype(F32)
    refs[n][...] = total.astype(BF)


def forward_kernel(dims, idx, *refs):
    heights, widths, channels = dims
    x_refs = packed(dims, refs[0:4])
    g_refs, f_refs, k_refs = refs[4:8], refs[8:12], refs[12:16]
    edges = refs[16:20]
    refs = refs[20:]
    merged_refs, scrs, wide = refs[0:4], refs[4:8], refs[8:12]
    units = []
    for b in range(4):
        h, w, c = heights[b], widths[b], channels[b]
        fill(scrs[b], 0, b, dims, lambda r: jnp.maximum(x_refs[b][r].astype(F32), 0.0), idx, *edges)
        resp = forward_taps(scrs[b], k_refs[b], h, w)
        gain = gain_row(g_refs[b])
        units.append(
            [
                (x_refs[b][r].astype(F32) + gain * resp[r * w : (r + 1) * w]).astype(BF)
                for r in range(h)
            ]
        )
    mixers = [f_refs[j][...] for j in range(4)]

    def mix(v, j, i):
        off = source_offset(channels, j, i)
        if j == 3:
            return dot(v, mixers[3][off : off + channels[i]])
        return dot(v, mixers[j][:, off : off + channels[i]], 1, 1)

    sums = [[u.astype(F32) for u in units[j]] for j in range(4)]
    for i in range(4):
        for j in range(i + 1, 4):
            f = 2 ** (j - i)
            pool = group_matrix(widths[j], widths[i], f)
            for r in range(heights[j]):
                s = dot(pool, units[i][r * f])
                for k in range(1, f):
                    s = s + dot(pool, units[i][r * f + k])
                s = (s * (1.0 / (f * f))).astype(BF)
                sums[j][r] = sums[j][r] + mix(s, j, i)
        for j in range(i):
            f = 2 ** (i - j)
            spread = group_matrix(widths[i], widths[j], f, True)
            for r in range(heights[i]):
                v = mix(dot(spread, units[i][r]).astype(BF), j, i)
                for k in range(f):
                    sums[j][r * f + k] = sums[j][r * f + k] + v
    for j in range(4):
        emit(j, heights, merged_refs[j], sums[j], wide[j])


def emit(b, heights, out, rows, stage):
    if b >= 2:
        for r in range(heights[b]):
            out[r] = rows[r].astype(BF)
        flush(out)
        return
    for r in range(heights[b]):
        stage[r] = rows[r].T
    out[...] = jnp.swapaxes(stage[...], 0, 1).astype(BF)
    flush(out)


def adjoint_kernel(dims, idx, *refs):
    heights, widths, channels = dims
    x_refs, sc_refs, up_refs = (packed(dims, refs[k : k + 4]) for k in (0, 4, 8))
    k_refs = refs[12:16]
    edges = refs[16:20]
    refs = refs[20:]
    back_refs, scrs, wide = refs[0:4], refs[4:8], refs[8:12]
    for b in range(4):
        h, w, c = heights[b], widths[b], channels[b]
        fill(scrs[b], 1, b, dims, lambda r: sc_refs[b][r].astype(F32), idx, *edges)
        adj = adjoint_taps(scrs[b], k_refs[b], h, w)
        back = [
            up_refs[b][r].astype(F32)
            + jnp.where(x_refs[b][r].astype(F32) > 0, adj[r * w : (r + 1) * w], 0.0)
            for r in range(h)
        ]
        emit(b, heights, back_refs[b], back, wide[b])


def coarse_kernel(dims, n_branch, n_chip, scale, idx, *refs):
    out, act, win, grad, acc, taps, sems = refs[-7:]
    w3, c3 = dims[1][3], dims[2][3]
    rows, cols = 2 * n_chip, n_branch * w3
    act[0] = jnp.zeros(act.shape[1:], F32)
    act[rows + 1] = jnp.zeros(act.shape[1:], F32)
    for r in range(rows):
        act[r + 1, 0:LEFT, :] = jnp.zeros((LEFT, c3), F32)
        act[r + 1, LEFT + cols :, :] = jnp.zeros((8, c3), F32)
    for m in range(2):
        for l in range(n_branch):
            for k in range(n_chip):
                src = refs[m * n_branch + l]
                r = (idx[2] + k) % n_chip * 2 + (idx[0] + m) % 2
                off = pl.multiple_of((idx[1] + l) % n_branch * w3, w3)
                act[r + 1, pl.ds(LEFT + off, w3), :] = src[k, 0].astype(F32)
                win[r, pl.ds(off, w3), :] = src[k, 1]
    for r in range(rows):
        grad[:, r * cols : (r + 1) * cols] = win[r].astype(F32).T.astype(BF)
    span = rows * cols
    step = min(span, 1024)
    copies = []
    for q in range(3):
        for r in range(rows + 2):
            win[r] = act[r, LEFT - 1 + q : LEFT - 1 + q + cols, :].astype(BF)
        for p in range(3):
            if step == span:
                total = dot(grad[...], win[p : p + rows].reshape(span, c3))
            else:
                acc[...] = jnp.zeros(acc.shape, F32)
                lines = step // cols

                @pl.loop(0, rows // lines)
                def _(t, p=p):
                    some = win[pl.ds(t * lines + p, lines)].reshape(step, c3)
                    acc[...] += dot(grad[:, pl.ds(pl.multiple_of(t * step, step), step)], some)

                total = acc[...]
            taps[p, q] = (total * scale).astype(BF)
            copies.append(pltpu.make_async_copy(taps.at[p, q], out.at[p, q], sems.at[p, q]))
            copies[-1].start()
    for copy in copies:
        copy.wait()


def finish_kernel(dims, n_branch, scales, idx, *refs):
    channels = dims[2]
    parts = refs[: 2 * n_branch]
    outs, flat = refs[-4:-1], refs[-1]
    c0, c1, c2 = channels[0], channels[1], channels[2]
    size = parts[0].shape[0]
    for k, part in enumerate(parts):
        core, band = (idx[0] + k // n_branch) % 2, (idx[1] + k) % n_branch
        at = pl.multiple_of((core * n_branch + band) * size, 16)
        flat[pl.ds(at, size), :] = part[...].astype(F32)
    base1 = 9 * c2 * 3 // 2
    base0 = base1 + 9 * c1
    half = c2 // 2
    for tap in range(9):
        p, q = tap // 3, tap % 3
        outs[2][p, q, :, 0:128] = (flat[tap * c2 : (tap + 1) * c2, :] * scales[2]).astype(BF)
        at = 9 * c2 + tap * half
        both = flat[at : at + half, :]
        tail = jnp.concatenate([both[:, :64], both[:, 64:]], axis=0)
        outs[2][p, q, :, 128:c2] = (tail * scales[2]).astype(BF)
        at = base1 + tap * c1
        outs[1][p, q] = (flat[at : at + c1, :c1] * scales[1]).astype(BF)
        at = base0 + (tap // 2) * c0
        lane = 64 * (tap % 2)
        outs[0][p, q] = (flat[at : at + c0, lane : lane + c0] * scales[0]).astype(BF)


def local(*args):
    maps, kernels, gains, mixers, cotans = (args[4 * k : 4 * k + 4] for k in range(5))
    n_rows, n_branch = lax.axis_size("rows"), lax.axis_size("branch")
    n_chip = n_rows // 2
    channels = [a.shape[0] for a in maps]
    heights = [a.shape[1] for a in maps]
    widths = [a.shape[2] for a in maps]
    dims = (heights, widths, channels)
    last = lambda a: jnp.transpose(a, (1, 2, 0))
    unlast = lambda a: jnp.transpose(a, (2, 0, 1))
    xs = [maps[0], maps[1], last(maps[2]), last(maps[3])]
    ds = [cotans[0], cotans[1], last(cotans[2]), last(cotans[3])]
    gs = [g.reshape(-1, 128) if g.shape[0] % 128 == 0 else g.reshape(1, -1) for g in gains]
    fs = [mixers[0], mixers[1], mixers[2], mixers[3].T]
    shapes = [(heights[b], widths[b], channels[b]) for b in range(4)]
    kept = [sds((h, w // 2, 128) if c <= 64 else (h, w, c), BF) for h, w, c in shapes]
    scales = [1.0 / math.sqrt(heights[b] * n_rows * widths[b] * n_branch) for b in range(4)]
    swap = lambda n: [(i, i ^ 1) for i in range(n)]
    hop = lambda n: [(i, i + 1 if i % 2 else i - 1) for i in range(1, n - 1)]
    core_swap = lambda a: lax.ppermute(a, "rows", swap(n_rows))
    from_branch = lambda k: [((i + k) % n_branch, i) for i in range(n_branch)]
    to_branch = lambda k: [(i, (i + k) % n_branch) for i in range(n_branch)]
    from_chip = lambda k: [((i + 2 * k) % n_rows, i) for i in range(n_rows)]

    outs = call(
        functools.partial(upstream_kernel, dims),
        kept * 3 + [sds((2, 144, PACK), BF)] * 2 + [sds((2, 16, PACK), BF)] * 2
        + [sds((2, heights[3] * widths[3], channels[3]), BF)],
        ds + fs + gs + xs,
        [pltpu.VMEM((2, 2, 144, PACK), BF)],
        placed=True, far=range(16), far_out=range(17), limit=WHOLE, flops=6 * 10**9,
    )
    xt, ups, scs = outs[:4], outs[4:8], outs[8:12]
    inner, outer, left, right, coarse = outs[12:]
    out_row = lax.ppermute(outer, "rows", hop(n_rows))
    in_row = core_swap(inner)
    inner, outer = call(
        corner_kernel, [sds((2, 32, PACK), BF)] * 2, [left, right, in_row, out_row],
        placed=True, far=range(4), far_out=range(2), limit=WHOLE,
    )
    out_col = lax.ppermute(outer, "branch", hop(n_branch))
    in_col = lax.ppermute(inner, "branch", swap(n_branch))
    edges = [in_row, out_row, in_col, out_col]

    pad = lambda b: pltpu.VMEM((heights[b] + 2, widths[b] + 16, channels[b]), F32)
    wide = [pltpu.VMEM((heights[b], channels[b], widths[b]), F32) for b in range(4)]
    pieces = 2 * n_branch
    packed_rows = 9 * (channels[2] * 3 // 2 + channels[1]) + 5 * channels[0]
    size = -(-packed_rows // (16 * pieces)) * 16
    part = sds((size, 128), BF)
    keep, send = call(
        functools.partial(weight_grads_kernel, dims),
        [sds((n_branch * size, 128), BF)] * 2,
        list(xt[:3]) + list(scs[:3]) + edges,
        [pltpu.VMEM((pieces * size, 128), BF), pad(0), pad(1), pad(2)],
        placed=True, far=(2, 5, 6, 7, 8, 9, 1, 4, 0, 3), far_out=(0, 1), limit=WHOLE, flops=4 * 10**9,
    )
    *parts, coarse = call(
        functools.partial(pair_sum_kernel, n_branch),
        [part] * n_branch + [sds(coarse.shape, BF)],
        [keep, core_swap(send), coarse],
        placed=True, far=range(3), far_out=range(n_branch + 1), limit=WHOLE,
    )
    got = [lax.ppermute(parts[k], "branch", to_branch(k)) for k in range(1, n_branch)]
    held = [coarse] + [lax.ppermute(coarse, "rows", from_chip(k)) for k in range(1, n_chip)]
    (held,) = call(
        functools.partial(stack_kernel, n_chip), [sds((n_chip,) + coarse.shape, BF)], held,
    )
    (part_sum,) = call(
        functools.partial(sum_kernel, n_branch), [part], [parts[0]] + got, deps=(held,)
    )
    got = [lax.ppermute(part_sum, "rows", from_chip(k)) for k in range(1, n_chip)]
    held = [held] + [lax.ppermute(held, "branch", from_branch(k)) for k in range(1, n_branch)]
    merged = call(
        functools.partial(forward_kernel, dims),
        [sds(maps[0].shape, BF), sds(maps[1].shape, BF), sds(shapes[2], BF), sds(shapes[3], BF)],
        list(xt) + gs + fs + list(kernels) + edges,
        [pad(b) for b in range(4)] + wide,
        placed=True, far_out=range(4), deps=(part_sum,), flops=6 * 10**9,
    )
    back = call(
        functools.partial(adjoint_kernel, dims),
        [sds(maps[0].shape, BF), sds(maps[1].shape, BF), sds(shapes[2], BF), sds(shapes[3], BF)],
        list(xt) + list(scs) + list(ups) + list(kernels) + edges,
        [pad(b) for b in range(4)] + wide,
        placed=True, far_out=range(4), deps=(part_sum,),
    )
    (total,) = call(
        functools.partial(ordered_sum_kernel, n_chip), [part], [part_sum] + got,
        [pltpu.VMEM((n_chip, size, 128), BF)], placed=True, deps=(merged[3], *held[1:]),
    )
    mine = [total] + [lax.ppermute(total, "branch", from_branch(k)) for k in range(1, n_branch)]
    held = held + [core_swap(a) for a in held]
    cols = n_branch * widths[3]
    (kgrad3,) = call(
        functools.partial(coarse_kernel, dims, n_branch, n_chip, scales[3]),
        [sds(kernels[3].shape, BF)],
        held,
        [
            pltpu.VMEM((n_rows + 2, cols + 16, channels[3]), F32),
            pltpu.VMEM((n_rows + 2, cols, channels[3]), BF),
            pltpu.VMEM((channels[3], n_rows * cols), BF),
            pltpu.VMEM((channels[3], channels[3]), F32),
            pltpu.VMEM(kernels[3].shape, BF),
            pltpu.SemaphoreType.DMA((3, 3)),
        ],
        placed=True, raw_out=(0,), deps=(total,), flops=5 * 10**9, limit=COARSE,
    )
    mine = mine + [core_swap(a) for a in mine]
    kgrads = call(
        functools.partial(finish_kernel, dims, n_branch, scales),
        [sds(k.shape, BF) for k in kernels[:3]],
        mine,
        [pltpu.VMEM((pieces * size, 128), F32)], placed=True, far_out=range(3), deps=(kgrad3, back[3]),
    )
    return (
        merged[0], merged[1], unlast(merged[2]), unlast(merged[3]),
        back[0], back[1], unlast(back[2]), unlast(back[3]),
        *kgrads, kgrad3,
    )


def solution(mesh):
    maps = P(None, "rows", "branch")
    in_specs = (maps,) * 4 + (P(),) * 12 + (maps,) * 4
    out_specs = (maps,) * 8 + (P(),) * 4
    return jax.shard_map(
        lambda *args: local(*args),
        mesh=mesh, in_specs=in_specs, out_specs=out_specs, check_vma=False,
    )
```

time: 120 us -> 88.2 us (0.73); the launches traced: 118 us -> 87.8 us
  waiting for transfers between devices: 33.3 us -> 13.8 us
  local copies, waits for them, and re-layouts: 25 us -> 5.58 us
  starting transfers between devices: 28.9 us -> 35.9 us
  Pallas kernels: 26.7 us -> 31.2 us
  other arithmetic: 3.02 us -> 0 us
    ppermute x18 -> x28, waiting for transfers between devices: 33.3 us -> 13.8 us  [the longest x3 4.06 us: local(): lax.ppermute(total, 'branch', from_branch(k))]
    unnamed x111 -> x76, local copies, waits for them, and re-layouts: 23.5 us -> 5.58 us
    ppermute x18 -> x28, starting transfers between devices: 28.9 us -> 35.9 us  [the longest x3 8.67 us: local(): lax.ppermute(parts[k], 'branch', to_branch(k))]
    pallas_call x4 -> x11, Pallas kernels: 26.7 us -> 31.2 us  [call(): pl.pallas_call(wrapped, out_shape=outs, in_specs=[space(k, far) for k in...]
    convert_element_type x2 -> x0, other arithmetic: 2.15 us -> none  [reduce_stage(): return out.astype(BF)]
  transfers between devices with their start and end apart: 18 -> 28, of which waited for: 13 -> 8; matrix products, arithmetic and copies ran while one was open for 1% -> 0% of each run, Pallas kernels for 9% -> 16%
where the time goes in v2:
time: 88.2 us; the launch traced here: 87.8 us
  starting transfers between devices  35.9 us (41%)
  Pallas kernels  31.2 us (35%)
  waiting for transfers between devices  13.8 us (16%)
  local copies, waits for them, and re-layouts  5.58 us (6%)
  between operations  1.43 us (2%)
    pallas_call x11, Pallas kernels, call(): pl.pallas_call(wrapped, out_shape=outs, in_specs=[space(k, far) for k in...  31.2 us
    ppermute x3, starting transfers between devices, local(): lax.ppermute(parts[k], 'branch', to_branch(k))  8.67 us
    ppermute x10, starting transfers between devices, local(): core_swap = lambda a: lax.ppermute(a, 'rows', swap(n_rows))  7.63 us
    ppermute x3, starting transfers between devices, local(): lax.ppermute(coarse, 'rows', from_chip(k))  6.59 us
    unnamed x76, local copies, waits for them, and re-layouts  5.58 us
    ppermute x3, waiting for transfers between devices, local(): lax.ppermute(total, 'branch', from_branch(k))  4.06 us
    ppermute x3, starting transfers between devices, local(): lax.ppermute(total, 'branch', from_branch(k))  3.54 us
    ppermute x3, starting transfers between devices, local(): lax.ppermute(held, 'branch', from_branch(k))  3.46 us
  transfers between devices with their start and end apart: 28, of which 8 were waited for; matrix products, arithmetic and copies ran while one was open for 0% of the time, Pallas kernels for 16%

profile of v2, /device:TPU:0, one launch (start us, length us, event | category | flops | bytes accessed | tf_op | source)
XLA Modules:
  0.0 87.8 jit_solution(17710313603126572151)
XLA Ops:
  0.6 6.9 %shard_map.283 = (bf16[8,128,128]{2,1,0:T(8,128)(2,1)}, bf16[4,128,96]{2,1,0:T(8,128)(2,1)}, bf16[2,64,192]{2,1,0:T(8,128)(2,1)}, bf16[1,32,384]{2,1,0:T(8,128)(...) custom-call(bf16[48,8,256]{2,1,0:T(8,128)(2,1)} %refs_0_.1, ...), custom_call_target="tpu_custom_call" | custom-call | flops 6000000000 | bytes 1000000 | tf_op jit(solution)/shard_map/pallas_call | solution.py:93
  10.2 1.8 %shard_map.284 = (bf16[2,32,384]{2,1,0:T(8,128)(2,1)}, bf16[2,32,384]{2,1,0:T(8,128)(2,1)}) custom-call(bf16[2,16,384]{2,1,0:T(8,128)(2,1)} %get-tuple-element.55.refs_0_, bf16[2,16,384]{2,1,0:T(8,128)(2,1)} %get-tuple-element.56.refs_1_, bf16[2,144,384]{2,1,0:T(8,128)(2,1)} %copy-done.5, bf16[2,144,384]{2,1,0:T(8,128)(2,1)} %copy-done.7), custom_call_target="tpu_custom_call" | custom-call | flops 2000000000 | bytes 1000000 | tf_op jit(solution)/shard_map/pallas_call | solution.py:93
  12.0 2.9 %collective-permute-start.2 = (bf16[2,32,384]{2,1,0:T(8,128)(2,1)}, bf16[2,32,384]{2,1,0:T(8,128)(2,1)S(1)}, u32[]{:S(2)}, u32[]{:S(2)}) collective-permute-start(bf16[2,32,384]{2,1,0:T(8,128)(2,1)} %get-tuple-element.57), channel_id=1, source_target_pairs={{0,8},{8,0},{16,24},{24,16},{1,9},{9,1},{17,25},{25,17},{2,10},{10... | collective-permute-start | bytes 147464 | tf_op jit(solution)/shard_map/ppermute | solution.py:608
  15.5 1.6 %collective-permute-done.2.refs_8_.refs_18_ = bf16[2,32,384]{2,1,0:T(8,128)(2,1)S(1)} collective-permute-done((bf16[2,32,384]{2,1,0:T(8,128)(2,1)}, bf16[2,32,384]{2,1,0:T(8,128)(2,1)S(1)}, u32[]{:S(2)}, u32[]{:S(2)}) %collective-permute-start.2) | collective-permute-done | bytes 49184 | tf_op jit(solution)/shard_map/ppermute | solution.py:608
  17.8 4.6 %shard_map.285 = (bf16[1856,128]{1,0:T(8,128)(2,1)}, bf16[1856,128]{1,0:T(8,128)(2,1)}) custom-call(bf16[8,128,128]{2,1,0:T(8,128)(2,1)} %get-tuple-element.49.refs_0_, bf16[4,128,96]{2,1,0:T(8,128)(2,1)} %get-tuple-element.50.refs_1_, bf16[2,64,192]{2,1,0:T(8,128)(2,1)} %get-tuple-element.51.refs_2_, ...), custom_call_target="tpu_custom_call" | custom-call | flops 4000000000 | bytes 1000000 | tf_op jit(solution)/shard_map/pallas_call | solution.py:93
  22.4 5.7 %collective-permute-start.4 = (bf16[1856,128]{1,0:T(8,128)(2,1)}, bf16[1856,128]{1,0:T(8,128)(2,1)S(1)}, u32[]{:S(2)}, u32[]{:S(2)}) collective-permute-start(bf16[1856,128]{1,0:T(8,128)(2,1)} %get-tuple-element.63), channel_id=1, source_target_pairs={{0,1},{1,0},{2,3},{3,2},{4,5},{5,4},{6,7},{7,6},{8,9},{9,8},{10,11... | collective-permute-start | bytes 1425416 | tf_op jit(solution)/shard_map/ppermute | solution.py:586
  28.1 1.7 %collective-permute-done.4.refs_1_ = bf16[1856,128]{1,0:T(8,128)(2,1)S(1)} collective-permute-done((bf16[1856,128]{1,0:T(8,128)(2,1)}, bf16[1856,128]{1,0:T(8,128)(2,1)S(1)}, u32[]{:S(2)}, u32[]{:S(2)}) %collective-permute-start.4) | collective-permute-done | bytes 475168 | tf_op jit(solution)/shard_map/ppermute | solution.py:586
  30.5 2.1 %shard_map.286 = (bf16[464,128]{1,0:T(8,128)(2,1)}, bf16[464,128]{1,0:T(8,128)(2,1)}, bf16[464,128]{1,0:T(8,128)(2,1)}, bf16[464,128]{1,0:T(8,128)(2,1)}, bf16[2,32,384]{2,1,0:T(8,128)(2,1)}) custom-call(bf16[1856,128]{1,0:T(8,128)(2,1)} %get-tuple-element.62.refs_0_, bf16[1856,128]{1,0:T(8,128)(2,1)} %copy-done.37, ...), custom_call_target="tpu_custom_call" | custom-call | flops 2000000000 | bytes 1000000 | tf_op jit(solution)/shard_map/pallas_call | solution.py:93
  32.7 2.7 %collective-permute-start.10 = (bf16[2,32,384]{2,1,0:T(8,128)(2,1)}, bf16[2,32,384]{2,1,0:T(8,128)(2,1)S(1)}, u32[]{:S(2)}, u32[]{:S(2)}) collective-permute-start(bf16[2,32,384]{2,1,0:T(8,128)(2,1)} %get-tuple-element.69.refs_0_), channel_id=1, source_target_pairs={{6,0},{7,1},{0,2},{1,3},{2,4},{3,5},{4,6},{5,7},{14,8},{15,9},{8,1... | collective-permute-start | bytes 147464 | tf_op jit(solution)/shard_map/ppermute | solution.py:631
  35.3 2.5 %collective-permute-start.9 = (bf16[2,32,384]{2,1,0:T(8,128)(2,1)}, bf16[2,32,384]{2,1,0:T(8,128)(2,1)S(1)}, u32[]{:S(2)}, u32[]{:S(2)}) collective-permute-start(bf16[2,32,384]{2,1,0:T(8,128)(2,1)} %get-tuple-element.69.refs_0_), channel_id=1, source_target_pairs={{4,0},{5,1},{6,2},{7,3},{0,4},{1,5},{2,6},{3,7},{12,8},{13,9},{14,... | collective-permute-start | bytes 147464 | tf_op jit(solution)/shard_map/ppermute | solution.py:631
  37.9 1.4 %collective-permute-start.8 = (bf16[2,32,384]{2,1,0:T(8,128)(2,1)}, bf16[2,32,384]{2,1,0:T(8,128)(2,1)S(1)}, u32[]{:S(2)}, u32[]{:S(2)}) collective-permute-start(bf16[2,32,384]{2,1,0:T(8,128)(2,1)} %get-tuple-element.69.refs_0_), channel_id=1, source_target_pairs={{2,0},{3,1},{4,2},{5,3},{6,4},{7,5},{0,6},{1,7},{10,8},{11,9},{12,... | collective-permute-start | bytes 147464 | tf_op jit(solution)/shard_map/ppermute | solution.py:631
  39.2 4.8 %collective-permute-start.5 = (bf16[464,128]{1,0:T(8,128)(2,1)}, bf16[464,128]{1,0:T(8,128)(2,1)S(1)}, u32[]{:S(2)}, u32[]{:S(2)}) collective-permute-start(bf16[464,128]{1,0:T(8,128)(2,1)} %get-tuple-element.66), channel_id=1, source_target_pairs={{0,8},{8,16},{16,24},{24,0},{1,9},{9,17},{17,25},{25,1},{2,10},{10... | collective-permute-start | bytes 356360 | tf_op jit(solution)/shard_map/ppermute | solution.py:630
  45.0 2.9 %collective-permute-start.7 = (bf16[464,128]{1,0:T(8,128)(2,1)}, bf16[464,128]{1,0:T(8,128)(2,1)S(1)}, u32[]{:S(2)}, u32[]{:S(2)}) collective-permute-start(bf16[464,128]{1,0:T(8,128)(2,1)} %get-tuple-element.68), channel_id=1, source_target_pairs={{0,24},{8,0},{16,8},{24,16},{1,25},{9,1},{17,9},{25,17},{2,26},{10... | collective-permute-start | bytes 356360 | tf_op jit(solution)/shard_map/ppermute | solution.py:630
  48.8 1.1 %collective-permute-done.6.refs_2_ = bf16[464,128]{1,0:T(8,128)(2,1)S(1)} collective-permute-done((bf16[464,128]{1,0:T(8,128)(2,1)}, bf16[464,128]{1,0:T(8,128)(2,1)S(1)}, u32[]{:S(2)}, u32[]{:S(2)}) %collective-permute-start.6) | collective-permute-done | bytes 118816 | tf_op jit(solution)/shard_map/ppermute | solution.py:630
  49.8 1.8 %collective-permute-done.7.refs_3_ = bf16[464,128]{1,0:T(8,128)(2,1)S(1)} collective-permute-done((bf16[464,128]{1,0:T(8,128)(2,1)}, bf16[464,128]{1,0:T(8,128)(2,1)S(1)}, u32[]{:S(2)}, u32[]{:S(2)}) %collective-permute-start.7) | collective-permute-done | bytes 118816 | tf_op jit(solution)/shard_map/ppermute | solution.py:630
  52.7 1.7 %collective-permute-start.16 = (bf16[4,2,32,384]{3,2,1,0:T(8,128)(2,1)S(1)}, bf16[4,2,32,384]{3,2,1,0:T(8,128)(2,1)S(1)}, u32[]{:S(2)}, u32[]{:S(2)}) collective-permute-start(bf16[4,2,32,384]{3,2,1,0:T(8,128)(2,1)S(1)} %shard_map.287.refs_4_.refs_0_), channel_id=1, source_target_pairs={{24,0},{0,8},{8,16},{16,24},{25,1},{1,9},{9,17},{17,25},{26,2},{2,... | collective-permute-start | bytes 589832 | tf_op jit(solution)/shard_map/ppermute | solution.py:639
  57.2 2.8 %collective-permute-done.13.refs_3_ = bf16[464,128]{1,0:T(8,128)(2,1)S(1)} collective-permute-done((bf16[464,128]{1,0:T(8,128)(2,1)S(1)}, bf16[464,128]{1,0:T(8,128)(2,1)S(1)}, u32[]{:S(2)}, u32[]{:S(2)}) %collective-permute-start.13) | collective-permute-done | bytes 118816 | tf_op jit(solution)/shard_map/ppermute | solution.py:638
  60.2 5.9 %shard_map.289 = (bf16[48,8,256]{2,1,0:T(8,128)(2,1)}, bf16[96,4,128]{2,1,0:T(4,128)(2,1)}, bf16[2,64,192]{2,1,0:T(8,128)(2,1)}, bf16[1,32,384]{2,1,0:T(8,128)(2,1)}) custom-call(bf16[8,128,128]{2,1,0:T(8,128)(2,1)S(1)} %copy-done.24, bf16[4,128,96]{2,1,0:T(8,128)(2,1)S(1)} %copy-done.27, bf16[2,64,192]{2,1,0:T(8,128)(2,1)S(1)} %copy-done.30, ...), custom_call_target="tpu_custom_call" | custom-call | flops 6000000000 | bytes 1000000 | tf_op jit(solution)/shard_map/pallas_call | solution.py:93
  67.2 1.7 %collective-permute-start.19 = (bf16[464,128]{1,0:T(8,128)(2,1)S(1)}, bf16[464,128]{1,0:T(8,128)(2,1)S(1)}, u32[]{:S(2)}, u32[]{:S(2)}) collective-permute-start(bf16[464,128]{1,0:T(8,128)(2,1)S(1)} %shard_map.291.refs_8_.refs_0_), channel_id=1, source_target_pairs={{24,0},{0,8},{8,16},{16,24},{25,1},{1,9},{9,17},{17,25},{26,2},{2,... | collective-permute-start | bytes 356360 | tf_op jit(solution)/shard_map/ppermute | solution.py:658
  70.5 3.4 %collective-permute-done.19.refs_3_ = bf16[464,128]{1,0:T(8,128)(2,1)S(1)} collective-permute-done((bf16[464,128]{1,0:T(8,128)(2,1)S(1)}, bf16[464,128]{1,0:T(8,128)(2,1)S(1)}, u32[]{:S(2)}, u32[]{:S(2)}) %collective-permute-start.19) | collective-permute-done | bytes 118816 | tf_op jit(solution)/shard_map/ppermute | solution.py:658
  74.8 3.0 %shard_map.290 = (bf16[48,8,256]{2,1,0:T(8,128)(2,1)}, bf16[96,4,128]{2,1,0:T(4,128)(2,1)}, bf16[2,64,192]{2,1,0:T(8,128)(2,1)}, bf16[1,32,384]{2,1,0:T(8,128)(2,1)}) custom-call(bf16[8,128,128]{2,1,0:T(8,128)(2,1)S(1)} %copy-done.24, bf16[4,128,96]{2,1,0:T(8,128)(2,1)S(1)} %copy-done.27, bf16[2,64,192]{2,1,0:T(8,128)(2,1)S(1)} %copy-done.30, ...), custom_call_target="tpu_custom_call" | custom-call | flops 2000000000 | bytes 1000000 | tf_op jit(solution)/shard_map/pallas_call | solution.py:93
  79.3 5.2 %shard_map.292.refs_8_ = bf16[3,3,384,384]{3,2,1,0:T(8,128)(2,1)} custom-call(bf16[4,2,32,384]{3,2,1,0:T(8,128)(2,1)S(1)} %shard_map.287.refs_4_.refs_0_, bf16[4,2,32,384]{3,2,1,0:T(8,128)(2,1)S(1)} %collective-permute-done.14.refs_5_.refs_1_, bf16[4,2,32,384]{3,2,1,0:T(8,128)(2,1)S(1)} %collective-permute-done.15.refs_6_.refs_2_, ...), custom_call_target="tpu_custom_call" | custom-call | flops 5000000000 | bytes 1000000 | tf_op jit(solution)/shard_map/pallas_call | solution.py:93
  84.5 1.7 %copy-done.21 = bf16[3,3,384,384]{3,2,1,0:T(8,128)(2,1)S(1)} copy-done((bf16[3,3,384,384]{3,2,1,0:T(8,128)(2,1)S(1)}, bf16[3,3,384,384]{3,2,1,0:T(8,128)(2,1)}, u32[]{:S(2)}) %copy-start.21) | copy-done | bytes 2654232
  86.3 1.4 %shard_map.293 = (bf16[3,3,48,48]{3,2,1,0:T(8,128)(2,1)}, bf16[3,3,96,96]{3,2,1,0:T(8,128)(2,1)}, bf16[3,3,192,192]{3,2,1,0:T(8,128)(2,1)}) custom-call(bf16[464,128]{1,0:T(8,128)(2,1)S(1)} %shard_map.291.refs_8_.refs_0_, bf16[464,128]{1,0:T(8,128)(2,1)S(1)} %collective-permute-done.17.refs_1_, bf16[464,128]{1,0:T(8,128)(2,1)S(1)} %collective-permute-done.18.refs_2_, ...), custom_call_target="tpu_custom_call" | custom-call | flops 2000000000 | bytes 1000000 | tf_op jit(solution)/shard_map/pallas_call | solution.py:93
  (119 shorter events, 15.0 us)
Async XLA Ops:
  12.0 5.2 %collective-permute-start.2 = (bf16[2,32,384]{2,1,0:T(8,128)(2,1)}, bf16[2,32,384]{2,1,0:T(8,128)(2,1)S(1)}, u32[]{:S(2)}, u32[]{:S(2)}) collective-permute-start(bf16[2,32,384]{2,1,0:T(8,128)(2,1)} %get-tuple-element.57), channel_id=1, source_target_pairs={{0,8},{8,0},{16,24},{24,16},{1,9},{9,1},{17,25},{25,17},{2,10},{10... | collective-permute-start | bytes 147464 | tf_op jit(solution)/shard_map/ppermute | solution.py:608
  22.4 7.4 %collective-permute-start.4 = (bf16[1856,128]{1,0:T(8,128)(2,1)}, bf16[1856,128]{1,0:T(8,128)(2,1)S(1)}, u32[]{:S(2)}, u32[]{:S(2)}) collective-permute-start(bf16[1856,128]{1,0:T(8,128)(2,1)} %get-tuple-element.63), channel_id=1, source_target_pairs={{0,1},{1,0},{2,3},{3,2},{4,5},{5,4},{6,7},{7,6},{8,9},{9,8},{10,11... | collective-permute-start | bytes 1425416 | tf_op jit(solution)/shard_map/ppermute | solution.py:586
  32.7 12.3 %collective-permute-start.10 = (bf16[2,32,384]{2,1,0:T(8,128)(2,1)}, bf16[2,32,384]{2,1,0:T(8,128)(2,1)S(1)}, u32[]{:S(2)}, u32[]{:S(2)}) collective-permute-start(bf16[2,32,384]{2,1,0:T(8,128)(2,1)} %get-tuple-element.69.refs_0_), channel_id=1, source_target_pairs={{6,0},{7,1},{0,2},{1,3},{2,4},{3,5},{4,6},{5,7},{14,8},{15,9},{8,1... | collective-permute-start | bytes 147464 | tf_op jit(solution)/shard_map/ppermute | solution.py:631
  35.3 12.6 %collective-permute-start.9 = (bf16[2,32,384]{2,1,0:T(8,128)(2,1)}, bf16[2,32,384]{2,1,0:T(8,128)(2,1)S(1)}, u32[]{:S(2)}, u32[]{:S(2)}) collective-permute-start(bf16[2,32,384]{2,1,0:T(8,128)(2,1)} %get-tuple-element.69.refs_0_), channel_id=1, source_target_pairs={{4,0},{5,1},{6,2},{7,3},{0,4},{1,5},{2,6},{3,7},{12,8},{13,9},{14,... | collective-permute-start | bytes 147464 | tf_op jit(solution)/shard_map/ppermute | solution.py:631
  37.9 10.1 %collective-permute-start.8 = (bf16[2,32,384]{2,1,0:T(8,128)(2,1)}, bf16[2,32,384]{2,1,0:T(8,128)(2,1)S(1)}, u32[]{:S(2)}, u32[]{:S(2)}) collective-permute-start(bf16[2,32,384]{2,1,0:T(8,128)(2,1)} %get-tuple-element.69.refs_0_), channel_id=1, source_target_pairs={{2,0},{3,1},{4,2},{5,3},{6,4},{7,5},{0,6},{1,7},{10,8},{11,9},{12,... | collective-permute-start | bytes 147464 | tf_op jit(solution)/shard_map/ppermute | solution.py:631
  39.2 9.5 %collective-permute-start.5 = (bf16[464,128]{1,0:T(8,128)(2,1)}, bf16[464,128]{1,0:T(8,128)(2,1)S(1)}, u32[]{:S(2)}, u32[]{:S(2)}) collective-permute-start(bf16[464,128]{1,0:T(8,128)(2,1)} %get-tuple-element.66), channel_id=1, source_target_pairs={{0,8},{8,16},{16,24},{24,0},{1,9},{9,17},{17,25},{25,1},{2,10},{10... | collective-permute-start | bytes 356360 | tf_op jit(solution)/shard_map/ppermute | solution.py:630
  44.0 5.8 %collective-permute-start.6 = (bf16[464,128]{1,0:T(8,128)(2,1)}, bf16[464,128]{1,0:T(8,128)(2,1)S(1)}, u32[]{:S(2)}, u32[]{:S(2)}) collective-permute-start(bf16[464,128]{1,0:T(8,128)(2,1)} %get-tuple-element.67), channel_id=1, source_target_pairs={{0,16},{8,24},{16,0},{24,8},{1,17},{9,25},{17,1},{25,9},{2,18},{10... | collective-permute-start | bytes 356360 | tf_op jit(solution)/shard_map/ppermute | solution.py:630
  45.0 6.7 %collective-permute-start.7 = (bf16[464,128]{1,0:T(8,128)(2,1)}, bf16[464,128]{1,0:T(8,128)(2,1)S(1)}, u32[]{:S(2)}, u32[]{:S(2)}) collective-permute-start(bf16[464,128]{1,0:T(8,128)(2,1)} %get-tuple-element.68), channel_id=1, source_target_pairs={{0,24},{8,0},{16,8},{24,16},{1,25},{9,1},{17,9},{25,17},{2,26},{10... | collective-permute-start | bytes 356360 | tf_op jit(solution)/shard_map/ppermute | solution.py:630
  52.0 8.0 %collective-permute-start.13 = (bf16[464,128]{1,0:T(8,128)(2,1)S(1)}, bf16[464,128]{1,0:T(8,128)(2,1)S(1)}, u32[]{:S(2)}, u32[]{:S(2)}) collective-permute-start(bf16[464,128]{1,0:T(8,128)(2,1)S(1)} %shard_map.288.refs_20_.refs_0_), channel_id=1, source_target_pairs={{6,0},{7,1},{0,2},{1,3},{2,4},{3,5},{4,6},{5,7},{14,8},{15,9},{8,1... | collective-permute-start | bytes 356360 | tf_op jit(solution)/shard_map/ppermute | solution.py:638
  52.7 13.5 %collective-permute-start.16 = (bf16[4,2,32,384]{3,2,1,0:T(8,128)(2,1)S(1)}, bf16[4,2,32,384]{3,2,1,0:T(8,128)(2,1)S(1)}, u32[]{:S(2)}, u32[]{:S(2)}) collective-permute-start(bf16[4,2,32,384]{3,2,1,0:T(8,128)(2,1)S(1)} %shard_map.287.refs_4_.refs_0_), channel_id=1, source_target_pairs={{24,0},{0,8},{8,16},{16,24},{25,1},{1,9},{9,17},{17,25},{26,2},{2,... | collective-permute-start | bytes 589832 | tf_op jit(solution)/shard_map/ppermute | solution.py:639
  54.4 11.8 %collective-permute-start.15 = (bf16[4,2,32,384]{3,2,1,0:T(8,128)(2,1)S(1)}, bf16[4,2,32,384]{3,2,1,0:T(8,128)(2,1)S(1)}, u32[]{:S(2)}, u32[]{:S(2)}) collective-permute-start(bf16[4,2,32,384]{3,2,1,0:T(8,128)(2,1)S(1)} %shard_map.287.refs_4_.refs_0_), channel_id=1, source_target_pairs={{16,0},{24,8},{0,16},{8,24},{17,1},{25,9},{1,17},{9,25},{18,2},{26... | collective-permute-start | bytes 589832 | tf_op jit(solution)/shard_map/ppermute | solution.py:639
  55.4 10.7 %collective-permute-start.14 = (bf16[4,2,32,384]{3,2,1,0:T(8,128)(2,1)S(1)}, bf16[4,2,32,384]{3,2,1,0:T(8,128)(2,1)S(1)}, u32[]{:S(2)}, u32[]{:S(2)}) collective-permute-start(bf16[4,2,32,384]{3,2,1,0:T(8,128)(2,1)S(1)} %shard_map.287.refs_4_.refs_0_), channel_id=1, source_target_pairs={{8,0},{16,8},{24,16},{0,24},{9,1},{17,9},{25,17},{1,25},{10,2},{18... | collective-permute-start | bytes 589832 | tf_op jit(solution)/shard_map/ppermute | solution.py:639
  56.2 9.9 %collective-permute-start.12 = (bf16[464,128]{1,0:T(8,128)(2,1)S(1)}, bf16[464,128]{1,0:T(8,128)(2,1)S(1)}, u32[]{:S(2)}, u32[]{:S(2)}) collective-permute-start(bf16[464,128]{1,0:T(8,128)(2,1)S(1)} %shard_map.288.refs_20_.refs_0_), channel_id=1, source_target_pairs={{4,0},{5,1},{6,2},{7,3},{0,4},{1,5},{2,6},{3,7},{12,8},{13,9},{14,... | collective-permute-start | bytes 356360 | tf_op jit(solution)/shard_map/ppermute | solution.py:638
  60.0 6.2 %collective-permute-start.11 = (bf16[464,128]{1,0:T(8,128)(2,1)S(1)}, bf16[464,128]{1,0:T(8,128)(2,1)S(1)}, u32[]{:S(2)}, u32[]{:S(2)}) collective-permute-start(bf16[464,128]{1,0:T(8,128)(2,1)S(1)} %shard_map.288.refs_20_.refs_0_), channel_id=1, source_target_pairs={{2,0},{3,1},{4,2},{5,3},{6,4},{7,5},{0,6},{1,7},{10,8},{11,9},{12,... | collective-permute-start | bytes 356360 | tf_op jit(solution)/shard_map/ppermute | solution.py:638
  67.2 6.7 %collective-permute-start.19 = (bf16[464,128]{1,0:T(8,128)(2,1)S(1)}, bf16[464,128]{1,0:T(8,128)(2,1)S(1)}, u32[]{:S(2)}, u32[]{:S(2)}) collective-permute-start(bf16[464,128]{1,0:T(8,128)(2,1)S(1)} %shard_map.291.refs_8_.refs_0_), channel_id=1, source_target_pairs={{24,0},{0,8},{8,16},{16,24},{25,1},{1,9},{9,17},{17,25},{26,2},{2,... | collective-permute-start | bytes 356360 | tf_op jit(solution)/shard_map/ppermute | solution.py:658
  68.9 9.8 %collective-permute-start.27 = (bf16[4,2,32,384]{3,2,1,0:T(8,128)(2,1)S(1)}, bf16[4,2,32,384]{3,2,1,0:T(8,128)(2,1)S(1)}, u32[]{:S(2)}, u32[]{:S(2)}) collective-permute-start(bf16[4,2,32,384]{3,2,1,0:T(8,128)(2,1)S(1)} %collective-permute-done.16.refs_7_.refs_3_), channel_id=1, source_target_pairs={{0,1},{1,0},{2,3},{3,2},{4,5},{5,4},{6,7},{7,6},{8,9},{9,8},{10,11... | collective-permute-start | bytes 589832 | tf_op jit(solution)/shard_map/ppermute | solution.py:586
  69.1 10.1 %collective-permute-start.26 = (bf16[4,2,32,384]{3,2,1,0:T(8,128)(2,1)S(1)}, bf16[4,2,32,384]{3,2,1,0:T(8,128)(2,1)S(1)}, u32[]{:S(2)}, u32[]{:S(2)}) collective-permute-start(bf16[4,2,32,384]{3,2,1,0:T(8,128)(2,1)S(1)} %collective-permute-done.15.refs_6_.refs_2_), channel_id=1, source_target_pairs={{0,1},{1,0},{2,3},{3,2},{4,5},{5,4},{6,7},{7,6},{8,9},{9,8},{10,11... | collective-permute-start | bytes 589832 | tf_op jit(solution)/shard_map/ppermute | solution.py:586
  69.4 9.9 %collective-permute-start.25 = (bf16[4,2,32,384]{3,2,1,0:T(8,128)(2,1)S(1)}, bf16[4,2,32,384]{3,2,1,0:T(8,128)(2,1)S(1)}, u32[]{:S(2)}, u32[]{:S(2)}) collective-permute-start(bf16[4,2,32,384]{3,2,1,0:T(8,128)(2,1)S(1)} %collective-permute-done.14.refs_5_.refs_1_), channel_id=1, source_target_pairs={{0,1},{1,0},{2,3},{3,2},{4,5},{5,4},{6,7},{7,6},{8,9},{9,8},{10,11... | collective-permute-start | bytes 589832 | tf_op jit(solution)/shard_map/ppermute | solution.py:586
  69.6 8.3 %collective-permute-start.18 = (bf16[464,128]{1,0:T(8,128)(2,1)S(1)}, bf16[464,128]{1,0:T(8,128)(2,1)S(1)}, u32[]{:S(2)}, u32[]{:S(2)}) collective-permute-start(bf16[464,128]{1,0:T(8,128)(2,1)S(1)} %shard_map.291.refs_8_.refs_0_), channel_id=1, source_target_pairs={{16,0},{24,8},{0,16},{8,24},{17,1},{25,9},{1,17},{9,25},{18,2},{26... | collective-permute-start | bytes 356360 | tf_op jit(solution)/shard_map/ppermute | solution.py:658
  73.8 4.8 %collective-permute-start.17 = (bf16[464,128]{1,0:T(8,128)(2,1)S(1)}, bf16[464,128]{1,0:T(8,128)(2,1)S(1)}, u32[]{:S(2)}, u32[]{:S(2)}) collective-permute-start(bf16[464,128]{1,0:T(8,128)(2,1)S(1)} %shard_map.291.refs_8_.refs_0_), channel_id=1, source_target_pairs={{8,0},{16,8},{24,16},{0,24},{9,1},{17,9},{25,17},{1,25},{10,2},{18... | collective-permute-start | bytes 356360 | tf_op jit(solution)/shard_map/ppermute | solution.py:658
  77.9 6.6 %collective-permute-start.20 = (bf16[464,128]{1,0:T(8,128)(2,1)S(1)}, bf16[464,128]{1,0:T(8,128)(2,1)S(1)}, u32[]{:S(2)}, u32[]{:S(2)}) collective-permute-start(bf16[464,128]{1,0:T(8,128)(2,1)S(1)} %shard_map.291.refs_8_.refs_0_), channel_id=1, source_target_pairs={{0,1},{1,0},{2,3},{3,2},{4,5},{5,4},{6,7},{7,6},{8,9},{9,8},{10,11... | collective-permute-start | bytes 356360 | tf_op jit(solution)/shard_map/ppermute | solution.py:586
  78.7 5.8 %collective-permute-start.23 = (bf16[464,128]{1,0:T(8,128)(2,1)S(1)}, bf16[464,128]{1,0:T(8,128)(2,1)S(1)}, u32[]{:S(2)}, u32[]{:S(2)}) collective-permute-start(bf16[464,128]{1,0:T(8,128)(2,1)S(1)} %collective-permute-done.19.refs_3_), channel_id=1, source_target_pairs={{0,1},{1,0},{2,3},{3,2},{4,5},{5,4},{6,7},{7,6},{8,9},{9,8},{10,11... | collective-permute-start | bytes 356360 | tf_op jit(solution)/shard_map/ppermute | solution.py:586
  78.7 5.8 %collective-permute-start.22 = (bf16[464,128]{1,0:T(8,128)(2,1)S(1)}, bf16[464,128]{1,0:T(8,128)(2,1)S(1)}, u32[]{:S(2)}, u32[]{:S(2)}) collective-permute-start(bf16[464,128]{1,0:T(8,128)(2,1)S(1)} %collective-permute-done.18.refs_2_), channel_id=1, source_target_pairs={{0,1},{1,0},{2,3},{3,2},{4,5},{5,4},{6,7},{7,6},{8,9},{9,8},{10,11... | collective-permute-start | bytes 356360 | tf_op jit(solution)/shard_map/ppermute | solution.py:586
  79.2 5.3 %collective-permute-start.21 = (bf16[464,128]{1,0:T(8,128)(2,1)S(1)}, bf16[464,128]{1,0:T(8,128)(2,1)S(1)}, u32[]{:S(2)}, u32[]{:S(2)}) collective-permute-start(bf16[464,128]{1,0:T(8,128)(2,1)S(1)} %collective-permute-done.17.refs_1_), channel_id=1, source_target_pairs={{0,1},{1,0},{2,3},{3,2},{4,5},{5,4},{6,7},{7,6},{8,9},{9,8},{10,11... | collective-permute-start | bytes 356360 | tf_op jit(solution)/shard_map/ppermute | solution.py:586
  (42 other events, 254.4 us)

commit v3 on v2

--- a/solution.py
+++ b/solution.py
@@ -65,8 +65,10 @@
             ref.flush()
 
 
-def call(body, outs, args, scratch=(), far=(), far_out=(), placed=False, deps=(), raw_out=(), flops=2 * 10**9, limit=24):
+def call(body, outs, args, scratch=(), far=(), far_out=(), placed=False, deps=(), raw_out=(), token=False, flops=2 * 10**9, limit=24):
     far, far_out = list(far), list(far_out)
+    if token:
+        outs = [*outs, sds((8, 128), F32)]
     n_in, n_out, n_far = len(args), len(outs), len(far)
     n_moved = n_far + len(far_out)
 
@@ -80,6 +82,8 @@
             ins[k] = Fetched(held[at], copy(ins[k], held[at], at))
         for at, k in enumerate(far_out, n_far):
             results[k] = Sent(held[at], copy(held[at], results[k], at))
+        if token:
+            results.pop()[...] = jnp.zeros((8, 128), F32)
         body(*([place] if placed else []), *ins, *results, *rest[n_out + n_moved : -1])
         for k in far_out:
             results[k].flush()
@@ -602,7 +606,7 @@
     in_row = core_swap(inner)
     inner, outer = call(
         corner_kernel, [sds((2, 32, PACK), BF)] * 2, [left, right, in_row, out_row],
-        placed=True, far=range(4), far_out=range(2), limit=WHOLE,
+        placed=True, flops=6 * 10**9,
     )
     out_col = lax.ppermute(outer, "branch", hop(n_branch))
     in_col = lax.ppermute(inner, "branch", swap(n_branch))
@@ -619,46 +623,47 @@
         [sds((n_branch * size, 128), BF)] * 2,
         list(xt[:3]) + list(scs[:3]) + edges,
         [pltpu.VMEM((pieces * size, 128), BF), pad(0), pad(1), pad(2)],
-        placed=True, far=(2, 5, 6, 7, 8, 9, 1, 4, 0, 3), far_out=(0, 1), limit=WHOLE, flops=4 * 10**9,
+        placed=True, flops=6 * 10**9,
     )
     *parts, coarse = call(
         functools.partial(pair_sum_kernel, n_branch),
         [part] * n_branch + [sds(coarse.shape, BF)],
         [keep, core_swap(send), coarse],
-        placed=True, far=range(3), far_out=range(n_branch + 1), limit=WHOLE,
+        placed=True,
     )
     got = [lax.ppermute(parts[k], "branch", to_branch(k)) for k in range(1, n_branch)]
     held = [coarse] + [lax.ppermute(coarse, "rows", from_chip(k)) for k in range(1, n_chip)]
+    (part_sum,) = call(
+        functools.partial(sum_kernel, n_branch), [part], [parts[0]] + got, deps=held[1:]
+    )
+    got = [lax.ppermute(part_sum, "rows", from_chip(k)) for k in range(1, n_chip)]
     (held,) = call(
         functools.partial(stack_kernel, n_chip), [sds((n_chip,) + coarse.shape, BF)], held,
-    )
-    (part_sum,) = call(
-        functools.partial(sum_kernel, n_branch), [part], [parts[0]] + got, deps=(held,)
-    )
-    got = [lax.ppermute(part_sum, "rows", from_chip(k)) for k in range(1, n_chip)]
+        deps=(part_sum,),
+    )
     held = [held] + [lax.ppermute(held, "branch", from_branch(k)) for k in range(1, n_branch)]
-    merged = call(
+    *merged, merged_token = call(
         functools.partial(forward_kernel, dims),
         [sds(maps[0].shape, BF), sds(maps[1].shape, BF), sds(shapes[2], BF), sds(shapes[3], BF)],
         list(xt) + gs + fs + list(kernels) + edges,
         [pad(b) for b in range(4)] + wide,
-        placed=True, far_out=range(4), deps=(part_sum,), flops=6 * 10**9,
-    )
-    back = call(
+        placed=True, far_out=range(4), token=True, deps=(part_sum,), flops=6 * 10**9,
+    )
+    *back, back_token = call(
         functools.partial(adjoint_kernel, dims),
         [sds(maps[0].shape, BF), sds(maps[1].shape, BF), sds(shapes[2], BF), sds(shapes[3], BF)],
         list(xt) + list(scs) + list(ups) + list(kernels) + edges,
         [pad(b) for b in range(4)] + wide,
-        placed=True, far_out=range(4), deps=(part_sum,),
+        placed=True, far_out=range(4), token=True, deps=(part_sum,),
     )
     (total,) = call(
         functools.partial(ordered_sum_kernel, n_chip), [part], [part_sum] + got,
-        [pltpu.VMEM((n_chip, size, 128), BF)], placed=True, deps=(merged[3], *held[1:]),
+        [pltpu.VMEM((n_chip, size, 128), BF)], placed=True, deps=(merged_token, *held[1:]),
     )
     mine = [total] + [lax.ppermute(total, "branch", from_branch(k)) for k in range(1, n_branch)]
     held = held + [core_swap(a) for a in held]
     cols = n_branch * widths[3]
-    (kgrad3,) = call(
+    kgrad3, coarse_token = call(
         functools.partial(coarse_kernel, dims, n_branch, n_chip, scales[3]),
         [sds(kernels[3].shape, BF)],
         held,
@@ -670,14 +675,14 @@
             pltpu.VMEM(kernels[3].shape, BF),
             pltpu.SemaphoreType.DMA((3, 3)),
         ],
-        placed=True, raw_out=(0,), deps=(total,), flops=5 * 10**9, limit=COARSE,
+        placed=True, raw_out=(0,), token=True, deps=(total,), flops=5 * 10**9, limit=COARSE,
     )
     mine = mine + [core_swap(a) for a in mine]
     kgrads = call(
         functools.partial(finish_kernel, dims, n_branch, scales),
         [sds(k.shape, BF) for k in kernels[:3]],
         mine,
-        [pltpu.VMEM((pieces * size, 128), F32)], placed=True, far_out=range(3), deps=(kgrad3, back[3]),
+        [pltpu.VMEM((pieces * size, 128), F32)], placed=True, far_out=range(3), deps=(coarse_token, back_token),
     )
     return (
         merged[0], merged[1], unlast(merged[2]), unlast(merged[3]),

time: 88.2 us -> 79 us (0.90)
  Pallas kernels: 31.2 us -> 25 us
  local copies, waits for them, and re-layouts: 5.58 us -> 1.62 us
    pallas_call x11, Pallas kernels: 31.2 us -> 25 us  [call(): pl.pallas_call(wrapped, out_shape=outs, in_specs=[space(k, far) for k in...]
    ppermute x3, waiting for transfers between devices: 0.01 us -> 4.59 us  [local(): lax.ppermute(coarse, 'rows', from_chip(k))]
    unnamed x76 -> x54, local copies, waits for them, and re-layouts: 5.58 us -> 1.62 us
    ppermute x3, waiting for transfers between devices: 2.89 us -> 0.01 us  [local(): lax.ppermute(parts[k], 'branch', to_branch(k))]
    ppermute x3, starting transfers between devices: 1.74 us -> 4.36 us  [local(): lax.ppermute(part_sum, 'rows', from_chip(k))]
    ppermute x3, starting transfers between devices: 3.46 us -> 1.59 us  [local(): lax.ppermute(held, 'branch', from_branch(k))]
    ppermute x3, waiting for transfers between devices: 2.83 us -> 1.63 us  [local(): lax.ppermute(part_sum, 'rows', from_chip(k))]
  transfers between devices with their start and end apart: 28 -> 28, of which waited for: 8 -> 8; matrix products, arithmetic and copies ran while one was open for 0% -> 0% of each run, Pallas kernels for 16% -> 18%
where the time goes in v3:
time: 79 us; the launch traced here: 78.7 us
  starting transfers between devices  36.2 us (46%)
  Pallas kernels  25 us (32%)
  waiting for transfers between devices  14.6 us (18%)
  local copies, waits for them, and re-layouts  1.62 us (2%)
  between operations  1.33 us (2%)
    pallas_call x11, Pallas kernels, call(): pl.pallas_call(wrapped, out_shape=outs, in_specs=[space(k, far) for k in...  25 us
    ppermute x3, starting transfers between devices, local(): lax.ppermute(parts[k], 'branch', to_branch(k))  8.73 us
    ppermute x10, starting transfers between devices, local(): core_swap = lambda a: lax.ppermute(a, 'rows', swap(n_rows))  7.42 us
    ppermute x3, starting transfers between devices, local(): lax.ppermute(coarse, 'rows', from_chip(k))  6.97 us
    ppermute x3, waiting for transfers between devices, local(): lax.ppermute(total, 'branch', from_branch(k))  4.84 us
    ppermute x3, waiting for transfers between devices, local(): lax.ppermute(coarse, 'rows', from_chip(k))  4.59 us
    ppermute x3, starting transfers between devices, local(): lax.ppermute(part_sum, 'rows', from_chip(k))  4.36 us
    ppermute x1, starting transfers between devices, local(): in_col = lax.ppermute(inner, 'branch', swap(n_branch))  2.93 us
  transfers between devices with their start and end apart: 28, of which 8 were waited for; matrix products, arithmetic and copies ran while one was open for 0% of the time, Pallas kernels for 18%

profile of v3, /device:TPU:0, one launch (start us, length us, event | category | flops | bytes accessed | tf_op | source)
XLA Modules:
  0.0 78.7 jit_solution(17607411132915853757)
XLA Ops:
  0.6 6.9 %shard_map.283 = (bf16[8,128,128]{2,1,0:T(8,128)(2,1)}, bf16[4,128,96]{2,1,0:T(8,128)(2,1)}, bf16[2,64,192]{2,1,0:T(8,128)(2,1)}, bf16[1,32,384]{2,1,0:T(8,128)(...) custom-call(bf16[48,8,256]{2,1,0:T(8,128)(2,1)} %refs_0_.1, ...), custom_call_target="tpu_custom_call" | custom-call | flops 6000000000 | bytes 1000000 | tf_op jit(solution)/shard_map/pallas_call | solution.py:97
  11.0 2.9 %collective-permute-start.2 = (bf16[2,32,384]{2,1,0:T(8,128)(2,1)S(1)}, bf16[2,32,384]{2,1,0:T(8,128)(2,1)S(1)}, u32[]{:S(2)}, u32[]{:S(2)}) collective-permute-start(bf16[2,32,384]{2,1,0:T(8,128)(2,1)S(1)} %get-tuple-element.61), channel_id=1, source_target_pairs={{0,8},{8,0},{16,24},{24,16},{1,9},{9,1},{17,25},{25,17},{2,10},{10... | collective-permute-start | bytes 147464 | tf_op jit(solution)/shard_map/ppermute | solution.py:612
  14.6 1.4 %collective-permute-done.2.refs_8_.refs_18_ = bf16[2,32,384]{2,1,0:T(8,128)(2,1)S(1)} collective-permute-done((bf16[2,32,384]{2,1,0:T(8,128)(2,1)S(1)}, bf16[2,32,384]{2,1,0:T(8,128)(2,1)S(1)}, u32[]{:S(2)}, u32[]{:S(2)}) %collective-permute-start.2) | collective-permute-done | bytes 49184 | tf_op jit(solution)/shard_map/ppermute | solution.py:612
  16.0 2.0 %shard_map.285 = (bf16[1856,128]{1,0:T(8,128)(2,1)S(1)}, bf16[1856,128]{1,0:T(8,128)(2,1)S(1)}) custom-call(bf16[8,128,128]{2,1,0:T(8,128)(2,1)S(1)} %copy-done.12, bf16[4,128,96]{2,1,0:T(8,128)(2,1)S(1)} %copy-done.15, bf16[2,64,192]{2,1,0:T(8,128)(2,1)S(1)} %copy-done.18, bf16[8,128,128]{2,1,0:T(8,128)(2,1)S(1)} %copy-done.14, ...), custom_call_target="tpu_custom_call" | custom-call | flops 6000000000 | bytes 1000000 | tf_op jit(solution)/shard_map/pallas_call | solution.py:97
  18.0 5.5 %collective-permute-start.4 = (bf16[1856,128]{1,0:T(8,128)(2,1)S(1)}, bf16[1856,128]{1,0:T(8,128)(2,1)S(1)}, u32[]{:S(2)}, u32[]{:S(2)}) collective-permute-start(bf16[1856,128]{1,0:T(8,128)(2,1)S(1)} %get-tuple-element.67), channel_id=1, source_target_pairs={{0,1},{1,0},{2,3},{3,2},{4,5},{5,4},{6,7},{7,6},{8,9},{9,8},{10,11... | collective-permute-start | bytes 1425416 | tf_op jit(solution)/shard_map/ppermute | solution.py:590
  23.5 1.5 %collective-permute-done.4.refs_1_ = bf16[1856,128]{1,0:T(8,128)(2,1)S(1)} collective-permute-done((bf16[1856,128]{1,0:T(8,128)(2,1)S(1)}, bf16[1856,128]{1,0:T(8,128)(2,1)S(1)}, u32[]{:S(2)}, u32[]{:S(2)}) %collective-permute-start.4) | collective-permute-done | bytes 475168 | tf_op jit(solution)/shard_map/ppermute | solution.py:590
  25.1 4.7 %collective-permute-start.5 = (bf16[464,128]{1,0:T(8,128)(2,1)S(1)}, bf16[464,128]{1,0:T(8,128)(2,1)S(1)}, u32[]{:S(2)}, u32[]{:S(2)}) collective-permute-start(bf16[464,128]{1,0:T(8,128)(2,1)S(1)} %get-tuple-element.70), channel_id=1, source_target_pairs={{0,8},{8,16},{16,24},{24,0},{1,9},{9,17},{17,25},{25,1},{2,10},{10... | collective-permute-start | bytes 356360 | tf_op jit(solution)/shard_map/ppermute | solution.py:634
  29.8 1.2 %collective-permute-start.6 = (bf16[464,128]{1,0:T(8,128)(2,1)S(1)}, bf16[464,128]{1,0:T(8,128)(2,1)S(1)}, u32[]{:S(2)}, u32[]{:S(2)}) collective-permute-start(bf16[464,128]{1,0:T(8,128)(2,1)S(1)} %get-tuple-element.71), channel_id=1, source_target_pairs={{0,16},{8,24},{16,0},{24,8},{1,17},{9,25},{17,1},{25,9},{2,18},{10... | collective-permute-start | bytes 356360 | tf_op jit(solution)/shard_map/ppermute | solution.py:634
  31.0 2.8 %collective-permute-start.7 = (bf16[464,128]{1,0:T(8,128)(2,1)S(1)}, bf16[464,128]{1,0:T(8,128)(2,1)S(1)}, u32[]{:S(2)}, u32[]{:S(2)}) collective-permute-start(bf16[464,128]{1,0:T(8,128)(2,1)S(1)} %get-tuple-element.72), channel_id=1, source_target_pairs={{0,24},{8,0},{16,8},{24,16},{1,25},{9,1},{17,9},{25,17},{2,26},{10... | collective-permute-start | bytes 356360 | tf_op jit(solution)/shard_map/ppermute | solution.py:634
  33.8 2.9 %collective-permute-start.10 = (bf16[2,32,384]{2,1,0:T(8,128)(2,1)S(1)}, bf16[2,32,384]{2,1,0:T(8,128)(2,1)S(1)}, u32[]{:S(2)}, u32[]{:S(2)}) collective-permute-start(bf16[2,32,384]{2,1,0:T(8,128)(2,1)S(1)} %get-tuple-element.73.refs_0_), channel_id=1, source_target_pairs={{6,0},{7,1},{0,2},{1,3},{2,4},{3,5},{4,6},{5,7},{14,8},{15,9},{8,1... | collective-permute-start | bytes 147464 | tf_op jit(solution)/shard_map/ppermute | solution.py:635
  36.7 2.6 %collective-permute-start.9 = (bf16[2,32,384]{2,1,0:T(8,128)(2,1)S(1)}, bf16[2,32,384]{2,1,0:T(8,128)(2,1)S(1)}, u32[]{:S(2)}, u32[]{:S(2)}) collective-permute-start(bf16[2,32,384]{2,1,0:T(8,128)(2,1)S(1)} %get-tuple-element.73.refs_0_), channel_id=1, source_target_pairs={{4,0},{5,1},{6,2},{7,3},{0,4},{1,5},{2,6},{3,7},{12,8},{13,9},{14,... | collective-permute-start | bytes 147464 | tf_op jit(solution)/shard_map/ppermute | solution.py:635
  39.3 2.0 %collective-permute-done.10.refs_6_.refs_3_ = bf16[2,32,384]{2,1,0:T(8,128)(2,1)S(1)} collective-permute-done((bf16[2,32,384]{2,1,0:T(8,128)(2,1)S(1)}, bf16[2,32,384]{2,1,0:T(8,128)(2,1)S(1)}, u32[]{:S(2)}, u32[]{:S(2)}) %collective-permute-start.10) | collective-permute-done | bytes 49184 | tf_op jit(solution)/shard_map/ppermute | solution.py:635
  41.3 1.5 %collective-permute-start.8 = (bf16[2,32,384]{2,1,0:T(8,128)(2,1)S(1)}, bf16[2,32,384]{2,1,0:T(8,128)(2,1)S(1)}, u32[]{:S(2)}, u32[]{:S(2)}) collective-permute-start(bf16[2,32,384]{2,1,0:T(8,128)(2,1)S(1)} %get-tuple-element.73.refs_0_), channel_id=1, source_target_pairs={{2,0},{3,1},{4,2},{5,3},{6,4},{7,5},{0,6},{1,7},{10,8},{11,9},{12,... | collective-permute-start | bytes 147464 | tf_op jit(solution)/shard_map/ppermute | solution.py:635
  42.8 2.6 %collective-permute-done.8.refs_4_.refs_1_ = bf16[2,32,384]{2,1,0:T(8,128)(2,1)S(1)} collective-permute-done((bf16[2,32,384]{2,1,0:T(8,128)(2,1)S(1)}, bf16[2,32,384]{2,1,0:T(8,128)(2,1)S(1)}, u32[]{:S(2)}, u32[]{:S(2)}) %collective-permute-start.8) | collective-permute-done | bytes 49184 | tf_op jit(solution)/shard_map/ppermute | solution.py:635
  45.7 4.3 %collective-permute-start.12 = (bf16[464,128]{1,0:T(8,128)(2,1)S(1)}, bf16[464,128]{1,0:T(8,128)(2,1)S(1)}, u32[]{:S(2)}, u32[]{:S(2)}) collective-permute-start(bf16[464,128]{1,0:T(8,128)(2,1)S(1)} %shard_map.287.refs_20_.refs_4_.refs_0_), channel_id=1, source_target_pairs={{4,0},{5,1},{6,2},{7,3},{0,4},{1,5},{2,6},{3,7},{12,8},{13,9},{14,... | collective-permute-start | bytes 356360 | tf_op jit(solution)/shard_map/ppermute | solution.py:639
  50.9 1.6 %collective-permute-done.13.refs_3_ = bf16[464,128]{1,0:T(8,128)(2,1)S(1)} collective-permute-done((bf16[464,128]{1,0:T(8,128)(2,1)S(1)}, bf16[464,128]{1,0:T(8,128)(2,1)S(1)}, u32[]{:S(2)}, u32[]{:S(2)}) %collective-permute-start.13) | collective-permute-done | bytes 118816 | tf_op jit(solution)/shard_map/ppermute | solution.py:639
  53.4 5.9 %shard_map.288 = (bf16[48,8,256]{2,1,0:T(8,128)(2,1)}, bf16[96,4,128]{2,1,0:T(4,128)(2,1)}, bf16[2,64,192]{2,1,0:T(8,128)(2,1)}, bf16[1,32,384]{2,1,0:T(8,128)(2,1)}, f32[8,128]{1,0:T(8,128)S(1)}) custom-call(bf16[8,128,128]{2,1,0:T(8,128)(2,1)S(1)} %copy-done.12, bf16[4,128,96]{2,1,0:T(8,128)(2,1)S(1)} %copy-done.15, bf16[2,64,192]{2,1,0:T(8,128)(2,1)S(1)} %copy-done.18, ...), custom_call_target="tpu_custom_call" | custom-call | flops 6000000000 | bytes 1000000 | tf_op jit(solution)/shard_map/pallas_call | solution.py:97
  59.6 1.5 %collective-permute-start.19 = (bf16[464,128]{1,0:T(8,128)(2,1)S(1)}, bf16[464,128]{1,0:T(8,128)(2,1)S(1)}, u32[]{:S(2)}, u32[]{:S(2)}) collective-permute-start(bf16[464,128]{1,0:T(8,128)(2,1)S(1)} %shard_map.291.refs_8_.refs_0_), channel_id=1, source_target_pairs={{24,0},{0,8},{8,16},{16,24},{25,1},{1,9},{9,17},{17,25},{26,2},{2,... | collective-permute-start | bytes 356360 | tf_op jit(solution)/shard_map/ppermute | solution.py:663
  61.9 0.9 %collective-permute-start.18 = (bf16[464,128]{1,0:T(8,128)(2,1)S(1)}, bf16[464,128]{1,0:T(8,128)(2,1)S(1)}, u32[]{:S(2)}, u32[]{:S(2)}) collective-permute-start(bf16[464,128]{1,0:T(8,128)(2,1)S(1)} %shard_map.291.refs_8_.refs_0_), channel_id=1, source_target_pairs={{16,0},{24,8},{0,16},{8,24},{17,1},{25,9},{1,17},{9,25},{18,2},{26... | collective-permute-start | bytes 356360 | tf_op jit(solution)/shard_map/ppermute | solution.py:663
  62.7 3.8 %collective-permute-done.19.refs_3_ = bf16[464,128]{1,0:T(8,128)(2,1)S(1)} collective-permute-done((bf16[464,128]{1,0:T(8,128)(2,1)S(1)}, bf16[464,128]{1,0:T(8,128)(2,1)S(1)}, u32[]{:S(2)}, u32[]{:S(2)}) %collective-permute-start.19) | collective-permute-done | bytes 118816 | tf_op jit(solution)/shard_map/ppermute | solution.py:663
  67.0 3.1 %shard_map.289 = (bf16[48,8,256]{2,1,0:T(8,128)(2,1)}, bf16[96,4,128]{2,1,0:T(4,128)(2,1)}, bf16[2,64,192]{2,1,0:T(8,128)(2,1)}, bf16[1,32,384]{2,1,0:T(8,128)(2,1)}, f32[8,128]{1,0:T(8,128)S(1)}) custom-call(bf16[8,128,128]{2,1,0:T(8,128)(2,1)S(1)} %copy-done.12, bf16[4,128,96]{2,1,0:T(8,128)(2,1)S(1)} %copy-done.15, bf16[2,64,192]{2,1,0:T(8,128)(2,1)S(1)} %copy-done.18, ...), custom_call_target="tpu_custom_call" | custom-call | flops 2000000000 | bytes 1000000 | tf_op jit(solution)/shard_map/pallas_call | solution.py:97
  70.2 1.1 %collective-permute-done.17.refs_1_ = bf16[464,128]{1,0:T(8,128)(2,1)S(1)} collective-permute-done((bf16[464,128]{1,0:T(8,128)(2,1)S(1)}, bf16[464,128]{1,0:T(8,128)(2,1)S(1)}, u32[]{:S(2)}, u32[]{:S(2)}) %collective-permute-start.17) | collective-permute-done | bytes 118816 | tf_op jit(solution)/shard_map/ppermute | solution.py:663
  71.9 5.2 %shard_map.292 = (bf16[3,3,384,384]{3,2,1,0:T(8,128)(2,1)}, f32[8,128]{1,0:T(8,128)S(1)}) custom-call(bf16[4,2,32,384]{3,2,1,0:T(8,128)(2,1)S(1)} %shard_map.290.refs_0_, bf16[4,2,32,384]{3,2,1,0:T(8,128)(2,1)S(1)} %collective-permute-done.14.refs_5_.refs_1_, bf16[4,2,32,384]{3,2,1,0:T(8,128)(2,1)S(1)} %collective-permute-done.15.refs_6_.refs_2_, ...), custom_call_target="tpu_custom_call" | custom-call | flops 5000000000 | bytes 1000000 | tf_op jit(solution)/shard_map/pallas_call | solution.py:97
  77.2 1.4 %shard_map.293 = (bf16[3,3,48,48]{3,2,1,0:T(8,128)(2,1)}, bf16[3,3,96,96]{3,2,1,0:T(8,128)(2,1)}, bf16[3,3,192,192]{3,2,1,0:T(8,128)(2,1)}) custom-call(bf16[464,128]{1,0:T(8,128)(2,1)S(1)} %shard_map.291.refs_8_.refs_0_, bf16[464,128]{1,0:T(8,128)(2,1)S(1)} %collective-permute-done.17.refs_1_, bf16[464,128]{1,0:T(8,128)(2,1)S(1)} %collective-permute-done.18.refs_2_, ...), custom_call_target="tpu_custom_call" | custom-call | flops 2000000000 | bytes 1000000 | tf_op jit(solution)/shard_map/pallas_call | solution.py:97
  (97 shorter events, 8.2 us)
Async XLA Ops:
  11.0 5.0 %collective-permute-start.2 = (bf16[2,32,384]{2,1,0:T(8,128)(2,1)S(1)}, bf16[2,32,384]{2,1,0:T(8,128)(2,1)S(1)}, u32[]{:S(2)}, u32[]{:S(2)}) collective-permute-start(bf16[2,32,384]{2,1,0:T(8,128)(2,1)S(1)} %get-tuple-element.61), channel_id=1, source_target_pairs={{0,8},{8,0},{16,24},{24,16},{1,9},{9,1},{17,25},{25,17},{2,10},{10... | collective-permute-start | bytes 147464 | tf_op jit(solution)/shard_map/ppermute | solution.py:612
  18.0 6.9 %collective-permute-start.4 = (bf16[1856,128]{1,0:T(8,128)(2,1)S(1)}, bf16[1856,128]{1,0:T(8,128)(2,1)S(1)}, u32[]{:S(2)}, u32[]{:S(2)}) collective-permute-start(bf16[1856,128]{1,0:T(8,128)(2,1)S(1)} %get-tuple-element.67), channel_id=1, source_target_pairs={{0,1},{1,0},{2,3},{3,2},{4,5},{5,4},{6,7},{7,6},{8,9},{9,8},{10,11... | collective-permute-start | bytes 1425416 | tf_op jit(solution)/shard_map/ppermute | solution.py:590
  25.1 20.3 %collective-permute-start.5 = (bf16[464,128]{1,0:T(8,128)(2,1)S(1)}, bf16[464,128]{1,0:T(8,128)(2,1)S(1)}, u32[]{:S(2)}, u32[]{:S(2)}) collective-permute-start(bf16[464,128]{1,0:T(8,128)(2,1)S(1)} %get-tuple-element.70), channel_id=1, source_target_pairs={{0,8},{8,16},{16,24},{24,0},{1,9},{9,17},{17,25},{25,1},{2,10},{10... | collective-permute-start | bytes 356360 | tf_op jit(solution)/shard_map/ppermute | solution.py:634
  29.8 15.6 %collective-permute-start.6 = (bf16[464,128]{1,0:T(8,128)(2,1)S(1)}, bf16[464,128]{1,0:T(8,128)(2,1)S(1)}, u32[]{:S(2)}, u32[]{:S(2)}) collective-permute-start(bf16[464,128]{1,0:T(8,128)(2,1)S(1)} %get-tuple-element.71), channel_id=1, source_target_pairs={{0,16},{8,24},{16,0},{24,8},{1,17},{9,25},{17,1},{25,9},{2,18},{10... | collective-permute-start | bytes 356360 | tf_op jit(solution)/shard_map/ppermute | solution.py:634
  31.0 14.4 %collective-permute-start.7 = (bf16[464,128]{1,0:T(8,128)(2,1)S(1)}, bf16[464,128]{1,0:T(8,128)(2,1)S(1)}, u32[]{:S(2)}, u32[]{:S(2)}) collective-permute-start(bf16[464,128]{1,0:T(8,128)(2,1)S(1)} %get-tuple-element.72), channel_id=1, source_target_pairs={{0,24},{8,0},{16,8},{24,16},{1,25},{9,1},{17,9},{25,17},{2,26},{10... | collective-permute-start | bytes 356360 | tf_op jit(solution)/shard_map/ppermute | solution.py:634
  33.8 7.5 %collective-permute-start.10 = (bf16[2,32,384]{2,1,0:T(8,128)(2,1)S(1)}, bf16[2,32,384]{2,1,0:T(8,128)(2,1)S(1)}, u32[]{:S(2)}, u32[]{:S(2)}) collective-permute-start(bf16[2,32,384]{2,1,0:T(8,128)(2,1)S(1)} %get-tuple-element.73.refs_0_), channel_id=1, source_target_pairs={{6,0},{7,1},{0,2},{1,3},{2,4},{3,5},{4,6},{5,7},{14,8},{15,9},{8,1... | collective-permute-start | bytes 147464 | tf_op jit(solution)/shard_map/ppermute | solution.py:635
  36.7 6.1 %collective-permute-start.9 = (bf16[2,32,384]{2,1,0:T(8,128)(2,1)S(1)}, bf16[2,32,384]{2,1,0:T(8,128)(2,1)S(1)}, u32[]{:S(2)}, u32[]{:S(2)}) collective-permute-start(bf16[2,32,384]{2,1,0:T(8,128)(2,1)S(1)} %get-tuple-element.73.refs_0_), channel_id=1, source_target_pairs={{4,0},{5,1},{6,2},{7,3},{0,4},{1,5},{2,6},{3,7},{12,8},{13,9},{14,... | collective-permute-start | bytes 147464 | tf_op jit(solution)/shard_map/ppermute | solution.py:635
  41.3 4.1 %collective-permute-start.8 = (bf16[2,32,384]{2,1,0:T(8,128)(2,1)S(1)}, bf16[2,32,384]{2,1,0:T(8,128)(2,1)S(1)}, u32[]{:S(2)}, u32[]{:S(2)}) collective-permute-start(bf16[2,32,384]{2,1,0:T(8,128)(2,1)S(1)} %get-tuple-element.73.refs_0_), channel_id=1, source_target_pairs={{2,0},{3,1},{4,2},{5,3},{6,4},{7,5},{0,6},{1,7},{10,8},{11,9},{12,... | collective-permute-start | bytes 147464 | tf_op jit(solution)/shard_map/ppermute | solution.py:635
  45.6 6.9 %collective-permute-start.13 = (bf16[464,128]{1,0:T(8,128)(2,1)S(1)}, bf16[464,128]{1,0:T(8,128)(2,1)S(1)}, u32[]{:S(2)}, u32[]{:S(2)}) collective-permute-start(bf16[464,128]{1,0:T(8,128)(2,1)S(1)} %shard_map.287.refs_20_.refs_4_.refs_0_), channel_id=1, source_target_pairs={{6,0},{7,1},{0,2},{1,3},{2,4},{3,5},{4,6},{5,7},{14,8},{15,9},{8,1... | collective-permute-start | bytes 356360 | tf_op jit(solution)/shard_map/ppermute | solution.py:639
  45.7 13.6 %collective-permute-start.12 = (bf16[464,128]{1,0:T(8,128)(2,1)S(1)}, bf16[464,128]{1,0:T(8,128)(2,1)S(1)}, u32[]{:S(2)}, u32[]{:S(2)}) collective-permute-start(bf16[464,128]{1,0:T(8,128)(2,1)S(1)} %shard_map.287.refs_20_.refs_4_.refs_0_), channel_id=1, source_target_pairs={{4,0},{5,1},{6,2},{7,3},{0,4},{1,5},{2,6},{3,7},{12,8},{13,9},{14,... | collective-permute-start | bytes 356360 | tf_op jit(solution)/shard_map/ppermute | solution.py:639
  50.0 9.4 %collective-permute-start.11 = (bf16[464,128]{1,0:T(8,128)(2,1)S(1)}, bf16[464,128]{1,0:T(8,128)(2,1)S(1)}, u32[]{:S(2)}, u32[]{:S(2)}) collective-permute-start(bf16[464,128]{1,0:T(8,128)(2,1)S(1)} %shard_map.287.refs_20_.refs_4_.refs_0_), channel_id=1, source_target_pairs={{2,0},{3,1},{4,2},{5,3},{6,4},{7,5},{0,6},{1,7},{10,8},{11,9},{12,... | collective-permute-start | bytes 356360 | tf_op jit(solution)/shard_map/ppermute | solution.py:639
  50.0 9.3 %collective-permute-start.16 = (bf16[4,2,32,384]{3,2,1,0:T(8,128)(2,1)S(1)}, bf16[4,2,32,384]{3,2,1,0:T(8,128)(2,1)S(1)}, u32[]{:S(2)}, u32[]{:S(2)}) collective-permute-start(bf16[4,2,32,384]{3,2,1,0:T(8,128)(2,1)S(1)} %shard_map.290.refs_0_), channel_id=1, source_target_pairs={{24,0},{0,8},{8,16},{16,24},{25,1},{1,9},{9,17},{17,25},{26,2},{2,... | collective-permute-start | bytes 589832 | tf_op jit(solution)/shard_map/ppermute | solution.py:644
  50.1 9.3 %collective-permute-start.15 = (bf16[4,2,32,384]{3,2,1,0:T(8,128)(2,1)S(1)}, bf16[4,2,32,384]{3,2,1,0:T(8,128)(2,1)S(1)}, u32[]{:S(2)}, u32[]{:S(2)}) collective-permute-start(bf16[4,2,32,384]{3,2,1,0:T(8,128)(2,1)S(1)} %shard_map.290.refs_0_), channel_id=1, source_target_pairs={{16,0},{24,8},{0,16},{8,24},{17,1},{25,9},{1,17},{9,25},{18,2},{26... | collective-permute-start | bytes 589832 | tf_op jit(solution)/shard_map/ppermute | solution.py:644
  52.5 6.9 %collective-permute-start.14 = (bf16[4,2,32,384]{3,2,1,0:T(8,128)(2,1)S(1)}, bf16[4,2,32,384]{3,2,1,0:T(8,128)(2,1)S(1)}, u32[]{:S(2)}, u32[]{:S(2)}) collective-permute-start(bf16[4,2,32,384]{3,2,1,0:T(8,128)(2,1)S(1)} %shard_map.290.refs_0_), channel_id=1, source_target_pairs={{8,0},{16,8},{24,16},{0,24},{9,1},{17,9},{25,17},{1,25},{10,2},{18... | collective-permute-start | bytes 589832 | tf_op jit(solution)/shard_map/ppermute | solution.py:644
  59.6 6.9 %collective-permute-start.19 = (bf16[464,128]{1,0:T(8,128)(2,1)S(1)}, bf16[464,128]{1,0:T(8,128)(2,1)S(1)}, u32[]{:S(2)}, u32[]{:S(2)}) collective-permute-start(bf16[464,128]{1,0:T(8,128)(2,1)S(1)} %shard_map.291.refs_8_.refs_0_), channel_id=1, source_target_pairs={{24,0},{0,8},{8,16},{16,24},{25,1},{1,9},{9,17},{17,25},{26,2},{2,... | collective-permute-start | bytes 356360 | tf_op jit(solution)/shard_map/ppermute | solution.py:663
  61.1 10.2 %collective-permute-start.27 = (bf16[4,2,32,384]{3,2,1,0:T(8,128)(2,1)S(1)}, bf16[4,2,32,384]{3,2,1,0:T(8,128)(2,1)S(1)}, u32[]{:S(2)}, u32[]{:S(2)}) collective-permute-start(bf16[4,2,32,384]{3,2,1,0:T(8,128)(2,1)S(1)} %collective-permute-done.16.refs_7_.refs_3_), channel_id=1, source_target_pairs={{0,1},{1,0},{2,3},{3,2},{4,5},{5,4},{6,7},{7,6},{8,9},{9,8},{10,11... | collective-permute-start | bytes 589832 | tf_op jit(solution)/shard_map/ppermute | solution.py:590
  61.3 10.5 %collective-permute-start.26 = (bf16[4,2,32,384]{3,2,1,0:T(8,128)(2,1)S(1)}, bf16[4,2,32,384]{3,2,1,0:T(8,128)(2,1)S(1)}, u32[]{:S(2)}, u32[]{:S(2)}) collective-permute-start(bf16[4,2,32,384]{3,2,1,0:T(8,128)(2,1)S(1)} %collective-permute-done.15.refs_6_.refs_2_), channel_id=1, source_target_pairs={{0,1},{1,0},{2,3},{3,2},{4,5},{5,4},{6,7},{7,6},{8,9},{9,8},{10,11... | collective-permute-start | bytes 589832 | tf_op jit(solution)/shard_map/ppermute | solution.py:590
  61.6 10.3 %collective-permute-start.25 = (bf16[4,2,32,384]{3,2,1,0:T(8,128)(2,1)S(1)}, bf16[4,2,32,384]{3,2,1,0:T(8,128)(2,1)S(1)}, u32[]{:S(2)}, u32[]{:S(2)}) collective-permute-start(bf16[4,2,32,384]{3,2,1,0:T(8,128)(2,1)S(1)} %collective-permute-done.14.refs_5_.refs_1_), channel_id=1, source_target_pairs={{0,1},{1,0},{2,3},{3,2},{4,5},{5,4},{6,7},{7,6},{8,9},{9,8},{10,11... | collective-permute-start | bytes 589832 | tf_op jit(solution)/shard_map/ppermute | solution.py:590
  61.9 8.3 %collective-permute-start.18 = (bf16[464,128]{1,0:T(8,128)(2,1)S(1)}, bf16[464,128]{1,0:T(8,128)(2,1)S(1)}, u32[]{:S(2)}, u32[]{:S(2)}) collective-permute-start(bf16[464,128]{1,0:T(8,128)(2,1)S(1)} %shard_map.291.refs_8_.refs_0_), channel_id=1, source_target_pairs={{16,0},{24,8},{0,16},{8,24},{17,1},{25,9},{1,17},{9,25},{18,2},{26... | collective-permute-start | bytes 356360 | tf_op jit(solution)/shard_map/ppermute | solution.py:663
  66.5 4.8 %collective-permute-start.17 = (bf16[464,128]{1,0:T(8,128)(2,1)S(1)}, bf16[464,128]{1,0:T(8,128)(2,1)S(1)}, u32[]{:S(2)}, u32[]{:S(2)}) collective-permute-start(bf16[464,128]{1,0:T(8,128)(2,1)S(1)} %shard_map.291.refs_8_.refs_0_), channel_id=1, source_target_pairs={{8,0},{16,8},{24,16},{0,24},{9,1},{17,9},{25,17},{1,25},{10,2},{18... | collective-permute-start | bytes 356360 | tf_op jit(solution)/shard_map/ppermute | solution.py:663
  70.2 7.0 %collective-permute-start.20 = (bf16[464,128]{1,0:T(8,128)(2,1)S(1)}, bf16[464,128]{1,0:T(8,128)(2,1)S(1)}, u32[]{:S(2)}, u32[]{:S(2)}) collective-permute-start(bf16[464,128]{1,0:T(8,128)(2,1)S(1)} %shard_map.291.refs_8_.refs_0_), channel_id=1, source_target_pairs={{0,1},{1,0},{2,3},{3,2},{4,5},{5,4},{6,7},{7,6},{8,9},{9,8},{10,11... | collective-permute-start | bytes 356360 | tf_op jit(solution)/shard_map/ppermute | solution.py:590
  71.3 5.8 %collective-permute-start.23 = (bf16[464,128]{1,0:T(8,128)(2,1)S(1)}, bf16[464,128]{1,0:T(8,128)(2,1)S(1)}, u32[]{:S(2)}, u32[]{:S(2)}) collective-permute-start(bf16[464,128]{1,0:T(8,128)(2,1)S(1)} %collective-permute-done.19.refs_3_), channel_id=1, source_target_pairs={{0,1},{1,0},{2,3},{3,2},{4,5},{5,4},{6,7},{7,6},{8,9},{9,8},{10,11... | collective-permute-start | bytes 356360 | tf_op jit(solution)/shard_map/ppermute | solution.py:590
  71.3 5.8 %collective-permute-start.22 = (bf16[464,128]{1,0:T(8,128)(2,1)S(1)}, bf16[464,128]{1,0:T(8,128)(2,1)S(1)}, u32[]{:S(2)}, u32[]{:S(2)}) collective-permute-start(bf16[464,128]{1,0:T(8,128)(2,1)S(1)} %collective-permute-done.18.refs_2_), channel_id=1, source_target_pairs={{0,1},{1,0},{2,3},{3,2},{4,5},{5,4},{6,7},{7,6},{8,9},{9,8},{10,11... | collective-permute-start | bytes 356360 | tf_op jit(solution)/shard_map/ppermute | solution.py:590
  71.8 5.3 %collective-permute-start.21 = (bf16[464,128]{1,0:T(8,128)(2,1)S(1)}, bf16[464,128]{1,0:T(8,128)(2,1)S(1)}, u32[]{:S(2)}, u32[]{:S(2)}) collective-permute-start(bf16[464,128]{1,0:T(8,128)(2,1)S(1)} %collective-permute-done.17.refs_1_), channel_id=1, source_target_pairs={{0,1},{1,0},{2,3},{3,2},{4,5},{5,4},{6,7},{7,6},{8,9},{9,8},{10,11... | collective-permute-start | bytes 356360 | tf_op jit(solution)/shard_map/ppermute | solution.py:590
  (31 other events, 187.3 us)

commit v4 on v3

--- a/solution.py
+++ b/solution.py
@@ -14,6 +14,7 @@
 PACK = 384
 WHOLE = 61
 COARSE = 46
+FORWARD, ADJOINT, GATHERED, SMALL = 6 * 10**9, 3 * 10**9, 5 * 10**9, 4 * 10**9
 
 
 def dot(a, b, ca=1, cb=0):
@@ -65,7 +66,7 @@
             ref.flush()
 
 
-def call(body, outs, args, scratch=(), far=(), far_out=(), placed=False, deps=(), raw_out=(), token=False, flops=2 * 10**9, limit=24):
+def call(body, outs, args, scratch=(), far=(), far_out=(), placed=False, deps=(), raw_out=(), token=False, flops=SMALL, limit=24):
     far, far_out = list(far), list(far_out)
     if token:
         outs = [*outs, sds((8, 128), F32)]
@@ -96,6 +97,7 @@
     moved = [args[k] for k in far] + [outs[k] for k in far_out]
     return pl.pallas_call(
         wrapped,
+        name=getattr(body, "func", body).__name__,
         out_shape=outs,
         in_specs=[space(k, far) for k in range(n_in)]
         + [pl.BlockSpec(memory_space=pl.ANY) for _ in deps],
@@ -543,14 +545,13 @@
 
 def finish_kernel(dims, n_branch, scales, idx, *refs):
     channels = dims[2]
-    parts = refs[: 2 * n_branch]
-    outs, flat = refs[-4:-1], refs[-1]
+    own, other, *outs, flat = refs
     c0, c1, c2 = channels[0], channels[1], channels[2]
-    size = parts[0].shape[0]
-    for k, part in enumerate(parts):
-        core, band = (idx[0] + k // n_branch) % 2, (idx[1] + k) % n_branch
-        at = pl.multiple_of((core * n_branch + band) * size, 16)
-        flat[pl.ds(at, size), :] = part[...].astype(F32)
+    size = own.shape[1]
+    for k in range(n_branch):
+        for part, core in ((own, idx[0]), (other, 1 - idx[0])):
+            at = pl.multiple_of((core * n_branch + (idx[1] + k) % n_branch) * size, 16)
+            flat[pl.ds(at, size), :] = part[k].astype(F32)
     base1 = 9 * c2 * 3 // 2
     base0 = base1 + 9 * c1
     half = c2 // 2
@@ -633,8 +634,15 @@
     )
     got = [lax.ppermute(parts[k], "branch", to_branch(k)) for k in range(1, n_branch)]
     held = [coarse] + [lax.ppermute(coarse, "rows", from_chip(k)) for k in range(1, n_chip)]
+    *back, back_token = call(
+        functools.partial(adjoint_kernel, dims),
+        [sds(maps[0].shape, BF), sds(maps[1].shape, BF), sds(shapes[2], BF), sds(shapes[3], BF)],
+        list(xt) + list(scs) + list(ups) + list(kernels) + edges,
+        [pad(b) for b in range(4)] + wide,
+        placed=True, far_out=range(4), token=True, deps=(parts[0],), flops=ADJOINT,
+    )
     (part_sum,) = call(
-        functools.partial(sum_kernel, n_branch), [part], [parts[0]] + got, deps=held[1:]
+        functools.partial(sum_kernel, n_branch), [part], [parts[0]] + got, deps=(back_token, *held[1:])
     )
     got = [lax.ppermute(part_sum, "rows", from_chip(k)) for k in range(1, n_chip)]
     (held,) = call(
@@ -647,14 +655,7 @@
         [sds(maps[0].shape, BF), sds(maps[1].shape, BF), sds(shapes[2], BF), sds(shapes[3], BF)],
         list(xt) + gs + fs + list(kernels) + edges,
         [pad(b) for b in range(4)] + wide,
-        placed=True, far_out=range(4), token=True, deps=(part_sum,), flops=6 * 10**9,
-    )
-    *back, back_token = call(
-        functools.partial(adjoint_kernel, dims),
-        [sds(maps[0].shape, BF), sds(maps[1].shape, BF), sds(shapes[2], BF), sds(shapes[3], BF)],
-        list(xt) + list(scs) + list(ups) + list(kernels) + edges,
-        [pad(b) for b in range(4)] + wide,
-        placed=True, far_out=range(4), token=True, deps=(part_sum,),
+        placed=True, far_out=range(4), token=True, deps=(part_sum,), flops=FORWARD,
     )
     (total,) = call(
         functools.partial(ordered_sum_kernel, n_chip), [part], [part_sum] + got,
@@ -675,14 +676,17 @@
             pltpu.VMEM(kernels[3].shape, BF),
             pltpu.SemaphoreType.DMA((3, 3)),
         ],
-        placed=True, raw_out=(0,), token=True, deps=(total,), flops=5 * 10**9, limit=COARSE,
-    )
-    mine = mine + [core_swap(a) for a in mine]
+        placed=True, raw_out=(0,), token=True, deps=(total,), flops=GATHERED, limit=COARSE,
+    )
+    (mine,) = call(
+        functools.partial(stack_kernel, n_branch), [sds((n_branch, size, 128), BF)], mine,
+        deps=(coarse_token, back_token,),
+    )
     kgrads = call(
         functools.partial(finish_kernel, dims, n_branch, scales),
         [sds(k.shape, BF) for k in kernels[:3]],
-        mine,
-        [pltpu.VMEM((pieces * size, 128), F32)], placed=True, far_out=range(3), deps=(coarse_token, back_token),
+        [mine, core_swap(mine)],
+        [pltpu.VMEM((pieces * size, 128), F32)], placed=True, far_out=range(3),
     )
     return (
         merged[0], merged[1], unlast(merged[2]), unlast(merged[3]),

time: 79 us -> 74 us (0.937)
  waiting for transfers between devices: 14.6 us -> 6.8 us
  starting transfers between devices: 36.2 us -> 38.9 us
    ppermute x3, waiting for transfers between devices: 4.84 us -> 0.01 us  [local(): lax.ppermute(total, 'branch', from_branch(k))]
    ppermute x3, waiting for transfers between devices: 4.59 us -> 0.01 us  [local(): lax.ppermute(coarse, 'rows', from_chip(k))]
    ppermute x3, starting transfers between devices: 1.59 us -> 4.56 us  [local(): lax.ppermute(held, 'branch', from_branch(k))]
    ppermute x10 -> x7, waiting for transfers between devices: 2.13 us -> 3.95 us  [local(): core_swap = lambda a: lax.ppermute(a, 'rows', swap(n_rows))]
    ppermute x10 -> x7, starting transfers between devices: 7.42 us -> 7.13 us  [local(): core_swap = lambda a: lax.ppermute(a, 'rows', swap(n_rows))]
    pallas_call x11 -> x12, Pallas kernels: 25 us -> 25.1 us  [call(): pl.pallas_call(wrapped, name=getattr(body, 'func', body).__name__, out_sh...]
  transfers between devices with their start and end apart: 28 -> 25, of which waited for: 8 -> 6; matrix products, arithmetic and copies ran while one was open for 0% -> 0% of each run, Pallas kernels for 18% -> 20%
where the time goes in v4:
time: 74 us; the launch traced here: 73.7 us
  starting transfers between devices  38.9 us (53%)
  Pallas kernels  25.1 us (34%)
  waiting for transfers between devices  6.8 us (9%)
  local copies, waits for them, and re-layouts  1.61 us (2%)
  between operations  1.29 us (2%)
    pallas_call x12, Pallas kernels, call(): pl.pallas_call(wrapped, name=getattr(body, 'func', body).__name__, out_sh...  25.1 us
    ppermute x3, starting transfers between devices, local(): lax.ppermute(parts[k], 'branch', to_branch(k))  8.67 us
    ppermute x7, starting transfers between devices, local(): core_swap = lambda a: lax.ppermute(a, 'rows', swap(n_rows))  7.13 us
    ppermute x3, starting transfers between devices, local(): lax.ppermute(coarse, 'rows', from_chip(k))  6.88 us
    ppermute x3, starting transfers between devices, local(): lax.ppermute(held, 'branch', from_branch(k))  4.56 us
    ppermute x7, waiting for transfers between devices, local(): core_swap = lambda a: lax.ppermute(a, 'rows', swap(n_rows))  3.95 us
    ppermute x3, starting transfers between devices, local(): lax.ppermute(part_sum, 'rows', from_chip(k))  3.88 us
    ppermute x3, starting transfers between devices, local(): lax.ppermute(total, 'branch', from_branch(k))  3.58 us
  transfers between devices with their start and end apart: 25, of which 6 were waited for; matrix products, arithmetic and copies ran while one was open for 0% of the time, Pallas kernels for 20%

profile of v4, /device:TPU:0, one launch (start us, length us, event | category | flops | bytes accessed | tf_op | source)
XLA Modules:
  0.0 73.7 jit_solution(3362065633821636006)
XLA Ops:
  0.6 6.9 %upstream_kernel.1 = (bf16[8,128,128]{2,1,0:T(8,128)(2,1)}, bf16[4,128,96]{2,1,0:T(8,128)(2,1)}, bf16[2,64,192]{2,1,0:T(8,128)(2,1)}, bf16[1,32,384]{2,1,0:T(8,1...) custom-call(bf16[48,8,256]{2,1,0:T(8,128)(2,1)} %refs_0_.1, ...), custom_call_target="tpu_custom_call" | custom-call | flops 6000000000 | bytes 1000000 | tf_op jit(solution)/shard_map/upstream_kernel/pallas_call | solution.py:98
  9.4 0.7 copy-done.25
  11.0 2.9 %collective-permute-start.2 = (bf16[2,32,384]{2,1,0:T(8,128)(2,1)S(1)}, bf16[2,32,384]{2,1,0:T(8,128)(2,1)S(1)}, u32[]{:S(2)}, u32[]{:S(2)}) collective-permute-start(bf16[2,32,384]{2,1,0:T(8,128)(2,1)S(1)} %get-tuple-element.61), channel_id=1, source_target_pairs={{0,8},{8,0},{16,24},{24,16},{1,9},{9,1},{17,25},{25,17},{2,10},{10... | collective-permute-start | bytes 147464 | tf_op jit(solution)/shard_map/ppermute | solution.py:613
  14.6 1.4 %collective-permute-done.2.refs_8_.refs_18_ = bf16[2,32,384]{2,1,0:T(8,128)(2,1)S(1)} collective-permute-done((bf16[2,32,384]{2,1,0:T(8,128)(2,1)S(1)}, bf16[2,32,384]{2,1,0:T(8,128)(2,1)S(1)}, u32[]{:S(2)}, u32[]{:S(2)}) %collective-permute-start.2) | collective-permute-done | bytes 49184 | tf_op jit(solution)/shard_map/ppermute | solution.py:613
  16.0 2.0 %weight_grads_kernel.1 = (bf16[1856,128]{1,0:T(8,128)(2,1)S(1)}, bf16[1856,128]{1,0:T(8,128)(2,1)S(1)}) custom-call(bf16[8,128,128]{2,1,0:T(8,128)(2,1)S(1)} %copy-done.12, bf16[4,128,96]{2,1,0:T(8,128)(2,1)S(1)} %copy-done.15, bf16[2,64,192]{2,1,0:T(8,128)(2,1)S(1)} %copy-done.18, bf16[8,128,128]{2,1,0:T(8,128)(2,1)S(1)} %copy-done.14, ...), custom_call_target="tpu_custom_call" | custom-call | flops 6000000000 | bytes 1000000 | tf_op jit(solution)/shard_map/weight_grads_kernel/pallas_call | solution.py:98
  18.1 5.5 %collective-permute-start.4 = (bf16[1856,128]{1,0:T(8,128)(2,1)S(1)}, bf16[1856,128]{1,0:T(8,128)(2,1)S(1)}, u32[]{:S(2)}, u32[]{:S(2)}) collective-permute-start(bf16[1856,128]{1,0:T(8,128)(2,1)S(1)} %get-tuple-element.67), channel_id=1, source_target_pairs={{0,1},{1,0},{2,3},{3,2},{4,5},{5,4},{6,7},{7,6},{8,9},{9,8},{10,11... | collective-permute-start | bytes 1425416 | tf_op jit(solution)/shard_map/ppermute | solution.py:591
  23.5 1.5 %collective-permute-done.4.refs_1_ = bf16[1856,128]{1,0:T(8,128)(2,1)S(1)} collective-permute-done((bf16[1856,128]{1,0:T(8,128)(2,1)S(1)}, bf16[1856,128]{1,0:T(8,128)(2,1)S(1)}, u32[]{:S(2)}, u32[]{:S(2)}) %collective-permute-start.4) | collective-permute-done | bytes 475168 | tf_op jit(solution)/shard_map/ppermute | solution.py:591
  25.2 2.9 %collective-permute-start.10 = (bf16[2,32,384]{2,1,0:T(8,128)(2,1)S(1)}, bf16[2,32,384]{2,1,0:T(8,128)(2,1)S(1)}, u32[]{:S(2)}, u32[]{:S(2)}) collective-permute-start(bf16[2,32,384]{2,1,0:T(8,128)(2,1)S(1)} %get-tuple-element.79.refs_0_), channel_id=1, source_target_pairs={{6,0},{7,1},{0,2},{1,3},{2,4},{3,5},{4,6},{5,7},{14,8},{15,9},{8,1... | collective-permute-start | bytes 147464 | tf_op jit(solution)/shard_map/ppermute | solution.py:636
  28.2 2.5 %collective-permute-start.9 = (bf16[2,32,384]{2,1,0:T(8,128)(2,1)S(1)}, bf16[2,32,384]{2,1,0:T(8,128)(2,1)S(1)}, u32[]{:S(2)}, u32[]{:S(2)}) collective-permute-start(bf16[2,32,384]{2,1,0:T(8,128)(2,1)S(1)} %get-tuple-element.79.refs_0_), channel_id=1, source_target_pairs={{4,0},{5,1},{6,2},{7,3},{0,4},{1,5},{2,6},{3,7},{12,8},{13,9},{14,... | collective-permute-start | bytes 147464 | tf_op jit(solution)/shard_map/ppermute | solution.py:636
  30.7 1.4 %collective-permute-start.8 = (bf16[2,32,384]{2,1,0:T(8,128)(2,1)S(1)}, bf16[2,32,384]{2,1,0:T(8,128)(2,1)S(1)}, u32[]{:S(2)}, u32[]{:S(2)}) collective-permute-start(bf16[2,32,384]{2,1,0:T(8,128)(2,1)S(1)} %get-tuple-element.79.refs_0_), channel_id=1, source_target_pairs={{2,0},{3,1},{4,2},{5,3},{6,4},{7,5},{0,6},{1,7},{10,8},{11,9},{12,... | collective-permute-start | bytes 147464 | tf_op jit(solution)/shard_map/ppermute | solution.py:636
  32.1 4.8 %collective-permute-start.5 = (bf16[464,128]{1,0:T(8,128)(2,1)S(1)}, bf16[464,128]{1,0:T(8,128)(2,1)S(1)}, u32[]{:S(2)}, u32[]{:S(2)}) collective-permute-start(bf16[464,128]{1,0:T(8,128)(2,1)S(1)} %get-tuple-element.70), channel_id=1, source_target_pairs={{0,8},{8,16},{16,24},{24,0},{1,9},{9,17},{17,25},{25,1},{2,10},{10... | collective-permute-start | bytes 356360 | tf_op jit(solution)/shard_map/ppermute | solution.py:635
  36.9 1.0 %collective-permute-start.6 = (bf16[464,128]{1,0:T(8,128)(2,1)S(1)}, bf16[464,128]{1,0:T(8,128)(2,1)S(1)}, u32[]{:S(2)}, u32[]{:S(2)}) collective-permute-start(bf16[464,128]{1,0:T(8,128)(2,1)S(1)} %get-tuple-element.71), channel_id=1, source_target_pairs={{0,16},{8,24},{16,0},{24,8},{1,17},{9,25},{17,1},{25,9},{2,18},{10... | collective-permute-start | bytes 356360 | tf_op jit(solution)/shard_map/ppermute | solution.py:635
  37.9 2.9 %collective-permute-start.7 = (bf16[464,128]{1,0:T(8,128)(2,1)S(1)}, bf16[464,128]{1,0:T(8,128)(2,1)S(1)}, u32[]{:S(2)}, u32[]{:S(2)}) collective-permute-start(bf16[464,128]{1,0:T(8,128)(2,1)S(1)} %get-tuple-element.72), channel_id=1, source_target_pairs={{0,24},{8,0},{16,8},{24,16},{1,25},{9,1},{17,9},{25,17},{2,26},{10... | collective-permute-start | bytes 356360 | tf_op jit(solution)/shard_map/ppermute | solution.py:635
  40.9 3.2 %adjoint_kernel.1 = (bf16[48,8,256]{2,1,0:T(8,128)(2,1)}, bf16[96,4,128]{2,1,0:T(4,128)(2,1)}, bf16[2,64,192]{2,1,0:T(8,128)(2,1)}, bf16[1,32,384]{2,1,0:T(8,128)(2,1)}, f32[8,128]{1,0:T(8,128)S(1)}) custom-call(bf16[8,128,128]{2,1,0:T(8,128)(2,1)S(1)} %copy-done.12, bf16[4,128,96]{2,1,0:T(8,128)(2,1)S(1)} %copy-done.15, bf16[2,64,192]{2,1,0:T(8,128)(2,1)S(1)} %copy-done.18, ...), custom_call_target="tpu_custom_call" | custom-call | flops 3000000000 | bytes 1000000 | tf_op jit(solution)/shard_map/adjoint_kernel/pallas_call | solution.py:98
  45.6 2.8 %collective-permute-start.11 = (bf16[464,128]{1,0:T(8,128)(2,1)S(1)}, bf16[464,128]{1,0:T(8,128)(2,1)S(1)}, u32[]{:S(2)}, u32[]{:S(2)}) collective-permute-start(bf16[464,128]{1,0:T(8,128)(2,1)S(1)} %sum_kernel.1.refs_20_.refs_4_.refs_0_), channel_id=1, source_target_pairs={{2,0},{3,1},{4,2},{5,3},{6,4},{7,5},{0,6},{1,7},{10,8},{11,9},{12,... | collective-permute-start | bytes 356360 | tf_op jit(solution)/shard_map/ppermute | solution.py:647
  48.4 1.8 %collective-permute-start.16 = (bf16[4,2,32,384]{3,2,1,0:T(8,128)(2,1)S(1)}, bf16[4,2,32,384]{3,2,1,0:T(8,128)(2,1)S(1)}, u32[]{:S(2)}, u32[]{:S(2)}) collective-permute-start(bf16[4,2,32,384]{3,2,1,0:T(8,128)(2,1)S(1)} %stack_kernel.2.refs_0_), channel_id=1, source_target_pairs={{24,0},{0,8},{8,16},{16,24},{25,1},{1,9},{9,17},{17,25},{26,2},{2,... | collective-permute-start | bytes 589832 | tf_op jit(solution)/shard_map/ppermute | solution.py:652
  50.2 1.1 %collective-permute-start.15 = (bf16[4,2,32,384]{3,2,1,0:T(8,128)(2,1)S(1)}, bf16[4,2,32,384]{3,2,1,0:T(8,128)(2,1)S(1)}, u32[]{:S(2)}, u32[]{:S(2)}) collective-permute-start(bf16[4,2,32,384]{3,2,1,0:T(8,128)(2,1)S(1)} %stack_kernel.2.refs_0_), channel_id=1, source_target_pairs={{16,0},{24,8},{0,16},{8,24},{17,1},{25,9},{1,17},{9,25},{18,2},{26... | collective-permute-start | bytes 589832 | tf_op jit(solution)/shard_map/ppermute | solution.py:652
  51.2 1.1 %collective-permute-done.13.refs_3_ = bf16[464,128]{1,0:T(8,128)(2,1)S(1)} collective-permute-done((bf16[464,128]{1,0:T(8,128)(2,1)S(1)}, bf16[464,128]{1,0:T(8,128)(2,1)S(1)}, u32[]{:S(2)}, u32[]{:S(2)}) %collective-permute-start.13) | collective-permute-done | bytes 118816 | tf_op jit(solution)/shard_map/ppermute | solution.py:647
  52.4 1.7 %collective-permute-start.14 = (bf16[4,2,32,384]{3,2,1,0:T(8,128)(2,1)S(1)}, bf16[4,2,32,384]{3,2,1,0:T(8,128)(2,1)S(1)}, u32[]{:S(2)}, u32[]{:S(2)}) collective-permute-start(bf16[4,2,32,384]{3,2,1,0:T(8,128)(2,1)S(1)} %stack_kernel.2.refs_0_), channel_id=1, source_target_pairs={{8,0},{16,8},{24,16},{0,24},{9,1},{17,9},{25,17},{1,25},{10,2},{18... | collective-permute-start | bytes 589832 | tf_op jit(solution)/shard_map/ppermute | solution.py:652
  54.2 5.9 %forward_kernel.1 = (bf16[48,8,256]{2,1,0:T(8,128)(2,1)}, bf16[96,4,128]{2,1,0:T(4,128)(2,1)}, bf16[2,64,192]{2,1,0:T(8,128)(2,1)}, bf16[1,32,384]{2,1,0:T(8,128)(2,1)}, f32[8,128]{1,0:T(8,128)S(1)}) custom-call(bf16[8,128,128]{2,1,0:T(8,128)(2,1)S(1)} %copy-done.12, bf16[4,128,96]{2,1,0:T(8,128)(2,1)S(1)} %copy-done.15, bf16[2,64,192]{2,1,0:T(8,128)(2,1)S(1)} %copy-done.18, ...), custom_call_target="tpu_custom_call" | custom-call | flops 6000000000 | bytes 1000000 | tf_op jit(solution)/shard_map/forward_kernel/pallas_call | solution.py:98
  62.2 2.7 %collective-permute-start.17 = (bf16[464,128]{1,0:T(8,128)(2,1)S(1)}, bf16[464,128]{1,0:T(8,128)(2,1)S(1)}, u32[]{:S(2)}, u32[]{:S(2)}) collective-permute-start(bf16[464,128]{1,0:T(8,128)(2,1)S(1)} %ordered_sum_kernel.1.refs_8_.refs_0_), channel_id=1, source_target_pairs={{8,0},{16,8},{24,16},{0,24},{9,1},{17,9},{25,17},{1,25},{10,2},{18... | collective-permute-start | bytes 356360 | tf_op jit(solution)/shard_map/ppermute | solution.py:664
  65.0 5.2 %coarse_kernel.1 = (bf16[3,3,384,384]{3,2,1,0:T(8,128)(2,1)}, f32[8,128]{1,0:T(8,128)S(1)}) custom-call(bf16[4,2,32,384]{3,2,1,0:T(8,128)(2,1)S(1)} %stack_kernel.2.refs_0_, bf16[4,2,32,384]{3,2,1,0:T(8,128)(2,1)S(1)} %collective-permute-done.14.refs_5_.refs_1_, bf16[4,2,32,384]{3,2,1,0:T(8,128)(2,1)S(1)} %collective-permute-done.15.refs_6_.refs_2_, ...), custom_call_target="tpu_custom_call" | custom-call | flops 5000000000 | bytes 1000000 | tf_op jit(solution)/shard_map/coarse_kernel/pallas_call | solution.py:98
  70.4 1.8 %collective-permute-done.24.refs_1_ = bf16[4,464,128]{2,1,0:T(8,128)(2,1)S(1)} collective-permute-done((bf16[4,464,128]{2,1,0:T(8,128)(2,1)S(1)}, bf16[4,464,128]{2,1,0:T(8,128)(2,1)S(1)}, u32[]{:S(2)}, u32[]{:S(2)}) %collective-permute-start.24) | collective-permute-done | bytes 475168 | tf_op jit(solution)/shard_map/ppermute | solution.py:591
  72.2 1.4 %finish_kernel.1 = (bf16[3,3,48,48]{3,2,1,0:T(8,128)(2,1)}, bf16[3,3,96,96]{3,2,1,0:T(8,128)(2,1)}, bf16[3,3,192,192]{3,2,1,0:T(8,128)(2,1)}) custom-call(bf16[4,464,128]{2,1,0:T(8,128)(2,1)S(1)} %stack_kernel.3.refs_0_, bf16[4,464,128]{2,1,0:T(8,128)(2,1)S(1)} %collective-permute-done.24.refs_1_), custom_call_target="tpu_custom_call" | custom-call | flops 4000000000 | bytes 1000000 | tf_op jit(solution)/shard_map/finish_kernel/pallas_call | solution.py:98
  (92 shorter events, 7.2 us)
Async XLA Ops:
  7.6 1.8 %collective-permute-start = (bf16[2,144,384]{2,1,0:T(8,128)(2,1)}, bf16[2,144,384]{2,1,0:T(8,128)(2,1)S(1)}, u32[]{:S(2)}, u32[]{:S(2)}) collective-permute-start(bf16[2,144,384]{2,1,0:T(8,128)(2,1)} %get-tuple-element.57), channel_id=1, source_target_pairs={{0,1},{1,0},{2,3},{3,2},{4,5},{5,4},{6,7},{7,6},{8,9},{9,8},{10,11... | collective-permute-start | bytes 663560 | tf_op jit(solution)/shard_map/ppermute | solution.py:591
  11.0 5.0 %collective-permute-start.2 = (bf16[2,32,384]{2,1,0:T(8,128)(2,1)S(1)}, bf16[2,32,384]{2,1,0:T(8,128)(2,1)S(1)}, u32[]{:S(2)}, u32[]{:S(2)}) collective-permute-start(bf16[2,32,384]{2,1,0:T(8,128)(2,1)S(1)} %get-tuple-element.61), channel_id=1, source_target_pairs={{0,8},{8,0},{16,24},{24,16},{1,9},{9,1},{17,25},{25,17},{2,10},{10... | collective-permute-start | bytes 147464 | tf_op jit(solution)/shard_map/ppermute | solution.py:613
  13.9 2.1 %collective-permute-start.3 = (bf16[2,32,384]{2,1,0:T(8,128)(2,1)S(1)}, bf16[2,32,384]{2,1,0:T(8,128)(2,1)S(1)}, u32[]{:S(2)}, u32[]{:S(2)}) collective-permute-start(bf16[2,32,384]{2,1,0:T(8,128)(2,1)S(1)} %get-tuple-element.62), channel_id=1, source_target_pairs={{8,16},{16,8},{9,17},{17,9},{10,18},{18,10},{11,19},{19,11},{12,20... | collective-permute-start | bytes 147464 | tf_op jit(solution)/shard_map/ppermute | solution.py:612
  18.1 6.9 %collective-permute-start.4 = (bf16[1856,128]{1,0:T(8,128)(2,1)S(1)}, bf16[1856,128]{1,0:T(8,128)(2,1)S(1)}, u32[]{:S(2)}, u32[]{:S(2)}) collective-permute-start(bf16[1856,128]{1,0:T(8,128)(2,1)S(1)} %get-tuple-element.67), channel_id=1, source_target_pairs={{0,1},{1,0},{2,3},{3,2},{4,5},{5,4},{6,7},{7,6},{8,9},{9,8},{10,11... | collective-permute-start | bytes 1425416 | tf_op jit(solution)/shard_map/ppermute | solution.py:591
  25.2 12.6 %collective-permute-start.10 = (bf16[2,32,384]{2,1,0:T(8,128)(2,1)S(1)}, bf16[2,32,384]{2,1,0:T(8,128)(2,1)S(1)}, u32[]{:S(2)}, u32[]{:S(2)}) collective-permute-start(bf16[2,32,384]{2,1,0:T(8,128)(2,1)S(1)} %get-tuple-element.79.refs_0_), channel_id=1, source_target_pairs={{6,0},{7,1},{0,2},{1,3},{2,4},{3,5},{4,6},{5,7},{14,8},{15,9},{8,1... | collective-permute-start | bytes 147464 | tf_op jit(solution)/shard_map/ppermute | solution.py:636
  28.2 15.8 %collective-permute-start.9 = (bf16[2,32,384]{2,1,0:T(8,128)(2,1)S(1)}, bf16[2,32,384]{2,1,0:T(8,128)(2,1)S(1)}, u32[]{:S(2)}, u32[]{:S(2)}) collective-permute-start(bf16[2,32,384]{2,1,0:T(8,128)(2,1)S(1)} %get-tuple-element.79.refs_0_), channel_id=1, source_target_pairs={{4,0},{5,1},{6,2},{7,3},{0,4},{1,5},{2,6},{3,7},{12,8},{13,9},{14,... | collective-permute-start | bytes 147464 | tf_op jit(solution)/shard_map/ppermute | solution.py:636
  30.7 13.3 %collective-permute-start.8 = (bf16[2,32,384]{2,1,0:T(8,128)(2,1)S(1)}, bf16[2,32,384]{2,1,0:T(8,128)(2,1)S(1)}, u32[]{:S(2)}, u32[]{:S(2)}) collective-permute-start(bf16[2,32,384]{2,1,0:T(8,128)(2,1)S(1)} %get-tuple-element.79.refs_0_), channel_id=1, source_target_pairs={{2,0},{3,1},{4,2},{5,3},{6,4},{7,5},{0,6},{1,7},{10,8},{11,9},{12,... | collective-permute-start | bytes 147464 | tf_op jit(solution)/shard_map/ppermute | solution.py:636
  32.1 11.9 %collective-permute-start.5 = (bf16[464,128]{1,0:T(8,128)(2,1)S(1)}, bf16[464,128]{1,0:T(8,128)(2,1)S(1)}, u32[]{:S(2)}, u32[]{:S(2)}) collective-permute-start(bf16[464,128]{1,0:T(8,128)(2,1)S(1)} %get-tuple-element.70), channel_id=1, source_target_pairs={{0,8},{8,16},{16,24},{24,0},{1,9},{9,17},{17,25},{25,1},{2,10},{10... | collective-permute-start | bytes 356360 | tf_op jit(solution)/shard_map/ppermute | solution.py:635
  36.9 7.2 %collective-permute-start.6 = (bf16[464,128]{1,0:T(8,128)(2,1)S(1)}, bf16[464,128]{1,0:T(8,128)(2,1)S(1)}, u32[]{:S(2)}, u32[]{:S(2)}) collective-permute-start(bf16[464,128]{1,0:T(8,128)(2,1)S(1)} %get-tuple-element.71), channel_id=1, source_target_pairs={{0,16},{8,24},{16,0},{24,8},{1,17},{9,25},{17,1},{25,9},{2,18},{10... | collective-permute-start | bytes 356360 | tf_op jit(solution)/shard_map/ppermute | solution.py:635
  37.9 6.5 %collective-permute-start.7 = (bf16[464,128]{1,0:T(8,128)(2,1)S(1)}, bf16[464,128]{1,0:T(8,128)(2,1)S(1)}, u32[]{:S(2)}, u32[]{:S(2)}) collective-permute-start(bf16[464,128]{1,0:T(8,128)(2,1)S(1)} %get-tuple-element.72), channel_id=1, source_target_pairs={{0,24},{8,0},{16,8},{24,16},{1,25},{9,1},{17,9},{25,17},{2,26},{10... | collective-permute-start | bytes 356360 | tf_op jit(solution)/shard_map/ppermute | solution.py:635
  44.5 7.9 %collective-permute-start.13 = (bf16[464,128]{1,0:T(8,128)(2,1)S(1)}, bf16[464,128]{1,0:T(8,128)(2,1)S(1)}, u32[]{:S(2)}, u32[]{:S(2)}) collective-permute-start(bf16[464,128]{1,0:T(8,128)(2,1)S(1)} %sum_kernel.1.refs_20_.refs_4_.refs_0_), channel_id=1, source_target_pairs={{6,0},{7,1},{0,2},{1,3},{2,4},{3,5},{4,6},{5,7},{14,8},{15,9},{8,1... | collective-permute-start | bytes 356360 | tf_op jit(solution)/shard_map/ppermute | solution.py:647
  45.2 14.9 %collective-permute-start.12 = (bf16[464,128]{1,0:T(8,128)(2,1)S(1)}, bf16[464,128]{1,0:T(8,128)(2,1)S(1)}, u32[]{:S(2)}, u32[]{:S(2)}) collective-permute-start(bf16[464,128]{1,0:T(8,128)(2,1)S(1)} %sum_kernel.1.refs_20_.refs_4_.refs_0_), channel_id=1, source_target_pairs={{4,0},{5,1},{6,2},{7,3},{0,4},{1,5},{2,6},{3,7},{12,8},{13,9},{14,... | collective-permute-start | bytes 356360 | tf_op jit(solution)/shard_map/ppermute | solution.py:647
  45.6 15.7 %collective-permute-start.11 = (bf16[464,128]{1,0:T(8,128)(2,1)S(1)}, bf16[464,128]{1,0:T(8,128)(2,1)S(1)}, u32[]{:S(2)}, u32[]{:S(2)}) collective-permute-start(bf16[464,128]{1,0:T(8,128)(2,1)S(1)} %sum_kernel.1.refs_20_.refs_4_.refs_0_), channel_id=1, source_target_pairs={{2,0},{3,1},{4,2},{5,3},{6,4},{7,5},{0,6},{1,7},{10,8},{11,9},{12,... | collective-permute-start | bytes 356360 | tf_op jit(solution)/shard_map/ppermute | solution.py:647
  48.4 11.8 %collective-permute-start.16 = (bf16[4,2,32,384]{3,2,1,0:T(8,128)(2,1)S(1)}, bf16[4,2,32,384]{3,2,1,0:T(8,128)(2,1)S(1)}, u32[]{:S(2)}, u32[]{:S(2)}) collective-permute-start(bf16[4,2,32,384]{3,2,1,0:T(8,128)(2,1)S(1)} %stack_kernel.2.refs_0_), channel_id=1, source_target_pairs={{24,0},{0,8},{8,16},{16,24},{25,1},{1,9},{9,17},{17,25},{26,2},{2,... | collective-permute-start | bytes 589832 | tf_op jit(solution)/shard_map/ppermute | solution.py:652
  50.2 10.6 %collective-permute-start.15 = (bf16[4,2,32,384]{3,2,1,0:T(8,128)(2,1)S(1)}, bf16[4,2,32,384]{3,2,1,0:T(8,128)(2,1)S(1)}, u32[]{:S(2)}, u32[]{:S(2)}) collective-permute-start(bf16[4,2,32,384]{3,2,1,0:T(8,128)(2,1)S(1)} %stack_kernel.2.refs_0_), channel_id=1, source_target_pairs={{16,0},{24,8},{0,16},{8,24},{17,1},{25,9},{1,17},{9,25},{18,2},{26... | collective-permute-start | bytes 589832 | tf_op jit(solution)/shard_map/ppermute | solution.py:652
  52.4 8.4 %collective-permute-start.14 = (bf16[4,2,32,384]{3,2,1,0:T(8,128)(2,1)S(1)}, bf16[4,2,32,384]{3,2,1,0:T(8,128)(2,1)S(1)}, u32[]{:S(2)}, u32[]{:S(2)}) collective-permute-start(bf16[4,2,32,384]{3,2,1,0:T(8,128)(2,1)S(1)} %stack_kernel.2.refs_0_), channel_id=1, source_target_pairs={{8,0},{16,8},{24,16},{0,24},{9,1},{17,9},{25,17},{1,25},{10,2},{18... | collective-permute-start | bytes 589832 | tf_op jit(solution)/shard_map/ppermute | solution.py:652
  60.1 1.6 %collective-permute-start.20 = (bf16[4,2,32,384]{3,2,1,0:T(8,128)(2,1)S(1)}, bf16[4,2,32,384]{3,2,1,0:T(8,128)(2,1)S(1)}, u32[]{:S(2)}, u32[]{:S(2)}) collective-permute-start(bf16[4,2,32,384]{3,2,1,0:T(8,128)(2,1)S(1)} %stack_kernel.2.refs_0_), channel_id=1, source_target_pairs={{0,1},{1,0},{2,3},{3,2},{4,5},{5,4},{6,7},{7,6},{8,9},{9,8},{10,11... | collective-permute-start | bytes 589832 | tf_op jit(solution)/shard_map/ppermute | solution.py:591
  60.2 2.0 %collective-permute-start.23 = (bf16[4,2,32,384]{3,2,1,0:T(8,128)(2,1)S(1)}, bf16[4,2,32,384]{3,2,1,0:T(8,128)(2,1)S(1)}, u32[]{:S(2)}, u32[]{:S(2)}) collective-permute-start(bf16[4,2,32,384]{3,2,1,0:T(8,128)(2,1)S(1)} %collective-permute-done.16.refs_7_.refs_3_), channel_id=1, source_target_pairs={{0,1},{1,0},{2,3},{3,2},{4,5},{5,4},{6,7},{7,6},{8,9},{9,8},{10,11... | collective-permute-start | bytes 589832 | tf_op jit(solution)/shard_map/ppermute | solution.py:591
  60.7 4.3 %collective-permute-start.22 = (bf16[4,2,32,384]{3,2,1,0:T(8,128)(2,1)S(1)}, bf16[4,2,32,384]{3,2,1,0:T(8,128)(2,1)S(1)}, u32[]{:S(2)}, u32[]{:S(2)}) collective-permute-start(bf16[4,2,32,384]{3,2,1,0:T(8,128)(2,1)S(1)} %collective-permute-done.15.refs_6_.refs_2_), channel_id=1, source_target_pairs={{0,1},{1,0},{2,3},{3,2},{4,5},{5,4},{6,7},{7,6},{8,9},{9,8},{10,11... | collective-permute-start | bytes 589832 | tf_op jit(solution)/shard_map/ppermute | solution.py:591
  60.8 4.2 %collective-permute-start.21 = (bf16[4,2,32,384]{3,2,1,0:T(8,128)(2,1)S(1)}, bf16[4,2,32,384]{3,2,1,0:T(8,128)(2,1)S(1)}, u32[]{:S(2)}, u32[]{:S(2)}) collective-permute-start(bf16[4,2,32,384]{3,2,1,0:T(8,128)(2,1)S(1)} %collective-permute-done.14.refs_5_.refs_1_), channel_id=1, source_target_pairs={{0,1},{1,0},{2,3},{3,2},{4,5},{5,4},{6,7},{7,6},{8,9},{9,8},{10,11... | collective-permute-start | bytes 589832 | tf_op jit(solution)/shard_map/ppermute | solution.py:591
  61.4 8.8 %collective-permute-start.19 = (bf16[464,128]{1,0:T(8,128)(2,1)S(1)}, bf16[464,128]{1,0:T(8,128)(2,1)S(1)}, u32[]{:S(2)}, u32[]{:S(2)}) collective-permute-start(bf16[464,128]{1,0:T(8,128)(2,1)S(1)} %ordered_sum_kernel.1.refs_8_.refs_0_), channel_id=1, source_target_pairs={{24,0},{0,8},{8,16},{16,24},{25,1},{1,9},{9,17},{17,25},{26,2},{2,... | collective-permute-start | bytes 356360 | tf_op jit(solution)/shard_map/ppermute | solution.py:664
  61.7 8.5 %collective-permute-start.18 = (bf16[464,128]{1,0:T(8,128)(2,1)S(1)}, bf16[464,128]{1,0:T(8,128)(2,1)S(1)}, u32[]{:S(2)}, u32[]{:S(2)}) collective-permute-start(bf16[464,128]{1,0:T(8,128)(2,1)S(1)} %ordered_sum_kernel.1.refs_8_.refs_0_), channel_id=1, source_target_pairs={{16,0},{24,8},{0,16},{8,24},{17,1},{25,9},{1,17},{9,25},{18,2},{26... | collective-permute-start | bytes 356360 | tf_op jit(solution)/shard_map/ppermute | solution.py:664
  62.2 8.0 %collective-permute-start.17 = (bf16[464,128]{1,0:T(8,128)(2,1)S(1)}, bf16[464,128]{1,0:T(8,128)(2,1)S(1)}, u32[]{:S(2)}, u32[]{:S(2)}) collective-permute-start(bf16[464,128]{1,0:T(8,128)(2,1)S(1)} %ordered_sum_kernel.1.refs_8_.refs_0_), channel_id=1, source_target_pairs={{8,0},{16,8},{24,16},{0,24},{9,1},{17,9},{25,17},{1,25},{10,2},{18... | collective-permute-start | bytes 356360 | tf_op jit(solution)/shard_map/ppermute | solution.py:664
  70.3 1.9 %collective-permute-start.24 = (bf16[4,464,128]{2,1,0:T(8,128)(2,1)S(1)}, bf16[4,464,128]{2,1,0:T(8,128)(2,1)S(1)}, u32[]{:S(2)}, u32[]{:S(2)}) collective-permute-start(bf16[4,464,128]{2,1,0:T(8,128)(2,1)S(1)} %stack_kernel.3.refs_0_), channel_id=1, source_target_pairs={{0,1},{1,0},{2,3},{3,2},{4,5},{5,4},{6,7},{7,6},{8,9},{9,8},{10,11... | collective-permute-start | bytes 1425416 | tf_op jit(solution)/shard_map/ppermute | solution.py:591
  (28 other events, 277.9 us)

commit v5 on v4

--- a/solution.py
+++ b/solution.py
@@ -173,10 +173,9 @@
     heights, widths, channels = dims
     d_refs, f_refs, g_refs, x_refs = refs[0:4], refs[4:8], refs[8:12], refs[12:16]
     xt, up_refs, sc_refs = refs[16:20], refs[20:24], refs[24:28]
-    inner, outer, left, right, coarse, ends = refs[28:34]
-    edges = [ends.at[0], ends.at[1], left, right]
-    left[...] = jnp.zeros(left.shape, F32).astype(BF)
-    right[...] = jnp.zeros(right.shape, F32).astype(BF)
+    inner, outer, sides, coarse, ends = refs[28:33]
+    edges = [ends.at[0], ends.at[1], sides.ref.at[0], sides.ref.at[1]]
+    sides[...] = jnp.zeros(sides.shape, F32).astype(BF)
     ends[:, :, 128:, :] = jnp.zeros((2, 2, 16, PACK), F32).astype(BF)
     dt = []
     for b in range(4):
@@ -390,13 +389,13 @@
         refs[-1][k] = refs[k][...]
 
 
-def corner_kernel(idx, left, right, in_row, out_row, inner, outer):
+def corner_kernel(idx, sides, in_row, out_row, inner, outer):
     core, band = idx[0], idx[1] % 2
     cols = []
-    for side, at in ((left, 128), (right, 136)):
+    for k, at in ((0, 128), (1, 136)):
         in_part, out_part = in_row[:, at : at + 8, :], out_row[:, at : at + 8, :]
         above, below = pick(core, out_part, in_part), pick(core, in_part, out_part)
-        cols.append(jnp.concatenate([side[...].astype(F32), above, below], axis=1))
+        cols.append(jnp.concatenate([sides[k].astype(F32), above, below], axis=1))
     inner[...] = pick(band, cols[1], cols[0]).astype(BF)
     outer[...] = pick(band, cols[0], cols[1]).astype(BF)
 
@@ -595,18 +594,18 @@
 
     outs = call(
         functools.partial(upstream_kernel, dims),
-        kept * 3 + [sds((2, 144, PACK), BF)] * 2 + [sds((2, 16, PACK), BF)] * 2
+        kept * 3 + [sds((2, 144, PACK), BF)] * 2 + [sds((2, 2, 16, PACK), BF)]
         + [sds((2, heights[3] * widths[3], channels[3]), BF)],
         ds + fs + gs + xs,
         [pltpu.VMEM((2, 2, 144, PACK), BF)],
-        placed=True, far=range(16), far_out=range(17), limit=WHOLE, flops=6 * 10**9,
+        placed=True, far=range(16), far_out=range(16), limit=WHOLE, flops=6 * 10**9,
     )
     xt, ups, scs = outs[:4], outs[4:8], outs[8:12]
-    inner, outer, left, right, coarse = outs[12:]
+    inner, outer, sides, coarse = outs[12:]
     out_row = lax.ppermute(outer, "rows", hop(n_rows))
     in_row = core_swap(inner)
     inner, outer = call(
-        corner_kernel, [sds((2, 32, PACK), BF)] * 2, [left, right, in_row, out_row],
+        corner_kernel, [sds((2, 32, PACK), BF)] * 2, [sides, in_row, out_row],
         placed=True, flops=6 * 10**9,
     )
     out_col = lax.ppermute(outer, "branch", hop(n_branch))

time: 74 us -> 73.3 us (level)
    unnamed x54 -> x52, local copies, waits for them, and re-layouts: 1.61 us -> 0.94 us
where the time goes in v5:
time: 73.3 us; the launch traced here: 73.1 us
  starting transfers between devices  38.9 us (53%)
  Pallas kernels  25.1 us (34%)
  waiting for transfers between devices  6.81 us (9%)
  between operations  1.29 us (2%)
  local copies, waits for them, and re-layouts  0.94 us (1%)
    pallas_call x12, Pallas kernels, call(): pl.pallas_call(wrapped, name=getattr(body, 'func', body).__name__, out_sh...  25.1 us
    ppermute x3, starting transfers between devices, local(): lax.ppermute(parts[k], 'branch', to_branch(k))  8.67 us
    ppermute x7, starting transfers between devices, local(): core_swap = lambda a: lax.ppermute(a, 'rows', swap(n_rows))  7.15 us
    ppermute x3, starting transfers between devices, local(): lax.ppermute(coarse, 'rows', from_chip(k))  6.88 us
    ppermute x3, starting transfers between devices, local(): lax.ppermute(held, 'branch', from_branch(k))  4.57 us
    ppermute x7, waiting for transfers between devices, local(): core_swap = lambda a: lax.ppermute(a, 'rows', swap(n_rows))  3.95 us
    ppermute x3, starting transfers between devices, local(): lax.ppermute(part_sum, 'rows', from_chip(k))  3.88 us
    ppermute x3, starting transfers between devices, local(): lax.ppermute(total, 'branch', from_branch(k))  3.57 us
  transfers between devices with their start and end apart: 25, of which 6 were waited for; matrix products, arithmetic and copies ran while one was open for 0% of the time, Pallas kernels for 20%

profile of v5, /device:TPU:0, one launch (start us, length us, event | category | flops | bytes accessed | tf_op | source)
XLA Modules:
  0.0 73.1 jit_solution(4504520811574416665)
XLA Ops:
  0.6 6.9 %upstream_kernel.1 = (bf16[8,128,128]{2,1,0:T(8,128)(2,1)}, bf16[4,128,96]{2,1,0:T(8,128)(2,1)}, bf16[2,64,192]{2,1,0:T(8,128)(2,1)}, bf16[1,32,384]{2,1,0:T(8,1...) custom-call(bf16[48,8,256]{2,1,0:T(8,128)(2,1)} %refs_0_.1, ...), custom_call_target="tpu_custom_call" | custom-call | flops 6000000000 | bytes 1000000 | tf_op jit(solution)/shard_map/upstream_kernel/pallas_call | solution.py:98
  9.4 0.8 %copy-done.25 = bf16[2,2,16,384]{3,2,1,0:T(8,128)(2,1)S(1)} copy-done((bf16[2,2,16,384]{3,2,1,0:T(8,128)(2,1)S(1)}, bf16[2,2,16,384]{3,2,1,0:T(8,128)(2,1)}, u32[]{:S(2)}) %copy-start.25) | copy-done | bytes 49176
  10.3 2.9 %collective-permute-start.2 = (bf16[2,32,384]{2,1,0:T(8,128)(2,1)S(1)}, bf16[2,32,384]{2,1,0:T(8,128)(2,1)S(1)}, u32[]{:S(2)}, u32[]{:S(2)}) collective-permute-start(bf16[2,32,384]{2,1,0:T(8,128)(2,1)S(1)} %get-tuple-element.59), channel_id=1, source_target_pairs={{0,8},{8,0},{16,24},{24,16},{1,9},{9,1},{17,25},{25,17},{2,10},{10... | collective-permute-start | bytes 147464 | tf_op jit(solution)/shard_map/ppermute | solution.py:612
  13.9 1.4 %collective-permute-done.2.refs_8_.refs_18_ = bf16[2,32,384]{2,1,0:T(8,128)(2,1)S(1)} collective-permute-done((bf16[2,32,384]{2,1,0:T(8,128)(2,1)S(1)}, bf16[2,32,384]{2,1,0:T(8,128)(2,1)S(1)}, u32[]{:S(2)}, u32[]{:S(2)}) %collective-permute-start.2) | collective-permute-done | bytes 49184 | tf_op jit(solution)/shard_map/ppermute | solution.py:612
  15.3 2.0 %weight_grads_kernel.1 = (bf16[1856,128]{1,0:T(8,128)(2,1)S(1)}, bf16[1856,128]{1,0:T(8,128)(2,1)S(1)}) custom-call(bf16[8,128,128]{2,1,0:T(8,128)(2,1)S(1)} %copy-done.12, bf16[4,128,96]{2,1,0:T(8,128)(2,1)S(1)} %copy-done.15, bf16[2,64,192]{2,1,0:T(8,128)(2,1)S(1)} %copy-done.18, bf16[8,128,128]{2,1,0:T(8,128)(2,1)S(1)} %copy-done.14, ...), custom_call_target="tpu_custom_call" | custom-call | flops 6000000000 | bytes 1000000 | tf_op jit(solution)/shard_map/weight_grads_kernel/pallas_call | solution.py:98
  17.4 5.5 %collective-permute-start.4 = (bf16[1856,128]{1,0:T(8,128)(2,1)S(1)}, bf16[1856,128]{1,0:T(8,128)(2,1)S(1)}, u32[]{:S(2)}, u32[]{:S(2)}) collective-permute-start(bf16[1856,128]{1,0:T(8,128)(2,1)S(1)} %get-tuple-element.65), channel_id=1, source_target_pairs={{0,1},{1,0},{2,3},{3,2},{4,5},{5,4},{6,7},{7,6},{8,9},{9,8},{10,11... | collective-permute-start | bytes 1425416 | tf_op jit(solution)/shard_map/ppermute | solution.py:590
  22.8 1.5 %collective-permute-done.4.refs_1_ = bf16[1856,128]{1,0:T(8,128)(2,1)S(1)} collective-permute-done((bf16[1856,128]{1,0:T(8,128)(2,1)S(1)}, bf16[1856,128]{1,0:T(8,128)(2,1)S(1)}, u32[]{:S(2)}, u32[]{:S(2)}) %collective-permute-start.4) | collective-permute-done | bytes 475168 | tf_op jit(solution)/shard_map/ppermute | solution.py:590
  24.5 2.9 %collective-permute-start.10 = (bf16[2,32,384]{2,1,0:T(8,128)(2,1)S(1)}, bf16[2,32,384]{2,1,0:T(8,128)(2,1)S(1)}, u32[]{:S(2)}, u32[]{:S(2)}) collective-permute-start(bf16[2,32,384]{2,1,0:T(8,128)(2,1)S(1)} %get-tuple-element.77.refs_0_), channel_id=1, source_target_pairs={{6,0},{7,1},{0,2},{1,3},{2,4},{3,5},{4,6},{5,7},{14,8},{15,9},{8,1... | collective-permute-start | bytes 147464 | tf_op jit(solution)/shard_map/ppermute | solution.py:635
  27.5 2.5 %collective-permute-start.9 = (bf16[2,32,384]{2,1,0:T(8,128)(2,1)S(1)}, bf16[2,32,384]{2,1,0:T(8,128)(2,1)S(1)}, u32[]{:S(2)}, u32[]{:S(2)}) collective-permute-start(bf16[2,32,384]{2,1,0:T(8,128)(2,1)S(1)} %get-tuple-element.77.refs_0_), channel_id=1, source_target_pairs={{4,0},{5,1},{6,2},{7,3},{0,4},{1,5},{2,6},{3,7},{12,8},{13,9},{14,... | collective-permute-start | bytes 147464 | tf_op jit(solution)/shard_map/ppermute | solution.py:635
  30.0 1.4 %collective-permute-start.8 = (bf16[2,32,384]{2,1,0:T(8,128)(2,1)S(1)}, bf16[2,32,384]{2,1,0:T(8,128)(2,1)S(1)}, u32[]{:S(2)}, u32[]{:S(2)}) collective-permute-start(bf16[2,32,384]{2,1,0:T(8,128)(2,1)S(1)} %get-tuple-element.77.refs_0_), channel_id=1, source_target_pairs={{2,0},{3,1},{4,2},{5,3},{6,4},{7,5},{0,6},{1,7},{10,8},{11,9},{12,... | collective-permute-start | bytes 147464 | tf_op jit(solution)/shard_map/ppermute | solution.py:635
  31.4 4.8 %collective-permute-start.5 = (bf16[464,128]{1,0:T(8,128)(2,1)S(1)}, bf16[464,128]{1,0:T(8,128)(2,1)S(1)}, u32[]{:S(2)}, u32[]{:S(2)}) collective-permute-start(bf16[464,128]{1,0:T(8,128)(2,1)S(1)} %get-tuple-element.68), channel_id=1, source_target_pairs={{0,8},{8,16},{16,24},{24,0},{1,9},{9,17},{17,25},{25,1},{2,10},{10... | collective-permute-start | bytes 356360 | tf_op jit(solution)/shard_map/ppermute | solution.py:634
  36.2 1.0 %collective-permute-start.6 = (bf16[464,128]{1,0:T(8,128)(2,1)S(1)}, bf16[464,128]{1,0:T(8,128)(2,1)S(1)}, u32[]{:S(2)}, u32[]{:S(2)}) collective-permute-start(bf16[464,128]{1,0:T(8,128)(2,1)S(1)} %get-tuple-element.69), channel_id=1, source_target_pairs={{0,16},{8,24},{16,0},{24,8},{1,17},{9,25},{17,1},{25,9},{2,18},{10... | collective-permute-start | bytes 356360 | tf_op jit(solution)/shard_map/ppermute | solution.py:634
  37.2 2.9 %collective-permute-start.7 = (bf16[464,128]{1,0:T(8,128)(2,1)S(1)}, bf16[464,128]{1,0:T(8,128)(2,1)S(1)}, u32[]{:S(2)}, u32[]{:S(2)}) collective-permute-start(bf16[464,128]{1,0:T(8,128)(2,1)S(1)} %get-tuple-element.70), channel_id=1, source_target_pairs={{0,24},{8,0},{16,8},{24,16},{1,25},{9,1},{17,9},{25,17},{2,26},{10... | collective-permute-start | bytes 356360 | tf_op jit(solution)/shard_map/ppermute | solution.py:634
  40.2 3.2 %adjoint_kernel.1 = (bf16[48,8,256]{2,1,0:T(8,128)(2,1)}, bf16[96,4,128]{2,1,0:T(4,128)(2,1)}, bf16[2,64,192]{2,1,0:T(8,128)(2,1)}, bf16[1,32,384]{2,1,0:T(8,128)(2,1)}, f32[8,128]{1,0:T(8,128)S(1)}) custom-call(bf16[8,128,128]{2,1,0:T(8,128)(2,1)S(1)} %copy-done.12, bf16[4,128,96]{2,1,0:T(8,128)(2,1)S(1)} %copy-done.15, bf16[2,64,192]{2,1,0:T(8,128)(2,1)S(1)} %copy-done.18, ...), custom_call_target="tpu_custom_call" | custom-call | flops 3000000000 | bytes 1000000 | tf_op jit(solution)/shard_map/adjoint_kernel/pallas_call | solution.py:98
  44.9 2.8 %collective-permute-start.11 = (bf16[464,128]{1,0:T(8,128)(2,1)S(1)}, bf16[464,128]{1,0:T(8,128)(2,1)S(1)}, u32[]{:S(2)}, u32[]{:S(2)}) collective-permute-start(bf16[464,128]{1,0:T(8,128)(2,1)S(1)} %sum_kernel.1.refs_20_.refs_4_.refs_0_), channel_id=1, source_target_pairs={{2,0},{3,1},{4,2},{5,3},{6,4},{7,5},{0,6},{1,7},{10,8},{11,9},{12,... | collective-permute-start | bytes 356360 | tf_op jit(solution)/shard_map/ppermute | solution.py:646
  47.7 1.8 %collective-permute-start.16 = (bf16[4,2,32,384]{3,2,1,0:T(8,128)(2,1)S(1)}, bf16[4,2,32,384]{3,2,1,0:T(8,128)(2,1)S(1)}, u32[]{:S(2)}, u32[]{:S(2)}) collective-permute-start(bf16[4,2,32,384]{3,2,1,0:T(8,128)(2,1)S(1)} %stack_kernel.2.refs_0_), channel_id=1, source_target_pairs={{24,0},{0,8},{8,16},{16,24},{25,1},{1,9},{9,17},{17,25},{26,2},{2,... | collective-permute-start | bytes 589832 | tf_op jit(solution)/shard_map/ppermute | solution.py:651
  49.5 1.1 %collective-permute-start.15 = (bf16[4,2,32,384]{3,2,1,0:T(8,128)(2,1)S(1)}, bf16[4,2,32,384]{3,2,1,0:T(8,128)(2,1)S(1)}, u32[]{:S(2)}, u32[]{:S(2)}) collective-permute-start(bf16[4,2,32,384]{3,2,1,0:T(8,128)(2,1)S(1)} %stack_kernel.2.refs_0_), channel_id=1, source_target_pairs={{16,0},{24,8},{0,16},{8,24},{17,1},{25,9},{1,17},{9,25},{18,2},{26... | collective-permute-start | bytes 589832 | tf_op jit(solution)/shard_map/ppermute | solution.py:651
  50.5 1.2 %collective-permute-done.13.refs_3_ = bf16[464,128]{1,0:T(8,128)(2,1)S(1)} collective-permute-done((bf16[464,128]{1,0:T(8,128)(2,1)S(1)}, bf16[464,128]{1,0:T(8,128)(2,1)S(1)}, u32[]{:S(2)}, u32[]{:S(2)}) %collective-permute-start.13) | collective-permute-done | bytes 118816 | tf_op jit(solution)/shard_map/ppermute | solution.py:646
  51.7 1.7 %collective-permute-start.14 = (bf16[4,2,32,384]{3,2,1,0:T(8,128)(2,1)S(1)}, bf16[4,2,32,384]{3,2,1,0:T(8,128)(2,1)S(1)}, u32[]{:S(2)}, u32[]{:S(2)}) collective-permute-start(bf16[4,2,32,384]{3,2,1,0:T(8,128)(2,1)S(1)} %stack_kernel.2.refs_0_), channel_id=1, source_target_pairs={{8,0},{16,8},{24,16},{0,24},{9,1},{17,9},{25,17},{1,25},{10,2},{18... | collective-permute-start | bytes 589832 | tf_op jit(solution)/shard_map/ppermute | solution.py:651
  53.5 5.9 %forward_kernel.1 = (bf16[48,8,256]{2,1,0:T(8,128)(2,1)}, bf16[96,4,128]{2,1,0:T(4,128)(2,1)}, bf16[2,64,192]{2,1,0:T(8,128)(2,1)}, bf16[1,32,384]{2,1,0:T(8,128)(2,1)}, f32[8,128]{1,0:T(8,128)S(1)}) custom-call(bf16[8,128,128]{2,1,0:T(8,128)(2,1)S(1)} %copy-done.12, bf16[4,128,96]{2,1,0:T(8,128)(2,1)S(1)} %copy-done.15, bf16[2,64,192]{2,1,0:T(8,128)(2,1)S(1)} %copy-done.18, ...), custom_call_target="tpu_custom_call" | custom-call | flops 6000000000 | bytes 1000000 | tf_op jit(solution)/shard_map/forward_kernel/pallas_call | solution.py:98
  61.6 2.7 %collective-permute-start.17 = (bf16[464,128]{1,0:T(8,128)(2,1)S(1)}, bf16[464,128]{1,0:T(8,128)(2,1)S(1)}, u32[]{:S(2)}, u32[]{:S(2)}) collective-permute-start(bf16[464,128]{1,0:T(8,128)(2,1)S(1)} %ordered_sum_kernel.1.refs_8_.refs_0_), channel_id=1, source_target_pairs={{8,0},{16,8},{24,16},{0,24},{9,1},{17,9},{25,17},{1,25},{10,2},{18... | collective-permute-start | bytes 356360 | tf_op jit(solution)/shard_map/ppermute | solution.py:663
  64.3 5.2 %coarse_kernel.1 = (bf16[3,3,384,384]{3,2,1,0:T(8,128)(2,1)}, f32[8,128]{1,0:T(8,128)S(1)}) custom-call(bf16[4,2,32,384]{3,2,1,0:T(8,128)(2,1)S(1)} %stack_kernel.2.refs_0_, bf16[4,2,32,384]{3,2,1,0:T(8,128)(2,1)S(1)} %collective-permute-done.14.refs_5_.refs_1_, bf16[4,2,32,384]{3,2,1,0:T(8,128)(2,1)S(1)} %collective-permute-done.15.refs_6_.refs_2_, ...), custom_call_target="tpu_custom_call" | custom-call | flops 5000000000 | bytes 1000000 | tf_op jit(solution)/shard_map/coarse_kernel/pallas_call | solution.py:98
  69.7 1.8 %collective-permute-done.24.refs_1_ = bf16[4,464,128]{2,1,0:T(8,128)(2,1)S(1)} collective-permute-done((bf16[4,464,128]{2,1,0:T(8,128)(2,1)S(1)}, bf16[4,464,128]{2,1,0:T(8,128)(2,1)S(1)}, u32[]{:S(2)}, u32[]{:S(2)}) %collective-permute-start.24) | collective-permute-done | bytes 475168 | tf_op jit(solution)/shard_map/ppermute | solution.py:590
  71.5 1.4 %finish_kernel.1 = (bf16[3,3,48,48]{3,2,1,0:T(8,128)(2,1)}, bf16[3,3,96,96]{3,2,1,0:T(8,128)(2,1)}, bf16[3,3,192,192]{3,2,1,0:T(8,128)(2,1)}) custom-call(bf16[4,464,128]{2,1,0:T(8,128)(2,1)S(1)} %stack_kernel.3.refs_0_, bf16[4,464,128]{2,1,0:T(8,128)(2,1)S(1)} %collective-permute-done.24.refs_1_), custom_call_target="tpu_custom_call" | custom-call | flops 4000000000 | bytes 1000000 | tf_op jit(solution)/shard_map/finish_kernel/pallas_call | solution.py:98
  (90 shorter events, 6.5 us)
Async XLA Ops:
  7.6 1.8 %collective-permute-start = (bf16[2,144,384]{2,1,0:T(8,128)(2,1)}, bf16[2,144,384]{2,1,0:T(8,128)(2,1)S(1)}, u32[]{:S(2)}, u32[]{:S(2)}) collective-permute-start(bf16[2,144,384]{2,1,0:T(8,128)(2,1)} %get-tuple-element.56), channel_id=1, source_target_pairs={{0,1},{1,0},{2,3},{3,2},{4,5},{5,4},{6,7},{7,6},{8,9},{9,8},{10,11... | collective-permute-start | bytes 663560 | tf_op jit(solution)/shard_map/ppermute | solution.py:590
  10.3 5.0 %collective-permute-start.2 = (bf16[2,32,384]{2,1,0:T(8,128)(2,1)S(1)}, bf16[2,32,384]{2,1,0:T(8,128)(2,1)S(1)}, u32[]{:S(2)}, u32[]{:S(2)}) collective-permute-start(bf16[2,32,384]{2,1,0:T(8,128)(2,1)S(1)} %get-tuple-element.59), channel_id=1, source_target_pairs={{0,8},{8,0},{16,24},{24,16},{1,9},{9,1},{17,25},{25,17},{2,10},{10... | collective-permute-start | bytes 147464 | tf_op jit(solution)/shard_map/ppermute | solution.py:612
  13.2 2.1 %collective-permute-start.3 = (bf16[2,32,384]{2,1,0:T(8,128)(2,1)S(1)}, bf16[2,32,384]{2,1,0:T(8,128)(2,1)S(1)}, u32[]{:S(2)}, u32[]{:S(2)}) collective-permute-start(bf16[2,32,384]{2,1,0:T(8,128)(2,1)S(1)} %get-tuple-element.60), channel_id=1, source_target_pairs={{8,16},{16,8},{9,17},{17,9},{10,18},{18,10},{11,19},{19,11},{12,20... | collective-permute-start | bytes 147464 | tf_op jit(solution)/shard_map/ppermute | solution.py:611
  17.4 6.9 %collective-permute-start.4 = (bf16[1856,128]{1,0:T(8,128)(2,1)S(1)}, bf16[1856,128]{1,0:T(8,128)(2,1)S(1)}, u32[]{:S(2)}, u32[]{:S(2)}) collective-permute-start(bf16[1856,128]{1,0:T(8,128)(2,1)S(1)} %get-tuple-element.65), channel_id=1, source_target_pairs={{0,1},{1,0},{2,3},{3,2},{4,5},{5,4},{6,7},{7,6},{8,9},{9,8},{10,11... | collective-permute-start | bytes 1425416 | tf_op jit(solution)/shard_map/ppermute | solution.py:590
  24.5 12.6 %collective-permute-start.10 = (bf16[2,32,384]{2,1,0:T(8,128)(2,1)S(1)}, bf16[2,32,384]{2,1,0:T(8,128)(2,1)S(1)}, u32[]{:S(2)}, u32[]{:S(2)}) collective-permute-start(bf16[2,32,384]{2,1,0:T(8,128)(2,1)S(1)} %get-tuple-element.77.refs_0_), channel_id=1, source_target_pairs={{6,0},{7,1},{0,2},{1,3},{2,4},{3,5},{4,6},{5,7},{14,8},{15,9},{8,1... | collective-permute-start | bytes 147464 | tf_op jit(solution)/shard_map/ppermute | solution.py:635
  27.5 15.9 %collective-permute-start.9 = (bf16[2,32,384]{2,1,0:T(8,128)(2,1)S(1)}, bf16[2,32,384]{2,1,0:T(8,128)(2,1)S(1)}, u32[]{:S(2)}, u32[]{:S(2)}) collective-permute-start(bf16[2,32,384]{2,1,0:T(8,128)(2,1)S(1)} %get-tuple-element.77.refs_0_), channel_id=1, source_target_pairs={{4,0},{5,1},{6,2},{7,3},{0,4},{1,5},{2,6},{3,7},{12,8},{13,9},{14,... | collective-permute-start | bytes 147464 | tf_op jit(solution)/shard_map/ppermute | solution.py:635
  30.0 13.3 %collective-permute-start.8 = (bf16[2,32,384]{2,1,0:T(8,128)(2,1)S(1)}, bf16[2,32,384]{2,1,0:T(8,128)(2,1)S(1)}, u32[]{:S(2)}, u32[]{:S(2)}) collective-permute-start(bf16[2,32,384]{2,1,0:T(8,128)(2,1)S(1)} %get-tuple-element.77.refs_0_), channel_id=1, source_target_pairs={{2,0},{3,1},{4,2},{5,3},{6,4},{7,5},{0,6},{1,7},{10,8},{11,9},{12,... | collective-permute-start | bytes 147464 | tf_op jit(solution)/shard_map/ppermute | solution.py:635
  31.4 11.9 %collective-permute-start.5 = (bf16[464,128]{1,0:T(8,128)(2,1)S(1)}, bf16[464,128]{1,0:T(8,128)(2,1)S(1)}, u32[]{:S(2)}, u32[]{:S(2)}) collective-permute-start(bf16[464,128]{1,0:T(8,128)(2,1)S(1)} %get-tuple-element.68), channel_id=1, source_target_pairs={{0,8},{8,16},{16,24},{24,0},{1,9},{9,17},{17,25},{25,1},{2,10},{10... | collective-permute-start | bytes 356360 | tf_op jit(solution)/shard_map/ppermute | solution.py:634
  36.2 7.2 %collective-permute-start.6 = (bf16[464,128]{1,0:T(8,128)(2,1)S(1)}, bf16[464,128]{1,0:T(8,128)(2,1)S(1)}, u32[]{:S(2)}, u32[]{:S(2)}) collective-permute-start(bf16[464,128]{1,0:T(8,128)(2,1)S(1)} %get-tuple-element.69), channel_id=1, source_target_pairs={{0,16},{8,24},{16,0},{24,8},{1,17},{9,25},{17,1},{25,9},{2,18},{10... | collective-permute-start | bytes 356360 | tf_op jit(solution)/shard_map/ppermute | solution.py:634
  37.2 6.5 %collective-permute-start.7 = (bf16[464,128]{1,0:T(8,128)(2,1)S(1)}, bf16[464,128]{1,0:T(8,128)(2,1)S(1)}, u32[]{:S(2)}, u32[]{:S(2)}) collective-permute-start(bf16[464,128]{1,0:T(8,128)(2,1)S(1)} %get-tuple-element.70), channel_id=1, source_target_pairs={{0,24},{8,0},{16,8},{24,16},{1,25},{9,1},{17,9},{25,17},{2,26},{10... | collective-permute-start | bytes 356360 | tf_op jit(solution)/shard_map/ppermute | solution.py:634
  43.8 7.9 %collective-permute-start.13 = (bf16[464,128]{1,0:T(8,128)(2,1)S(1)}, bf16[464,128]{1,0:T(8,128)(2,1)S(1)}, u32[]{:S(2)}, u32[]{:S(2)}) collective-permute-start(bf16[464,128]{1,0:T(8,128)(2,1)S(1)} %sum_kernel.1.refs_20_.refs_4_.refs_0_), channel_id=1, source_target_pairs={{6,0},{7,1},{0,2},{1,3},{2,4},{3,5},{4,6},{5,7},{14,8},{15,9},{8,1... | collective-permute-start | bytes 356360 | tf_op jit(solution)/shard_map/ppermute | solution.py:646
  44.5 14.9 %collective-permute-start.12 = (bf16[464,128]{1,0:T(8,128)(2,1)S(1)}, bf16[464,128]{1,0:T(8,128)(2,1)S(1)}, u32[]{:S(2)}, u32[]{:S(2)}) collective-permute-start(bf16[464,128]{1,0:T(8,128)(2,1)S(1)} %sum_kernel.1.refs_20_.refs_4_.refs_0_), channel_id=1, source_target_pairs={{4,0},{5,1},{6,2},{7,3},{0,4},{1,5},{2,6},{3,7},{12,8},{13,9},{14,... | collective-permute-start | bytes 356360 | tf_op jit(solution)/shard_map/ppermute | solution.py:646
  44.9 15.7 %collective-permute-start.11 = (bf16[464,128]{1,0:T(8,128)(2,1)S(1)}, bf16[464,128]{1,0:T(8,128)(2,1)S(1)}, u32[]{:S(2)}, u32[]{:S(2)}) collective-permute-start(bf16[464,128]{1,0:T(8,128)(2,1)S(1)} %sum_kernel.1.refs_20_.refs_4_.refs_0_), channel_id=1, source_target_pairs={{2,0},{3,1},{4,2},{5,3},{6,4},{7,5},{0,6},{1,7},{10,8},{11,9},{12,... | collective-permute-start | bytes 356360 | tf_op jit(solution)/shard_map/ppermute | solution.py:646
  47.7 11.8 %collective-permute-start.16 = (bf16[4,2,32,384]{3,2,1,0:T(8,128)(2,1)S(1)}, bf16[4,2,32,384]{3,2,1,0:T(8,128)(2,1)S(1)}, u32[]{:S(2)}, u32[]{:S(2)}) collective-permute-start(bf16[4,2,32,384]{3,2,1,0:T(8,128)(2,1)S(1)} %stack_kernel.2.refs_0_), channel_id=1, source_target_pairs={{24,0},{0,8},{8,16},{16,24},{25,1},{1,9},{9,17},{17,25},{26,2},{2,... | collective-permute-start | bytes 589832 | tf_op jit(solution)/shard_map/ppermute | solution.py:651
  49.5 10.6 %collective-permute-start.15 = (bf16[4,2,32,384]{3,2,1,0:T(8,128)(2,1)S(1)}, bf16[4,2,32,384]{3,2,1,0:T(8,128)(2,1)S(1)}, u32[]{:S(2)}, u32[]{:S(2)}) collective-permute-start(bf16[4,2,32,384]{3,2,1,0:T(8,128)(2,1)S(1)} %stack_kernel.2.refs_0_), channel_id=1, source_target_pairs={{16,0},{24,8},{0,16},{8,24},{17,1},{25,9},{1,17},{9,25},{18,2},{26... | collective-permute-start | bytes 589832 | tf_op jit(solution)/shard_map/ppermute | solution.py:651
  51.7 8.4 %collective-permute-start.14 = (bf16[4,2,32,384]{3,2,1,0:T(8,128)(2,1)S(1)}, bf16[4,2,32,384]{3,2,1,0:T(8,128)(2,1)S(1)}, u32[]{:S(2)}, u32[]{:S(2)}) collective-permute-start(bf16[4,2,32,384]{3,2,1,0:T(8,128)(2,1)S(1)} %stack_kernel.2.refs_0_), channel_id=1, source_target_pairs={{8,0},{16,8},{24,16},{0,24},{9,1},{17,9},{25,17},{1,25},{10,2},{18... | collective-permute-start | bytes 589832 | tf_op jit(solution)/shard_map/ppermute | solution.py:651
  59.5 1.6 %collective-permute-start.20 = (bf16[4,2,32,384]{3,2,1,0:T(8,128)(2,1)S(1)}, bf16[4,2,32,384]{3,2,1,0:T(8,128)(2,1)S(1)}, u32[]{:S(2)}, u32[]{:S(2)}) collective-permute-start(bf16[4,2,32,384]{3,2,1,0:T(8,128)(2,1)S(1)} %stack_kernel.2.refs_0_), channel_id=1, source_target_pairs={{0,1},{1,0},{2,3},{3,2},{4,5},{5,4},{6,7},{7,6},{8,9},{9,8},{10,11... | collective-permute-start | bytes 589832 | tf_op jit(solution)/shard_map/ppermute | solution.py:590
  59.5 2.0 %collective-permute-start.23 = (bf16[4,2,32,384]{3,2,1,0:T(8,128)(2,1)S(1)}, bf16[4,2,32,384]{3,2,1,0:T(8,128)(2,1)S(1)}, u32[]{:S(2)}, u32[]{:S(2)}) collective-permute-start(bf16[4,2,32,384]{3,2,1,0:T(8,128)(2,1)S(1)} %collective-permute-done.16.refs_7_.refs_3_), channel_id=1, source_target_pairs={{0,1},{1,0},{2,3},{3,2},{4,5},{5,4},{6,7},{7,6},{8,9},{9,8},{10,11... | collective-permute-start | bytes 589832 | tf_op jit(solution)/shard_map/ppermute | solution.py:590
  60.0 4.3 %collective-permute-start.22 = (bf16[4,2,32,384]{3,2,1,0:T(8,128)(2,1)S(1)}, bf16[4,2,32,384]{3,2,1,0:T(8,128)(2,1)S(1)}, u32[]{:S(2)}, u32[]{:S(2)}) collective-permute-start(bf16[4,2,32,384]{3,2,1,0:T(8,128)(2,1)S(1)} %collective-permute-done.15.refs_6_.refs_2_), channel_id=1, source_target_pairs={{0,1},{1,0},{2,3},{3,2},{4,5},{5,4},{6,7},{7,6},{8,9},{9,8},{10,11... | collective-permute-start | bytes 589832 | tf_op jit(solution)/shard_map/ppermute | solution.py:590
  60.1 4.2 %collective-permute-start.21 = (bf16[4,2,32,384]{3,2,1,0:T(8,128)(2,1)S(1)}, bf16[4,2,32,384]{3,2,1,0:T(8,128)(2,1)S(1)}, u32[]{:S(2)}, u32[]{:S(2)}) collective-permute-start(bf16[4,2,32,384]{3,2,1,0:T(8,128)(2,1)S(1)} %collective-permute-done.14.refs_5_.refs_1_), channel_id=1, source_target_pairs={{0,1},{1,0},{2,3},{3,2},{4,5},{5,4},{6,7},{7,6},{8,9},{9,8},{10,11... | collective-permute-start | bytes 589832 | tf_op jit(solution)/shard_map/ppermute | solution.py:590
  60.7 8.8 %collective-permute-start.19 = (bf16[464,128]{1,0:T(8,128)(2,1)S(1)}, bf16[464,128]{1,0:T(8,128)(2,1)S(1)}, u32[]{:S(2)}, u32[]{:S(2)}) collective-permute-start(bf16[464,128]{1,0:T(8,128)(2,1)S(1)} %ordered_sum_kernel.1.refs_8_.refs_0_), channel_id=1, source_target_pairs={{24,0},{0,8},{8,16},{16,24},{25,1},{1,9},{9,17},{17,25},{26,2},{2,... | collective-permute-start | bytes 356360 | tf_op jit(solution)/shard_map/ppermute | solution.py:663
  61.0 8.5 %collective-permute-start.18 = (bf16[464,128]{1,0:T(8,128)(2,1)S(1)}, bf16[464,128]{1,0:T(8,128)(2,1)S(1)}, u32[]{:S(2)}, u32[]{:S(2)}) collective-permute-start(bf16[464,128]{1,0:T(8,128)(2,1)S(1)} %ordered_sum_kernel.1.refs_8_.refs_0_), channel_id=1, source_target_pairs={{16,0},{24,8},{0,16},{8,24},{17,1},{25,9},{1,17},{9,25},{18,2},{26... | collective-permute-start | bytes 356360 | tf_op jit(solution)/shard_map/ppermute | solution.py:663
  61.6 8.0 %collective-permute-start.17 = (bf16[464,128]{1,0:T(8,128)(2,1)S(1)}, bf16[464,128]{1,0:T(8,128)(2,1)S(1)}, u32[]{:S(2)}, u32[]{:S(2)}) collective-permute-start(bf16[464,128]{1,0:T(8,128)(2,1)S(1)} %ordered_sum_kernel.1.refs_8_.refs_0_), channel_id=1, source_target_pairs={{8,0},{16,8},{24,16},{0,24},{9,1},{17,9},{25,17},{1,25},{10,2},{18... | collective-permute-start | bytes 356360 | tf_op jit(solution)/shard_map/ppermute | solution.py:663
  69.6 1.9 %collective-permute-start.24 = (bf16[4,464,128]{2,1,0:T(8,128)(2,1)S(1)}, bf16[4,464,128]{2,1,0:T(8,128)(2,1)S(1)}, u32[]{:S(2)}, u32[]{:S(2)}) collective-permute-start(bf16[4,464,128]{2,1,0:T(8,128)(2,1)S(1)} %stack_kernel.3.refs_0_), channel_id=1, source_target_pairs={{0,1},{1,0},{2,3},{3,2},{4,5},{5,4},{6,7},{7,6},{8,9},{9,8},{10,11... | collective-permute-start | bytes 1425416 | tf_op jit(solution)/shard_map/ppermute | solution.py:590
  (27 other events, 277.2 us)
